TPU v7x, 32 devices: a whole 2x2x4 slice. The times are simulated.
32 devices in a mesh: gx: 8 (over z, y), gy: 4 (over x, core).
Axes of the slice: x: 2, y: 2, z: 4, core: 2. Of those that a mesh axis runs over, the one named last changes fastest.
Arguments:
- velocity: float32 [3, 32, 32, 128], P(None, 'gx', 'gy'), may hold values from -6 to 6
- cotangent: float32 [3, 32, 32, 128], P(None, 'gx', 'gy'), may hold values from -10.5 to 13.5
- weight_in: float32 [6, 64], replicated, may hold values from -2.5 to 2.5
- bias_in: float32 [64], replicated, may hold values from -3 to 3
- weight_out: float32 [64, 3], replicated, may hold values from -0.75 to 0.75
Outputs:
- new_velocity: float32 [3, 32, 32, 128], P(None, 'gx', 'gy')
- grad_velocity: float32 [3, 32, 32, 128], P(None, 'gx', 'gy')
- grad_weight_in: float32 [6, 64], replicated
- grad_bias_in: float32 [64], replicated
- grad_weight_out: float32 [64, 3], replicated
All inputs are finite; a program needn't handle non-finite values.
Results may differ from a plain program's by a relative error of at most 0.0003.
Values sent between devices are 32-bit elements; how exact they have to be, the bound alone decides.
No kernel may reach another device: no remote copies, remote signals or barrier semaphores. Data moves between devices by JAX's collectives and lax.ppermute only.
A program may use at most 64 MiB of HBM per device.

v0:
```python
import jax
import jax.numpy as jnp
import numpy as np
from jax import lax
from jax.sharding import PartitionSpec as P

FILTER_ALPHA = 0.499
FILTER_GAIN = 0.5 + FILTER_ALPHA
COMPACT_ALPHA = 1.0 / 3.0
STEP_SIZE = 0.5
PRECISE = lax.Precision.HIGHEST


def extended(array, sides, width):
    for axis, dim in sides:
        devices, length = (lax.axis_size(axis), array.shape[dim])
        up = [(i, (i + 1) % devices) for i in range(devices - 1)]
        down = [(j, i) for i, j in up]
        last = lax.slice_in_dim(array, length - width, length, axis=dim)
        leading = lax.slice_in_dim(array, 0, width, axis=dim)
        before = lax.ppermute(last, axis, up)
        after = lax.ppermute(leading, axis, down)
        array = jnp.concatenate([before, array, after], axis=dim)
    return array


def carried_in(part, axis, combine, identity, reverse):
    count = lax.axis_size(axis)
    place = lax.axis_index(axis)
    ahead = count - 1 - place if reverse else place
    gathered = jax.tree.map(lambda a: lax.all_gather(a, axis), part)
    state = jax.tree.map(lambda a, e: jnp.zeros_like(a) + jnp.asarray(e, a.dtype), part, identity)

    def one(turn, state):
        source = count - 1 - turn if reverse else turn
        return combine(
            state, jax.tree.map(lambda a: lax.dynamic_index_in_dim(a, source, 0, False), gathered)
        )

    return lax.fori_loop(0, ahead, one, state)


def derivative_table(length):
    weights = 7.0 / 9.0 * (np.eye(length, k=1) - np.eye(length, k=-1)) + 1.0 / 36.0 * (
        np.eye(length, k=2) - np.eye(length, k=-2)
    )
    uppers = np.zeros(length)
    before = 0.0
    previous = np.zeros(length)
    for position in range(length):
        scale = 1.0 / (1.0 - COMPACT_ALPHA * before)
        weights[position] = (weights[position] - COMPACT_ALPHA * previous) * scale
        before = COMPACT_ALPHA * scale
        uppers[position] = before
        previous = weights[position]
    for position in reversed(range(length - 1)):
        weights[position] = weights[position] - uppers[position] * weights[position + 1]
    return weights.astype(np.float32)


def sweep_tables(length):
    scales = np.zeros(length)
    uppers = np.zeros(length)
    before = 0.0
    for position in range(length):
        scales[position] = 1.0 / (1.0 - FILTER_ALPHA * before)
        before = FILTER_ALPHA * scales[position]
        uppers[position] = before
    return (scales.astype(np.float32), uppers.astype(np.float32))


def combine(earlier, later):
    return (earlier[0] * later[0], later[0] * earlier[1] + later[1])


def smooth_x(values):
    x_rows = values.shape[1]
    scales_all, uppers_all = sweep_tables(x_rows * lax.axis_size("gx"))
    offset = lax.axis_index("gx") * x_rows
    scales = lax.dynamic_slice_in_dim(jnp.asarray(scales_all), offset, x_rows)
    uppers = lax.dynamic_slice_in_dim(jnp.asarray(uppers_all), offset, x_rows)
    padded = extended(values, (("gx", 1),), 1)
    right_side = FILTER_GAIN * values + 0.5 * FILTER_GAIN * (padded[:, :-2] + padded[:, 2:])
    previous = jnp.zeros_like(values[:, 0])
    factor = jnp.ones((1, 1), jnp.float32)
    partial_rows = []
    factors = []
    for row_index in range(x_rows):
        previous = (right_side[:, row_index] - FILTER_ALPHA * previous) * scales[row_index]
        factor = factor * (-FILTER_ALPHA * scales[row_index])
        partial_rows.append(previous)
        factors.append(factor)
    identity = (jnp.ones((1, 1), jnp.float32), jnp.zeros_like(previous))
    incoming = carried_in((factor, previous), "gx", combine, identity, False)
    eliminated = [
        partial_rows[row_index] + factors[row_index] * incoming[1] for row_index in range(x_rows)
    ]
    following = jnp.zeros_like(previous)
    factor = jnp.ones((1, 1), jnp.float32)
    solved_rows = [None] * x_rows
    back_factors = [None] * x_rows
    for row_index in reversed(range(x_rows)):
        following = eliminated[row_index] - uppers[row_index] * following
        factor = factor * -uppers[row_index]
        solved_rows[row_index] = following
        back_factors[row_index] = factor
    upper_value = carried_in((factor, following), "gx", combine, identity, True)
    finished = [
        solved_rows[row_index] + back_factors[row_index] * upper_value[1]
        for row_index in range(x_rows)
    ]
    return jnp.stack(finished, axis=1)


def y_pass(values, table):
    derived = jnp.einsum(
        "ab,kxbz->kxaz",
        table,
        lax.all_to_all(values, "gy", split_axis=3, concat_axis=2, tiled=True),
        precision=PRECISE,
    )
    return lax.all_to_all(derived, "gy", split_axis=2, concat_axis=3, tiled=True)


def closure_plane(feature_plane, cotangent_plane, weight_in, bias_in, weight_out):
    pre = jnp.dot(weight_in.T, feature_plane, precision=PRECISE) + bias_in[:, None]
    hidden = jnp.tanh(pre)
    forcing = jnp.dot(weight_out.T, hidden, precision=PRECISE)
    grad_out = STEP_SIZE * cotangent_plane
    grad_hidden = jnp.dot(weight_out, grad_out, precision=PRECISE)
    grad_pre = grad_hidden * (1.0 - hidden * hidden)
    grad_feature = jnp.dot(weight_in, grad_pre, precision=PRECISE)
    sum_in = jnp.dot(feature_plane, grad_pre.T, precision=PRECISE)
    sum_bias = jnp.sum(grad_pre, axis=1)
    sum_out = jnp.dot(hidden, grad_out.T, precision=PRECISE)
    return (forcing, grad_feature, sum_in, sum_bias, sum_out)


def local(velocity, cotangent, weight_in, bias_in, weight_out):
    x_rows = velocity.shape[1]
    y_rows = velocity.shape[2]
    z_length = velocity.shape[3]
    y_length = y_rows * lax.axis_size("gy")
    y_table = jnp.asarray(derivative_table(y_length))
    z_table = jnp.asarray(derivative_table(z_length))
    smoothed = smooth_x(velocity)
    along_z = jnp.einsum("ab,kxyb->kxya", z_table, smoothed, precision=PRECISE)
    along_y = y_pass(smoothed, y_table)
    features = jnp.concatenate([along_y, along_z], axis=0)
    plane_cells = y_rows * z_length
    forcing_rows = []
    gradient_rows = []
    sum_in = jnp.zeros((6, weight_in.shape[1]), jnp.float32)
    sum_bias = jnp.zeros((weight_in.shape[1],), jnp.float32)
    sum_out = jnp.zeros((weight_in.shape[1], 3), jnp.float32)
    for row_index in range(x_rows):
        feature_plane = features[:, row_index].reshape(6, plane_cells)
        cotangent_plane = cotangent[:, row_index].reshape(3, plane_cells)
        forcing, grad_feature, part_in, part_bias, part_out = closure_plane(
            feature_plane, cotangent_plane, weight_in, bias_in, weight_out
        )
        forcing_rows.append(forcing.reshape(3, y_rows, z_length))
        gradient_rows.append(grad_feature.reshape(6, y_rows, z_length))
        sum_in = sum_in + part_in
        sum_bias = sum_bias + part_bias
        sum_out = sum_out + part_out
    new_velocity = velocity + STEP_SIZE * jnp.stack(forcing_rows, axis=1)
    grad_features = jnp.stack(gradient_rows, axis=1)
    back_y = y_pass(grad_features[0:3], y_table.T)
    back_z = jnp.einsum("ba,kxyb->kxya", z_table, grad_features[3:6], precision=PRECISE)
    grad_velocity = cotangent + smooth_x(back_y + back_z)
    totals = lax.psum((sum_in, sum_bias, sum_out), ("gx", "gy"))
    cells = float(x_rows * lax.axis_size("gx") * y_length * z_length)
    return (new_velocity, grad_velocity, totals[0] / cells, totals[1] / cells, totals[2] / cells)


def solution(mesh):
    in_specs = (P(None, "gx", "gy", None), P(None, "gx", "gy", None), P(), P(), P())
    out_specs = (P(None, "gx", "gy", None), P(None, "gx", "gy", None), P(), P(), P())
    return jax.shard_map(local, mesh=mesh, in_specs=in_specs, out_specs=out_specs, check_vma=False)
```

profile of v0, /device:TPU:0, one launch (start us, length us, event | category | flops | bytes accessed | tf_op | source)
XLA Modules:
  0.0 311.0 jit_solution(10085472661946085653)
XLA Ops:
  1.4 4.9 %collective-permute-start = (f32[3,1,8,128]{3,2,0,1:T(8,128)S(1)}, f32[3,1,8,128]{3,2,0,1:T(8,128)S(1)}, u32[]{:S(2)}, u32[]{:S(2)}) collective-permute-start(f32[3,1,8,128]{3,2,0,1:T(8,128)S(1)} %get-tuple-element.343), channel_id=1, source_target_pairs={{0,4},{4,8},{8,12},{12,16},{16,20},{20,24},{24,28},{1,5},{5,9},{9,... | collective-permute-start | bytes 36872 | tf_op jit(solution)/shard_map/ppermute | solution.py:21
  6.2 1.3 collective-permute-start.1
  17.0 22.8 %all-reduce.3 = (f32[8]{0:T(128)S(1)}, f32[8]{0:T(128)S(1)}) all-reduce(f32[8]{0:T(128)S(1)} %dynamic-update-slice.1, f32[8]{0:T(128)S(1)} %dynamic-update-slice), channel_id=1, replica_groups=mesh['gx'=8,'gy'=4] {'gx'}, use_global_device_ids=true, to_apply=%add.1 | all-reduce | flops 16 | bytes 128
  41.1 2.5 multiply_bitcast_fusion.1
  43.6 30.5 %all-gather.2 = f32[24,1,8,128]{3,2,1,0:T(8,128)S(1)} all-gather(f32[3,1,8,128]{3,2,1,0:T(8,128)S(1)} %multiply_bitcast_fusion.1), channel_id=4, replica_groups=mesh['gx'=8,'gy'=4] {'gx'}, dimensions={0}, use_global_device_ids=true | all-gather | bytes 110592 | tf_op jit(solution)/shard_map/all_gather | solution.py:31
  74.2 4.6 %fusion.64 = (f32[3,8,128]{2,1,0:T(8,128)S(1)}, f32[3,8,128]{2,1,0:T(8,128)S(1)}, f32[3,8,128]{2,1,0:T(8,128)S(1)}) fusion(f32[3,8,128]{2,1,0:T(8,128)S(1)} %get-tuple-element.261, f32[3,4,8,128]{3,2,0,1:T(8,128)S(1)} %fusion.9, f32[]{:T(128)} %bitcast.18, f32[]{:T(128)S(6)} %mul.642, f32[]{:T(128)} %bitcast.8, f32[]{:T(128)} %bitcast.20, f32[]{:T(128)S(6)} %mul.663, ...), kind=kLoop, calls=%fused_computation.134 | loop fusion | flops 76800 | bytes 98352 | tf_op jit(solution)/shard_map/sub | solution.py:103
  78.7 35.4 %all-gather = f32[24,8,128]{2,1,0:T(8,128)S(1)} all-gather(f32[3,8,128]{2,1,0:T(8,128)S(1)} %get-tuple-element.328), channel_id=2, replica_groups=mesh['gx'=8,'gy'=4] {'gx'}, dimensions={0}, use_global_device_ids=true | all-gather | bytes 110592 | tf_op jit(solution)/shard_map/all_gather | solution.py:31
  114.2 8.8 %while.53 = (s32[]{:T(128)}, f32[3,8,128]{2,1,0:T(8,128)S(1)}, s32[]{:T(128)}, f32[8,1,1]{0,2,1:T(1,128)S(1)}, f32[8,3,8,128]{3,2,1,0:T(8,128)S(1)}, /*index=5*/s32[]{:T(128)}, s32[]{:T(128)}, s32[]{:T(128)}, s32[]{:T(128)}) while((s32[]{:T(128)}, f32[3,8,128]{2,1,0:T(8,128)S(1)}, s32[]{:T(128)}, f32[8,1,1]{0,2,1:T(1,128)S(1)}, ...), condition=%wide.region_3.4_spmd, body=%wide.region_2.3_spmd.sunk | while | flops 6150 | bytes 37031 | solution.py:40
  123.0 2.0 add_bitcast_fusion.6
  125.3 1.4 reshape.250
  126.8 3.4 %all-to-all-start = ((f32[4,1,3072]{2,1,0:T(1,128)}), f32[4,1,3072]{2,1,0:T(1,128)S(1)}, u32[]{:S(2)}, u32[]{:S(2)}) async-start(f32[4,1,3072]{2,1,0:T(1,128)} %reshape.250), calls=%async_computation | async-start | bytes 98304 | tf_op jit(solution)/shard_map/all_to_all | solution.py:119
  130.2 4.0 %all-to-all-done = f32[4,1,3072]{2,1,0:T(1,128)S(1)} async-done(((f32[4,1,3072]{2,1,0:T(1,128)}), f32[4,1,3072]{2,1,0:T(1,128)S(1)}, u32[]{:S(2)}, u32[]{:S(2)}) %all-to-all-start) | async-done | bytes 49184 | tf_op jit(solution)/shard_map/all_to_all | solution.py:119
  135.5 1.0 reshape.251
  138.1 0.8 reshape.252
  138.9 3.4 %all-to-all-start.1 = ((f32[4,1,3072]{2,1,0:T(1,128)}), f32[4,1,3072]{2,1,0:T(1,128)S(1)}, u32[]{:S(2)}, u32[]{:S(2)}) async-start(f32[4,1,3072]{2,1,0:T(1,128)} %reshape.252), calls=%async_computation.1 | async-start | bytes 98304 | tf_op jit(solution)/shard_map/all_to_all | solution.py:122
  142.6 3.7 %all-to-all-done.1 = f32[4,1,3072]{2,1,0:T(1,128)S(1)} async-done(((f32[4,1,3072]{2,1,0:T(1,128)}), f32[4,1,3072]{2,1,0:T(1,128)S(1)}, u32[]{:S(2)}, u32[]{:S(2)}) %all-to-all-start.1) | async-done | bytes 49184 | tf_op jit(solution)/shard_map/all_to_all | solution.py:122
  157.4 1.4 reshape.254
  158.9 3.3 %all-to-all-start.2 = ((f32[4,1,3072]{2,1,0:T(1,128)}), f32[4,1,3072]{2,1,0:T(1,128)S(1)}, u32[]{:S(2)}, u32[]{:S(2)}) async-start(f32[4,1,3072]{2,1,0:T(1,128)} %reshape.254), calls=%async_computation.2 | async-start | bytes 98304 | tf_op jit(solution)/shard_map/all_to_all | solution.py:119
  162.2 37.2 %all-reduce.2 = (f32[6,64]{1,0:T(8,128)S(1)}, f32[64]{0:T(128)S(1)}, f32[64,3]{0,1:T(4,128)S(1)}) all-reduce(f32[6,64]{1,0:T(8,128)S(1)} %convolution_add_fusion.5, f32[64]{0:T(128)S(1)} %add_add_fusion, f32[64,3]{0,1:T(4,128)S(1)} %convolution_add_fusion.8), channel_id=1, replica_groups=mesh['gx'=8,'gy'=4] {'gx','gy'}, use_global_device_ids=true, to_apply=%region_8.9 | all-reduce | flops 640 | bytes 5120 | tf_op jit(solution)/shard_map/psum | solution.py:172
  201.4 1.0 reshape.255
  204.1 0.8 reshape.256
  204.8 3.5 %all-to-all-start.3 = ((f32[4,1,3072]{2,1,0:T(1,128)}), f32[4,1,3072]{2,1,0:T(1,128)S(1)}, u32[]{:S(2)}, u32[]{:S(2)}) async-start(f32[4,1,3072]{2,1,0:T(1,128)} %reshape.256), calls=%async_computation.3 | async-start | bytes 98304 | tf_op jit(solution)/shard_map/all_to_all | solution.py:122
  209.0 3.5 %all-to-all-done.3 = f32[4,1,3072]{2,1,0:T(1,128)S(1)} async-done(((f32[4,1,3072]{2,1,0:T(1,128)}), f32[4,1,3072]{2,1,0:T(1,128)S(1)}, u32[]{:S(2)}, u32[]{:S(2)}) %all-to-all-start.3) | async-done | bytes 49184 | tf_op jit(solution)/shard_map/all_to_all | solution.py:122
  214.5 3.9 %collective-permute-start.2 = (f32[3,1,8,128]{3,2,0,1:T(8,128)S(1)}, f32[3,1,8,128]{3,2,0,1:T(8,128)S(1)}, u32[]{:S(2)}, u32[]{:S(2)}) collective-permute-start(f32[3,1,8,128]{3,2,0,1:T(8,128)S(1)} %get-tuple-element.337), channel_id=1, source_target_pairs={{0,4},{4,8},{8,12},{12,16},{16,20},{20,24},{24,28},{1,5},{5,9},{9,... | collective-permute-start | bytes 36872 | tf_op jit(solution)/shard_map/ppermute | solution.py:21
  218.4 1.3 collective-permute-start.3
  220.2 4.1 %collective-permute-done.3 = f32[3,1,8,128]{3,2,0,1:T(8,128)S(1)} collective-permute-done((f32[3,1,8,128]{3,2,0,1:T(8,128)S(1)}, f32[3,1,8,128]{3,2,0,1:T(8,128)S(1)}, u32[]{:S(2)}, u32[]{:S(2)}) %collective-permute-start.3) | collective-permute-done | bytes 12320 | tf_op jit(solution)/shard_map/ppermute | solution.py:22
  224.3 2.5 multiply_bitcast_fusion
  226.8 30.6 %all-gather.3 = f32[24,1,8,128]{3,2,1,0:T(8,128)S(1)} all-gather(f32[3,1,8,128]{3,2,1,0:T(8,128)S(1)} %multiply_bitcast_fusion), channel_id=5, replica_groups=mesh['gx'=8,'gy'=4] {'gx'}, dimensions={0}, use_global_device_ids=true | all-gather | bytes 110592 | tf_op jit(solution)/shard_map/all_gather | solution.py:31
  257.4 4.6 %fusion.58 = (f32[3,8,128]{2,1,0:T(8,128)S(1)}, f32[3,8,128]{2,1,0:T(8,128)S(1)}, f32[3,8,128]{2,1,0:T(8,128)S(1)}) fusion(f32[3,8,128]{2,1,0:T(8,128)S(1)} %get-tuple-element.263, f32[3,4,8,128]{3,2,0,1:T(8,128)S(1)} %fusion.6, f32[]{:T(128)} %bitcast.18, f32[]{:T(128)S(6)} %mul.642, f32[]{:T(128)} %bitcast.8, f32[]{:T(128)} %bitcast.20, f32[]{:T(128)S(6)} %mul.663, ...), kind=kLoop, calls=%fused_computation.123 | loop fusion | flops 76800 | bytes 98352 | tf_op jit(solution)/shard_map/sub | solution.py:103
  262.0 37.6 %all-gather.1 = f32[24,8,128]{2,1,0:T(8,128)S(1)} all-gather(f32[3,8,128]{2,1,0:T(8,128)S(1)} %get-tuple-element.325), channel_id=3, replica_groups=mesh['gx'=8,'gy'=4] {'gx'}, dimensions={0}, use_global_device_ids=true | all-gather | bytes 110592 | tf_op jit(solution)/shard_map/all_gather | solution.py:31
  299.5 8.8 %while.55 = (s32[]{:T(128)}, f32[3,8,128]{2,1,0:T(8,128)S(1)}, s32[]{:T(128)}, f32[8,1,1]{0,2,1:T(1,128)S(1)}, f32[8,3,8,128]{3,2,1,0:T(8,128)S(1)}, /*index=5*/s32[]{:T(128)}, s32[]{:T(128)}, s32[]{:T(128)}, s32[]{:T(128)}) while((s32[]{:T(128)}, f32[3,8,128]{2,1,0:T(8,128)S(1)}, s32[]{:T(128)}, f32[8,1,1]{0,2,1:T(1,128)S(1)}, ...), condition=%wide.region_7.8_spmd, body=%wide.region_6.7_spmd.sunk | while | flops 6150 | bytes 37031 | solution.py:40
  308.4 2.0 add_bitcast_fusion.2
  (141 shorter events, 44.1 us)
Async XLA Ops:
  0.6 146.9 %copy-start = (f32[6,64]{1,0:T(8,128)S(1)}, f32[6,64]{1,0:T(8,128)}, u32[]{:S(2)}) copy-start(f32[6,64]{1,0:T(8,128)} %param.21) | copy-start | bytes 4612
  1.4 39.7 %collective-permute-start = (f32[3,1,8,128]{3,2,0,1:T(8,128)S(1)}, f32[3,1,8,128]{3,2,0,1:T(8,128)S(1)}, u32[]{:S(2)}, u32[]{:S(2)}) collective-permute-start(f32[3,1,8,128]{3,2,0,1:T(8,128)S(1)} %get-tuple-element.343), channel_id=1, source_target_pairs={{0,4},{4,8},{8,12},{12,16},{16,20},{20,24},{24,28},{1,5},{5,9},{9,... | collective-permute-start | bytes 36872 | tf_op jit(solution)/shard_map/ppermute | solution.py:21
  6.2 34.8 %collective-permute-start.1 = (f32[3,1,8,128]{3,2,0,1:T(8,128)S(1)}, f32[3,1,8,128]{3,2,0,1:T(8,128)S(1)}, u32[]{:S(2)}, u32[]{:S(2)}) collective-permute-start(f32[3,1,8,128]{3,2,0,1:T(8,128)S(1)} %get-tuple-element.344), channel_id=1, source_target_pairs={{4,0},{8,4},{12,8},{16,12},{20,16},{24,20},{28,24},{5,1},{9,5},{13... | collective-permute-start | bytes 36872 | tf_op jit(solution)/shard_map/ppermute | solution.py:22
  7.6 0.7 copy-start.11
  7.6 0.7 copy-start.10
  7.6 4.8 %copy-start.9 = (u32[32]{0:T(128)S(1)}, u32[32]{0:T(128)}, u32[]{:S(2)}) copy-start(u32[32]{0:T(128)} %constant.158) | copy-start | bytes 388
  7.6 32.2 %copy-start.1 = (f32[3,4,8,128]{3,2,1,0:T(8,128)S(1)}, f32[3,4,8,128]{3,2,1,0:T(8,128)}, u32[]{:S(2)}) copy-start(f32[3,4,8,128]{3,2,1,0:T(8,128)} %param.19) | copy-start | bytes 147460
  126.8 3.4 %copy-start.2 = (f32[3,4,8,128]{3,2,1,0:T(8,128)S(1)}, f32[3,4,8,128]{3,2,1,0:T(8,128)}, u32[]{:S(2)}) copy-start(f32[3,4,8,128]{3,2,1,0:T(8,128)} %param.20) | copy-start | bytes 147460
  126.8 7.4 %all-to-all-start = ((f32[4,1,3072]{2,1,0:T(1,128)}), f32[4,1,3072]{2,1,0:T(1,128)S(1)}, u32[]{:S(2)}, u32[]{:S(2)}) async-start(f32[4,1,3072]{2,1,0:T(1,128)} %reshape.250), calls=%async_computation | async-start | bytes 98304 | tf_op jit(solution)/shard_map/all_to_all | solution.py:119
  136.7 0.7 copy-start.7
  138.9 3.4 %copy-start.5 = (f32[128,128,1,1]{1,0,3,2:T(8,128)S(1)}, f32[128,128,1,1]{1,0,3,2:T(8,128)}, u32[]{:S(2)}) copy-start(f32[128,128,1,1]{1,0,3,2:T(8,128)} %constant.169) | copy-start | bytes 196612
  138.9 7.4 %all-to-all-start.1 = ((f32[4,1,3072]{2,1,0:T(1,128)}), f32[4,1,3072]{2,1,0:T(1,128)S(1)}, u32[]{:S(2)}, u32[]{:S(2)}) async-start(f32[4,1,3072]{2,1,0:T(1,128)} %reshape.252), calls=%async_computation.1 | async-start | bytes 98304 | tf_op jit(solution)/shard_map/all_to_all | solution.py:122
  147.5 0.7 copy-start.8
  148.6 0.7 copy-start.3
  158.9 41.8 %all-to-all-start.2 = ((f32[4,1,3072]{2,1,0:T(1,128)}), f32[4,1,3072]{2,1,0:T(1,128)S(1)}, u32[]{:S(2)}, u32[]{:S(2)}) async-start(f32[4,1,3072]{2,1,0:T(1,128)} %reshape.254), calls=%async_computation.2 | async-start | bytes 98304 | tf_op jit(solution)/shard_map/all_to_all | solution.py:119
  202.7 0.7 copy-start.6
  204.8 7.6 %all-to-all-start.3 = ((f32[4,1,3072]{2,1,0:T(1,128)}), f32[4,1,3072]{2,1,0:T(1,128)S(1)}, u32[]{:S(2)}, u32[]{:S(2)}) async-start(f32[4,1,3072]{2,1,0:T(1,128)} %reshape.256), calls=%async_computation.3 | async-start | bytes 98304 | tf_op jit(solution)/shard_map/all_to_all | solution.py:122
  213.4 0.8 copy-start.4
  214.5 5.7 %collective-permute-start.2 = (f32[3,1,8,128]{3,2,0,1:T(8,128)S(1)}, f32[3,1,8,128]{3,2,0,1:T(8,128)S(1)}, u32[]{:S(2)}, u32[]{:S(2)}) collective-permute-start(f32[3,1,8,128]{3,2,0,1:T(8,128)S(1)} %get-tuple-element.337), channel_id=1, source_target_pairs={{0,4},{4,8},{8,12},{12,16},{16,20},{20,24},{24,28},{1,5},{5,9},{9,... | collective-permute-start | bytes 36872 | tf_op jit(solution)/shard_map/ppermute | solution.py:21
  218.4 5.9 %collective-permute-start.3 = (f32[3,1,8,128]{3,2,0,1:T(8,128)S(1)}, f32[3,1,8,128]{3,2,0,1:T(8,128)S(1)}, u32[]{:S(2)}, u32[]{:S(2)}) collective-permute-start(f32[3,1,8,128]{3,2,0,1:T(8,128)S(1)} %get-tuple-element.338), channel_id=1, source_target_pairs={{4,0},{8,4},{12,8},{16,12},{20,16},{24,20},{28,24},{5,1},{9,5},{13... | collective-permute-start | bytes 36872 | tf_op jit(solution)/shard_map/ppermute | solution.py:22
where the time goes:
time: 313 us; the launch traced here: 311 us
  blocking collectives  194 us (62%)
  other arithmetic  32.6 us (10%)
  local copies, waits for them, and re-layouts  26.2 us (8%)
  starting transfers between devices  25 us (8%)
  waiting for transfers between devices  15.3 us (5%)
  matrix products  9.72 us (3%)
  between operations  7.72 us (2%)
    all_gather x4, blocking collectives, carried_in(): gathered = jax.tree.map(lambda a: lax.all_gather(a, axis), part)  134 us
    psum x1, blocking collectives, local(): totals = lax.psum((sum_in, sum_bias, sum_out), ('gx', 'gy'))  37.2 us
    unnamed x1, blocking collectives  22.8 us
    unnamed x39, local copies, waits for them, and re-layouts  13 us
    add x14, other arithmetic, combine(): return (earlier[0] * later[0], later[0] * earlier[1] + later[1])  9.14 us
    sub x2, other arithmetic, smooth_x(): following = eliminated[row_index] - uppers[row_index] * following  9.12 us
    ppermute x2, starting transfers between devices, extended(): before = lax.ppermute(last, axis, up)  8.76 us
    dynamic_slice x14, local copies, waits for them, and re-layouts, one(): lax.dynamic_index_in_dim(a, source, 0, False)  8.19 us
  transfers between devices with their start and end apart: 8, of which 4 were waited for; matrix products, arithmetic and copies ran while one was open for 2% of the time, Pallas kernels for 0%

commit v1 on v0

v1 whole, which is shorter than its diff:
```python
import jax
import jax.numpy as jnp
import numpy as np
from jax import lax
from jax.sharding import PartitionSpec as P

FILTER_ALPHA = 0.499
FILTER_GAIN = 0.5 + FILTER_ALPHA
COMPACT_ALPHA = 1.0 / 3.0
STEP_SIZE = 0.5
PRECISE = lax.Precision.HIGHEST


def beside(length, offset):
    return np.eye(length, k=offset) + np.eye(length, k=-offset)


def smooth_table(length):
    left = np.eye(length) + FILTER_ALPHA * beside(length, 1)
    right = FILTER_GAIN * np.eye(length) + 0.5 * FILTER_GAIN * beside(length, 1)
    return np.linalg.solve(left, right)


def derivative_table(length):
    left = np.eye(length) + COMPACT_ALPHA * beside(length, 1)
    right = 7.0 / 9.0 * (np.eye(length, k=1) - np.eye(length, k=-1)) + 1.0 / 36.0 * (
        np.eye(length, k=2) - np.eye(length, k=-2)
    )
    return np.linalg.solve(left, right)


def table(values):
    return jnp.asarray(values.astype(np.float32))


def local(velocity, cotangent, weight_in, bias_in, weight_out):
    axes = ("gx", "gy")
    x_devices, y_devices = lax.axis_size("gx"), lax.axis_size("gy")
    devices = x_devices * y_devices
    _, x_rows, y_rows, z_length = velocity.shape
    x_length, y_length = x_rows * x_devices, y_rows * y_devices
    units = weight_in.shape[1]
    z_rows = -(-z_length // devices)
    padding = z_rows * devices - z_length

    z_table = table(derivative_table(z_length))
    y_table = table(derivative_table(y_length))
    x_table = table(smooth_table(x_length))

    along_z = jnp.einsum("ab,kxyb->kxya", z_table, velocity, precision=PRECISE)
    fields = jnp.concatenate([velocity, along_z, cotangent], axis=0)
    fields = jnp.pad(fields, ((0, 0), (0, 0), (0, 0), (0, padding)))
    fields = fields.reshape(9, x_rows, y_rows, z_rows, devices)
    fields = fields.transpose(4, 0, 3, 1, 2).reshape(devices, 9, z_rows * x_rows * y_rows)
    fields = lax.all_to_all(fields, axes, 0, 0, tiled=True)
    fields = fields.reshape(x_devices, y_devices, 9, z_rows, x_rows, y_rows)
    fields = fields.transpose(2, 0, 4, 3, 1, 5).reshape(9, x_length, z_rows, y_length)

    smoothed = jnp.einsum("ab,kbzy->kazy", x_table, fields[:6], precision=PRECISE)
    along_y = jnp.einsum("ab,kxzb->kxza", y_table, smoothed[:3], precision=PRECISE)
    features = jnp.concatenate([along_y, smoothed[3:]], axis=0).reshape(6, -1)
    grad_out = STEP_SIZE * fields[6:].reshape(3, -1)

    hidden = jnp.tanh(jnp.dot(weight_in.T, features, precision=PRECISE) + bias_in[:, None])
    forcing = jnp.dot(weight_out.T, hidden, precision=PRECISE)
    grad_pre = jnp.dot(weight_out, grad_out, precision=PRECISE) * (1.0 - hidden * hidden)
    grad_features = jnp.dot(weight_in, grad_pre, precision=PRECISE)
    sum_in = jnp.dot(features, grad_pre.T, precision=PRECISE)
    sum_bias = jnp.sum(grad_pre, axis=1)
    sum_out = jnp.dot(grad_out, hidden.T, precision=PRECISE)

    grad_features = grad_features.reshape(6, x_length, z_rows, y_length)
    back_y = jnp.einsum("ba,kxzb->kxza", y_table, grad_features[:3], precision=PRECISE)
    back = jnp.concatenate([back_y, grad_features[3:]], axis=0)
    back = jnp.einsum("ab,kbzy->kazy", x_table, back, precision=PRECISE)
    back = jnp.concatenate([forcing.reshape(3, x_length, z_rows, y_length), back], axis=0)
    back = back.reshape(9, x_devices, x_rows, z_rows, y_devices, y_rows)
    back = back.transpose(1, 4, 0, 3, 2, 5).reshape(devices, -1)
    sums = jnp.concatenate([sum_in, sum_bias[None], sum_out], axis=0).reshape(1, -1)
    cells = back.shape[1]
    back = jnp.concatenate([back, jnp.broadcast_to(sums, (devices, 10 * units))], axis=1)
    back = lax.all_to_all(back, axes, 0, 0, tiled=True)

    sums = jnp.sum(back[:, cells:], axis=0).reshape(10, units)
    sums = sums / float(x_length * y_length * z_length)
    back = back[:, :cells].reshape(devices, 9, z_rows, x_rows, y_rows)
    back = back.transpose(1, 3, 4, 2, 0).reshape(9, x_rows, y_rows, -1)[..., :z_length]
    new_velocity = velocity + STEP_SIZE * back[:3]
    back_z = jnp.einsum("ba,kxyb->kxya", z_table, back[6:], precision=PRECISE)
    grad_velocity = cotangent + back[3:6] + back_z
    return (new_velocity, grad_velocity, sums[:6], sums[6], sums[7:].T)


def solution(mesh):
    in_specs = (P(None, "gx", "gy", None), P(None, "gx", "gy", None), P(), P(), P())
    out_specs = (P(None, "gx", "gy", None), P(None, "gx", "gy", None), P(), P(), P())
    return jax.shard_map(local, mesh=mesh, in_specs=in_specs, out_specs=out_specs, check_vma=False)
```

time: 313 us -> 59.7 us (0.19)
  blocking collectives: 194 us -> 29.7 us
  other arithmetic: 32.6 us -> 2.41 us
  starting transfers between devices: 25 us -> 0 us
  waiting for transfers between devices: 15.3 us -> 0 us
  local copies, waits for them, and re-layouts: 26.2 us -> 16.5 us
  between operations: 7.72 us -> 1.04 us
    all_gather x4 -> x0, blocking collectives: 134 us -> none  [carried_in(): gathered = jax.tree.map(lambda a: lax.all_gather(a, axis), part)]
    psum x1 -> x0, blocking collectives: 37.2 us -> none  [local(): totals = lax.psum((sum_in, sum_bias, sum_out), ('gx', 'gy'))]
    all_to_all x0 -> x2, blocking collectives: none -> 29.7 us  [the longest x1 17.7 us: local(): fields = lax.all_to_all(fields, axes, 0, 0, tiled=True)]
    unnamed x1 -> x0, blocking collectives: 22.8 us -> none
    all_to_all x4 -> x0, starting transfers between devices: 13.6 us -> none  [the longest x2 6.95 us: y_pass(): lax.all_to_all(derived, 'gy', split_axis=2, concat_axis=3, tiled=True)]
    unnamed x39 -> x16, local copies, waits for them, and re-layouts: 13 us -> 0.06 us
    ppermute x4 -> x0, starting transfers between devices: 11.3 us -> none  [the longest x2 8.76 us: extended(): before = lax.ppermute(last, axis, up)]
    all_to_all x4 -> x0, waiting for transfers between devices: 11.2 us -> none  [the longest x2 7.19 us: y_pass(): lax.all_to_all(derived, 'gy', split_axis=2, concat_axis=3, tiled=True)]
  transfers between devices with their start and end apart: 8 -> 0, of which waited for: 4 -> 0; matrix products, arithmetic and copies ran while one was open for 2% -> 0% of each run, Pallas kernels for 0% -> 0%
where the time goes in v1:
time: 59.7 us; the launch traced here: 59.5 us
  blocking collectives  29.7 us (50%)
  local copies, waits for them, and re-layouts  16.5 us (28%)
  matrix products  9.76 us (16%)
  other arithmetic  2.41 us (4%)
  between operations  1.04 us (2%)
    all_to_all x1, blocking collectives, local(): fields = lax.all_to_all(fields, axes, 0, 0, tiled=True)  17.7 us
    all_to_all x1, blocking collectives, local(): back = lax.all_to_all(back, axes, 0, 0, tiled=True)  12 us
    reshape x2, local copies, waits for them, and re-layouts, local(): fields = fields.reshape(x_devices, y_devices, 9, z_rows, x_rows, y_rows)  4.18 us
    reshape x1, local copies, waits for them, and re-layouts, local(): back = back.transpose(1, 4, 0, 3, 2, 5).reshape(devices, -1)  2.66 us
    slice x5, local copies, waits for them, and re-layouts, local(): return (new_velocity, grad_velocity, sums[:6], sums[6], sums[7:].T)  1.91 us
    concatenate x2, local copies, waits for them, and re-layouts, local(): jnp.concatenate([forcing.reshape(3, x_length, z_rows, y_length), back], a...  1.66 us
    slice x3, local copies, waits for them, and re-layouts, local(): fields[:6]  1.29 us
    dot_general x1, matrix products, local(): jnp.dot(weight_out, grad_out, precision=PRECISE) * (1.0 - hidden * hidden)  1.27 us

profile of v1, /device:TPU:0, one launch (start us, length us, event | category | flops | bytes accessed | tf_op | source)
XLA Modules:
  0.0 59.5 jit_solution(2183893651809782241)
XLA Ops:
  0.6 1.1 %convolution_bitcast_fusion.4 = f32[3,4,8,128]{3,2,1,0:T(8,128)S(1)} fusion(f32[128,128,1,1]{1,0,3,2:T(8,128)} %constant.22, f32[3,4,8,128]{3,2,1,0:T(8,128)} %param.8), kind=kOutput, calls=%fused_computation.10 | convolution fusion | flops 18874368 | bytes 163840 | tf_op jit(solution)/shard_map/ab,kxyb->kxya/dot_general | solution.py:50
  1.7 0.8 %pad_maximum_fusion.1 = f32[9,4,8,128]{3,2,1,0:T(8,128)S(1)} fusion(f32[3,4,8,128]{3,2,1,0:T(8,128)} %param.9, f32[3,4,8,128]{3,2,1,0:T(8,128)S(1)} %convolution_bitcast_fusion.4, f32[3,4,8,128]{3,2,1,0:T(8,128)} %param.8), kind=kLoop, calls=%fused_computation.21 | loop fusion | flops 73728 | bytes 294912 | tf_op jit(solution)/shard_map/concatenate | solution.py:51
  2.6 0.3 reshape.61
  3.0 0.3 copy.71
  3.3 17.7 %all_to_all.17 = f32[32,9,128]{2,1,0:T(8,128)S(1)} all-to-all(f32[32,9,128]{2,1,0:T(8,128)S(1)} %copy.71), channel_id=1, replica_groups=mesh['gx'=8,'gy'=4] {'gx','gy'}, dimensions={0} | all-to-all | bytes 294912 | tf_op jit(solution)/shard_map/all_to_all | solution.py:55
  21.0 2.8 %reshape.70 = f32[8,4,9,4,4,8]{5,4,3,2,1,0:T(4,128)S(1)} reshape(f32[32,9,128]{2,1,0:T(8,128)S(1)} %all_to_all.17) | data formatting | bytes 294912 | tf_op jit(solution)/shard_map/reshape | solution.py:56
  23.8 1.4 %copy.105 = f32[8,4,9,4,4,8]{5,0,1,3,4,2:T(8,128)S(1)} copy(f32[8,4,9,4,4,8]{5,4,3,2,1,0:T(4,128)S(1)} %reshape.70) | data formatting | bytes 294912 | tf_op jit(solution)/shard_map/reshape | solution.py:56
  25.5 0.4 copy.74
  25.9 0.7 %slice.67 = f32[6,32,4,32]{3,1,2,0:T(8,128)S(1)} reshape(f32[6,8,4,4,4,8]{5,4,2,1,3,0:T(4,128)S(1)} %copy.74) | data formatting | bytes 196608 | tf_op jit(solution)/shard_map/slice | solution.py:59
  26.8 0.8 %mul.27 = f32[3,4096]{1,0:T(4,128)S(1)} reshape(f32[3,8,4,4,4,8]{5,4,3,2,1,0:T(4,128)S(1)} %copy.79) | data formatting | bytes 98304 | tf_op jit(solution)/shard_map/mul | solution.py:62
  27.7 0.8 %convolution_bitcast_fusion.3 = f32[6,32,4,32]{1,3,2,0:T(8,128)S(1)} fusion(f32[6,32,4,32]{3,1,2,0:T(8,128)S(1)} %slice.67, f32[32,32,1,1]{1,0,3,2:T(8,128)S(1)} %copy-done.4), kind=kOutput, calls=%fused_computation.8 | convolution fusion | flops 9437184 | bytes 200704 | tf_op jit(solution)/shard_map/ab,kbzy->kazy/dot_general | solution.py:59
  28.5 0.3 fusion.12
  29.4 1.0 %fusion = f32[4096,64]{0,1:T(8,128)S(1)} fusion(f32[6,4096]{1,0:T(8,128)S(1)} %reshape.64, f32[6,64]{1,0:T(8,128)S(1)} %copy-done, f32[64]{0:T(128)S(1)} %copy-done.7), kind=kOutput, calls=%fused_computation.2 | convolution fusion | flops 19136512 | bytes 1148672 | tf_op jit(solution)/shard_map/dot_general | solution.py:64
  30.4 0.9 %fusion.11 = f32[3,64]{1,0:T(4,128)S(1)} fusion(f32[3,4096]{1,0:T(4,128)S(1)} %mul.27, f32[4096,64]{0,1:T(8,128)S(1)} %fusion), kind=kOutput, calls=%fused_computation.29 | convolution fusion | flops 9437184 | bytes 1098496 | tf_op jit(solution)/shard_map/dot_general | solution.py:70
  31.3 0.7 %convolution_bitcast_fusion.1 = f32[3,4096]{1,0:T(4,128)S(1)} fusion(f32[4096,64]{0,1:T(8,128)S(1)} %fusion, f32[64,3]{0,1:T(4,128)S(1)} %copy-done.6), kind=kOutput, calls=%fused_computation.4 | convolution fusion | flops 9437184 | bytes 1098496 | tf_op jit(solution)/shard_map/dot_general | solution.py:65
  32.0 1.3 %fusion.9 = (f32[64]{0:T(128)S(1)}, f32[4096,64]{0,1:T(8,128)S(1)}) fusion(f32[4096,64]{0,1:T(8,128)S(1)} %fusion, f32[3,4096]{1,0:T(4,128)S(1)} %mul.27, f32[64,3]{0,1:T(4,128)S(1)} %copy-done.6), kind=kOutput, calls=%fused_computation.27 | convolution fusion | flops 10485696 | bytes 2147328 | tf_op jit(solution)/shard_map/dot_general | solution.py:66
  33.3 0.9 %fusion.10 = f32[6,64]{1,0:T(8,128)S(1)} fusion(f32[6,4096]{1,0:T(8,128)S(1)} %reshape.64, f32[4096,64]{0,1:T(8,128)S(1)} %get-tuple-element.11), kind=kOutput, calls=%fused_computation.28 | convolution fusion | flops 18874368 | bytes 1148416 | tf_op jit(solution)/shard_map/dot_general | solution.py:68
  34.2 0.7 %convolution_bitcast_fusion = f32[6,4096]{1,0:T(8,128)S(1)} fusion(f32[4096,64]{0,1:T(8,128)S(1)} %get-tuple-element.11, f32[6,64]{1,0:T(8,128)S(1)} %copy-done), kind=kOutput, calls=%fused_computation.3 | convolution fusion | flops 18874368 | bytes 1148416 | tf_op jit(solution)/shard_map/dot_general | solution.py:67
  35.1 0.3 fusion.4
  35.6 1.0 %convolution_bitcast_fusion.2 = f32[6,32,4,32]{1,3,2,0:T(8,128)S(1)} fusion(f32[32,32,1,1]{1,0,3,2:T(8,128)S(1)} %copy-done.4, f32[3,32,4,32]{3,1,2,0:T(8,128)S(1)} %copy.81, f32[3,32,4,32]{3,1,2,0:T(8,128)S(1)} %fusion.4), kind=kOutput, calls=%fused_computation.7 | convolution fusion | flops 9461760 | bytes 200704 | tf_op jit(solution)/shard_map/ab,kbzy->kazy/dot_general | solution.py:75
  36.8 1.0 %concatenate.25 = f32[3,8,4,4,4,8]{5,4,3,2,1,0:T(4,128)S(1)} reshape(f32[3,4096]{1,0:T(4,128)S(1)} %convolution_bitcast_fusion.1) | data formatting | bytes 98304 | tf_op jit(solution)/shard_map/concatenate | solution.py:76
  37.7 0.7 %concatenate.27 = f32[6,8,4,4,4,8]{5,4,2,1,3,0:T(4,128)S(1)} reshape(f32[6,32,4,32]{3,1,2,0:T(8,128)S(1)} %copy.83) | data formatting | bytes 196608 | tf_op jit(solution)/shard_map/concatenate | solution.py:76
  38.4 0.6 %maximum_bitcast_fusion = f32[8,4,9,4,4,8]{5,1,4,0,3,2:T(4,128)S(1)} fusion(f32[6,8,4,4,4,8]{5,4,2,1,3,0:T(4,128)S(1)} %concatenate.27, f32[3,8,4,4,4,8]{5,4,3,2,1,0:T(4,128)S(1)} %concatenate.25), kind=kLoop, calls=%fused_computation.5 | loop fusion | flops 36864 | bytes 294912 | tf_op jit(solution)/shard_map/transpose | solution.py:78
  39.1 0.6 %copy.85 = f32[8,4,9,4,4,8]{5,4,3,2,1,0:T(4,128)S(1)} copy(f32[8,4,9,4,4,8]{5,1,4,0,3,2:T(4,128)S(1)} %maximum_bitcast_fusion) | data formatting | bytes 294912 | tf_op jit(solution)/shard_map/transpose | solution.py:78
  39.7 2.7 %reshape.65 = f32[32,1152]{1,0:T(8,128)S(1)} reshape(f32[8,4,9,4,4,8]{5,4,3,2,1,0:T(4,128)S(1)} %copy.85) | data formatting | bytes 294912 | tf_op jit(solution)/shard_map/reshape | solution.py:78
  42.6 12.0 %all_to_all.18 = f32[32,1,1792]{2,1,0:T(1,128)S(1)} all-to-all(f32[32,1,1792]{2,1,0:T(1,128)S(1)} %copy.86), channel_id=1, replica_groups=mesh['gx'=8,'gy'=4] {'gx','gy'}, dimensions={0} | all-to-all | bytes 458752 | tf_op jit(solution)/shard_map/all_to_all | solution.py:82
  54.6 0.3 copy.87
  55.2 0.5 slice.84
  56.1 0.7 %slice.86 = f32[3,64]{1,0:T(4,128)} reshape(f32[192]{0:T(256)S(1)} %slice.85) | data formatting | bytes 1536 | tf_op jit(solution)/shard_map/slice | solution.py:91
  56.8 0.7 %slice.83 = f32[6,64]{1,0:T(8,128)} reshape(f32[384]{0:T(512)S(1)} %slice.82) | data formatting | bytes 3072 | tf_op jit(solution)/shard_map/slice | solution.py:91
  58.0 0.6 %add.20 = f32[3,4,8,128]{3,2,1,0:T(8,128)} add(f32[3,4,8,128]{3,2,1,0:T(8,128)S(1)} %copy-done.1, f32[3,4,8,128]{3,2,1,0:T(8,128)S(1)} %mul.32) | non-fusion elementwise | flops 12288 | bytes 147456 | tf_op jit(solution)/shard_map/add | solution.py:88
  58.7 0.8 %convolution_add_fusion.1 = f32[3,4,8,128]{3,2,1,0:T(8,128)} fusion(f32[3,4,8,128]{3,2,1,0:T(8,128)S(1)} %slice.80, f32[128,128,1,1]{1,0,3,2:T(8,128)S(1)} %copy-done.2, f32[3,4,8,128]{3,2,1,0:T(8,128)S(1)} %copy-done.3, f32[3,4,8,128]{3,2,1,0:T(8,128)S(1)} %slice.78), kind=kOutput, calls=%fused_computation.9 | convolution fusion | flops 18898944 | bytes 262144 | tf_op jit(solution)/shard_map/ba,kxyb->kxya/dot_general | solution.py:89
  (46 shorter events, 3.1 us)
Async XLA Ops:
  0.6 28.7 %copy-start = (f32[6,64]{1,0:T(8,128)S(1)}, f32[6,64]{1,0:T(8,128)}, u32[]{:S(2)}) copy-start(f32[6,64]{1,0:T(8,128)} %param.10) | copy-start | bytes 4612
  25.9 1.7 %copy-start.4 = (f32[32,32,1,1]{1,0,3,2:T(8,128)S(1)}, f32[32,32,1,1]{1,0,3,2:T(8,128)}, u32[]{:S(2)}) copy-start(f32[32,32,1,1]{1,0,3,2:T(8,128)} %constant.23) | copy-start | bytes 12292
  25.9 2.6 %copy-start.5 = (f32[32,32,1,1]{1,0,3,2:T(8,128)S(1)}, f32[32,32,1,1]{1,0,3,2:T(8,128)}, u32[]{:S(2)}) copy-start(f32[32,32,1,1]{1,0,3,2:T(8,128)} %constant.24) | copy-start | bytes 12292
  26.8 2.5 %copy-start.7 = (f32[64]{0:T(128)S(1)}, f32[64]{0:T(128)}, u32[]{:S(2)}) copy-start(f32[64]{0:T(128)} %param.11) | copy-start | bytes 772
  28.5 2.8 %copy-start.6 = (f32[64,3]{0,1:T(4,128)S(1)}, f32[64,3]{0,1:T(4,128)}, u32[]{:S(2)}) copy-start(f32[64,3]{0,1:T(4,128)} %param.12) | copy-start | bytes 2308
  55.0 3.1 %copy-start.1 = (f32[3,4,8,128]{3,2,1,0:T(8,128)S(1)}, f32[3,4,8,128]{3,2,1,0:T(8,128)}, u32[]{:S(2)}) copy-start(f32[3,4,8,128]{3,2,1,0:T(8,128)} %param.8) | copy-start | bytes 147460
  55.0 3.7 %copy-start.2 = (f32[128,128,1,1]{1,0,3,2:T(8,128)S(1)}, f32[128,128,1,1]{1,0,3,2:T(8,128)}, u32[]{:S(2)}) copy-start(f32[128,128,1,1]{1,0,3,2:T(8,128)} %constant.22) | copy-start | bytes 196612
  55.0 3.7 %copy-start.3 = (f32[3,4,8,128]{3,2,1,0:T(8,128)S(1)}, f32[3,4,8,128]{3,2,1,0:T(8,128)}, u32[]{:S(2)}) copy-start(f32[3,4,8,128]{3,2,1,0:T(8,128)} %param.9) | copy-start | bytes 147460

commit v2 on v1

--- a/solution.py
+++ b/solution.py
@@ -1,7 +1,11 @@
+import functools
+
 import jax
 import jax.numpy as jnp
 import numpy as np
 from jax import lax
+from jax.experimental import pallas as pl
+from jax.experimental.pallas import tpu as pltpu
 from jax.sharding import PartitionSpec as P
 
 FILTER_ALPHA = 0.499
@@ -9,6 +13,9 @@
 COMPACT_ALPHA = 1.0 / 3.0
 STEP_SIZE = 0.5
 PRECISE = lax.Precision.HIGHEST
+LANES = 128
+SENT = 9
+RETURNED = 14
 
 
 def beside(length, offset):
@@ -33,7 +40,7 @@
     return jnp.asarray(values.astype(np.float32))
 
 
-def local(velocity, cotangent, weight_in, bias_in, weight_out):
+def local_plain(velocity, cotangent, weight_in, bias_in, weight_out):
     axes = ("gx", "gy")
     x_devices, y_devices = lax.axis_size("gx"), lax.axis_size("gy")
     devices = x_devices * y_devices
@@ -91,6 +98,273 @@
     return (new_velocity, grad_velocity, sums[:6], sums[6], sums[7:].T)
 
 
+def exchange(parts, width):
+    parts = list(parts)
+    lane = lax.broadcasted_iota(jnp.int32, parts[0].shape, 1)
+    step = len(parts) // 2
+    while step:
+        shift = step * width
+        upper = (lane & shift) != 0
+        for low in range(len(parts)):
+            if low & step == 0:
+                first, second = parts[low], parts[low + step]
+                parts[low] = jnp.where(upper, pltpu.roll(second, shift, 1), first)
+                parts[low + step] = jnp.where(upper, second, pltpu.roll(first, LANES - shift, 1))
+        step //= 2
+    return parts
+
+
+def solve_rows(rows):
+    length = len(rows)
+    half = length // 2
+    scales = []
+    before = 0.0
+    for _ in range(half):
+        scales.append(1.0 / (1.0 - FILTER_ALPHA * FILTER_ALPHA * before))
+        before = scales[-1]
+    solved = [None] * length
+    for sign in (1, -1):
+        order = range(half) if sign == 1 else range(length - 1, length - 1 - half, -1)
+        last = None
+        for turn, row in enumerate(order):
+            value = rows[row] * scales[turn]
+            if last is not None:
+                value = value - last * (FILTER_ALPHA * scales[turn])
+            solved[row] = last = value
+    below, above = solved[half - 1], solved[half]
+    ratio = FILTER_ALPHA * scales[half - 1]
+    middle = 1.0 / (1.0 - ratio * ratio)
+    solved[half - 1] = (below - ratio * above) * middle
+    solved[half] = (above - ratio * below) * middle
+    for turn in reversed(range(half - 1)):
+        factor = FILTER_ALPHA * scales[turn]
+        solved[turn] = solved[turn] - factor * solved[turn + 1]
+        row = length - 1 - turn
+        solved[row] = solved[row] - factor * solved[row - 1]
+    return solved
+
+
+def smooth_rows(rows):
+    own = 0.5 * FILTER_GAIN / FILTER_ALPHA
+    solved = solve_rows(rows)
+    return [own * row + (FILTER_GAIN - own) * value for row, value in zip(rows, solved)]
+
+
+def times(left, right, contract=(1, 0)):
+    dims = (((contract[0],), (contract[1],)), ((), ()))
+    return lax.dot_general(left, right, dims, precision=PRECISE, preferred_element_type=jnp.float32)
+
+
+def pack_kernel(velocity_ref, cotangent_ref, table_ref, out_ref):
+    _, x_rows, y_rows, z_length = velocity_ref.shape
+    block = x_rows * y_rows
+    groups = LANES // block
+    devices = z_length // groups
+    velocity = velocity_ref[...].reshape(3 * block, z_length)
+    cotangent = cotangent_ref[...].reshape(3 * block, z_length)
+    along_z = times(velocity, table_ref[...])
+    fill = jnp.zeros(((-SENT % groups) * block, z_length), jnp.float32)
+    rows = jnp.concatenate(
+        [velocity, along_z, cotangent[block:], cotangent[:block], fill], axis=0
+    )
+    for start in range(0, SENT, groups):
+        turned = rows[start * block : (start + groups) * block].T
+        parts = [turned[group * devices : (group + 1) * devices] for group in range(groups)]
+        parts = exchange(parts, block)
+        for field in range(start, min(start + groups, SENT)):
+            out_ref[pl.ds(field, devices, stride=SENT), :] = parts[field - start]
+
+
+def middle_kernel(x_devices, in_ref, y_ref, weight_in_ref, bias_ref, weight_out_ref, out_ref, tail_ref):
+    y_devices = in_ref.shape[0] // SENT // x_devices
+    x_rows = y_devices
+    x_length = x_devices * x_rows
+    units = weight_in_ref.shape[1]
+    y_rows = y_ref.shape[0] // y_devices
+    row8 = lax.broadcasted_iota(jnp.int32, (8, LANES), 0)
+
+    planes = []
+    for x_device in range(x_devices):
+        first = x_device * y_devices
+        parts = [in_ref[(first + turn) * SENT : (first + turn) * SENT + 8, :] for turn in range(y_devices)]
+        planes.extend(exchange(parts, y_rows))
+    tails = [
+        in_ref[pl.ds(turn * SENT + 8, x_devices, stride=y_devices * SENT), :]
+        for turn in range(y_devices)
+    ]
+    tails = exchange(tails, y_rows)
+
+    groups = LANES // y_ref.shape[0]
+    y_table = y_ref[...]
+    y_wide = jnp.concatenate([jnp.concatenate([y_table] * groups, axis=1)] * groups, axis=0)
+    same = [
+        lax.broadcasted_iota(jnp.int32, (LANES, LANES), dim) // y_ref.shape[0] for dim in (0, 1)
+    ]
+    y_wide = jnp.where(same[0] == same[1], y_wide, 0.0)
+
+    smoothed = smooth_rows(planes)
+    along_y = times(jnp.concatenate(smoothed, axis=0), y_wide, (1, 1))
+    upper_rows = []
+    lower_rows = []
+    for x in range(x_length):
+        features = jnp.where(row8 < 3, along_y[8 * x : 8 * x + 8], smoothed[x])
+        features = jnp.where(row8 < 6, features, jnp.where(row8 == 6, 1.0, 0.0))
+        last = tails[x % x_rows][x // x_rows : x // x_rows + 1]
+        upper_rows.append(features)
+        lower_rows.append(jnp.where(row8 == 5, last, planes[x]))
+
+    weight_out = weight_out_ref[...]
+    weight_in = weight_in_ref[...]
+    zeros = functools.partial(jnp.zeros, dtype=jnp.float32)
+    before = jnp.concatenate(
+        [
+            jnp.concatenate([weight_in, bias_ref[...], zeros((9, units))], axis=0),
+            jnp.concatenate([zeros((13, units)), STEP_SIZE * weight_out], axis=0),
+        ],
+        axis=1,
+    )
+    after = jnp.concatenate(
+        [
+            jnp.concatenate([zeros((6, units)), weight_out, zeros((7, units))], axis=0),
+            jnp.concatenate([weight_in, zeros((10, units))], axis=0),
+        ],
+        axis=1,
+    )
+
+    at_once = 8
+    sums = zeros((16, 2 * units))
+    results = []
+    for start in range(0, x_length, at_once):
+        stop = start + at_once
+        cells = jnp.concatenate(
+            [
+                jnp.concatenate(upper_rows[start:stop], axis=1),
+                jnp.concatenate(lower_rows[start:stop], axis=1),
+            ],
+            axis=0,
+        )
+        both = times(before, cells, (0, 0))
+        hidden = jnp.tanh(both[:units])
+        grad_pre = both[units:] * (1.0 - hidden * hidden)
+        both = jnp.concatenate([hidden, grad_pre], axis=0)
+        sums = sums + times(cells, both, (1, 1))
+        result = times(after, both)
+        for turn in range(at_once):
+            results.append(result[:8, turn * LANES : (turn + 1) * LANES])
+            x = start + turn
+            place = (x % x_rows) * x_devices + x // x_rows
+            tail_ref[place : place + 1, :] = result[8:9, turn * LANES : (turn + 1) * LANES]
+
+    back_y = times(jnp.concatenate(results, axis=0), y_wide)
+    back = [
+        jnp.where(row8 < 3, back_y[8 * x : 8 * x + 8], results[x]) for x in range(x_length)
+    ]
+    back = smooth_rows(back)
+    back = [jnp.where(row8 < 6, value, result) for value, result in zip(back, results)]
+    for x_device in range(x_devices):
+        first = x_device * y_devices
+        parts = exchange(back[first : first + x_rows], y_rows)
+        for turn in range(y_devices):
+            place = (first + turn) * RETURNED
+            out_ref[place : place + 8, :] = parts[turn]
+    tails = [tail_ref[x * x_devices : (x + 1) * x_devices, :] for x in range(x_rows)]
+    tails = exchange(tails, y_rows)
+    for turn in range(y_devices):
+        out_ref[pl.ds(turn * RETURNED + 8, x_devices, stride=y_devices * RETURNED), :] = tails[turn]
+
+    moved = jnp.concatenate([sums[5:7, units:], STEP_SIZE * sums[13:16, :units]], axis=0)
+    packed = jnp.concatenate([sums[:5, units:], moved], axis=1)
+    for device in range(x_devices * y_devices):
+        place = device * RETURNED + SENT
+        out_ref[place : place + 5, :] = packed
+
+
+def unpack_kernel(cells, in_ref, velocity_ref, cotangent_ref, table_ref, new_ref, grad_ref, in_grad_ref, bias_grad_ref, out_grad_ref):
+    _, x_rows, y_rows, z_length = velocity_ref.shape
+    block = x_rows * y_rows
+    groups = LANES // block
+    devices = z_length // groups
+    units = in_grad_ref.shape[1]
+    fields = []
+    for start in range(0, SENT, groups):
+        parts = [
+            in_ref[pl.ds(min(field, SENT - 1), devices, stride=RETURNED), :]
+            for field in range(start, start + groups)
+        ]
+        turned = jnp.concatenate(exchange(parts, block), axis=0).T
+        fields.extend(turned[turn * block : (turn + 1) * block] for turn in range(groups))
+    shape = (3, x_rows, y_rows, z_length)
+    forcing = jnp.concatenate(fields[6:9], axis=0).reshape(shape)
+    new_ref[...] = velocity_ref[...] + STEP_SIZE * forcing
+    back_z = times(jnp.concatenate(fields[3:6], axis=0), table_ref[...])
+    back = jnp.concatenate(fields[:3], axis=0) + back_z
+    grad_ref[...] = cotangent_ref[...] + back.reshape(shape)
+
+    sums = in_ref[SENT : SENT + 5, :]
+    for device in range(1, devices):
+        place = device * RETURNED + SENT
+        sums = sums + in_ref[place : place + 5, :]
+    sums = sums / cells
+    in_grad_ref[:5, :] = sums[:, :units]
+    in_grad_ref[5:, :] = sums[:1, units:]
+    bias_grad_ref[...] = sums[1:2, units:]
+    out_grad_ref[...] = sums[2:, units:]
+
+
+def on_device(kernel, shapes, scratch=()):
+    return pl.pallas_call(
+        kernel,
+        out_shape=[jax.ShapeDtypeStruct(shape, jnp.float32) for shape in shapes],
+        scratch_shapes=[pltpu.VMEM(shape, jnp.float32) for shape in scratch],
+        compiler_params=pltpu.CompilerParams(vmem_limit_bytes=32 * 1024 * 1024),
+    )
+
+
+def fits(velocity, units):
+    x_devices, y_devices = lax.axis_size("gx"), lax.axis_size("gy")
+    _, x_rows, y_rows, z_length = velocity.shape
+    return (
+        z_length == LANES
+        and x_rows * y_rows * LANES == LANES * LANES // 4
+        and x_devices * y_devices * 4 == LANES
+        and x_devices == 8
+        and y_devices == x_rows
+        and y_rows % 8 == 0
+        and 2 * units == LANES
+    )
+
+
+def local_kernels(velocity, cotangent, weight_in, bias_in, weight_out):
+    axes = ("gx", "gy")
+    x_devices, y_devices = lax.axis_size("gx"), lax.axis_size("gy")
+    devices = x_devices * y_devices
+    _, x_rows, y_rows, z_length = velocity.shape
+    units = weight_in.shape[1]
+    cells = x_rows * x_devices * y_rows * y_devices * z_length
+    z_table = derivative_table(z_length)
+
+    (sent,) = on_device(pack_kernel, [(devices * SENT, LANES)])(velocity, cotangent, table(z_table.T))
+    sent = sent.reshape(devices, 1, SENT * LANES)
+    sent = lax.all_to_all(sent, axes, 0, 0, tiled=True).reshape(devices * SENT, LANES)
+    (back,) = on_device(
+        functools.partial(middle_kernel, x_devices),
+        [(devices * RETURNED, LANES)],
+        [(x_devices * x_rows, LANES)],
+    )(sent, table(derivative_table(y_rows * y_devices)), weight_in, bias_in[None], weight_out.T)
+    back = back.reshape(devices, 1, RETURNED * LANES)
+    back = lax.all_to_all(back, axes, 0, 0, tiled=True).reshape(devices * RETURNED, LANES)
+    shapes = [velocity.shape, velocity.shape, (6, units), (1, units), (3, units)]
+    new, grad, grad_in, grad_bias, grad_out = on_device(
+        functools.partial(unpack_kernel, float(cells)), shapes
+    )(back, velocity, cotangent, table(z_table))
+    return (new, grad, grad_in, grad_bias[0], grad_out.T)
+
+
+def local(velocity, cotangent, weight_in, bias_in, weight_out):
+    chosen = local_kernels if fits(velocity, weight_in.shape[1]) else local_plain
+    return chosen(velocity, cotangent, weight_in, bias_in, weight_out)
+
+
 def solution(mesh):
     in_specs = (P(None, "gx", "gy", None), P(None, "gx", "gy", None), P(), P(), P())
     out_specs = (P(None, "gx", "gy", None), P(None, "gx", "gy", None), P(), P(), P())

time: 59.7 us -> 38.2 us (0.64)
  local copies, waits for them, and re-layouts: 16.5 us -> 3.14 us
  matrix products: 9.76 us -> 0 us
  Pallas kernels: 0 us -> 6.69 us
  other arithmetic: 2.41 us -> 0 us
  blocking collectives: 29.7 us -> 27.3 us
    dot_general x12 -> x0, matrix products: 9.76 us -> none  [the longest x1 1.27 us: local(): jnp.dot(weight_out, grad_out, precision=PRECISE) * (1.0 - hidden * hidden)]
    reshape x7 -> x0, local copies, waits for them, and re-layouts: 7.82 us -> none  [the longest x2 4.18 us: local(): fields = fields.reshape(x_devices, y_devices, 9, z_rows, x_rows, y_rows)]
    pallas_call x0 -> x3, Pallas kernels: none -> 6.69 us  [the longest x1 5.21 us: local_kernels(): on_device(functools.partial(middle_kernel, x_devices), [(devices * RETURN...]
    slice x18 -> x0, local copies, waits for them, and re-layouts: 4.14 us -> none  [the longest x5 1.91 us: local(): return (new_velocity, grad_velocity, sums[:6], sums[6], sums[7:].T)]
    unnamed x16 -> x20, local copies, waits for them, and re-layouts: 0.06 us -> 3.14 us
    all_to_all x2, blocking collectives: 29.7 us -> 27.3 us  [the longest x1 15.5 us: local_kernels(): lax.all_to_all(sent, axes, 0, 0, tiled=True).reshape(devices * SENT, LANES)]
    concatenate x4 -> x0, local copies, waits for them, and re-layouts: 1.85 us -> none  [the longest x2 1.66 us: local(): jnp.concatenate([forcing.reshape(3, x_length, z_rows, y_length), back], a...]
    mul x4 -> x0, local copies, waits for them, and re-layouts: 1.27 us -> none  [the longest x2 1.01 us: local(): grad_out = STEP_SIZE * fields[6:].reshape(3, -1)]
where the time goes in v2:
time: 38.2 us; the launch traced here: 37.8 us
  blocking collectives  27.3 us (71%)
  Pallas kernels  6.69 us (18%)
  local copies, waits for them, and re-layouts  3.14 us (8%)
  between operations  0.7 us (2%)
    all_to_all x1, blocking collectives, local_kernels(): lax.all_to_all(sent, axes, 0, 0, tiled=True).reshape(devices * SENT, LANES)  15.5 us
    all_to_all x1, blocking collectives, local_kernels(): lax.all_to_all(back, axes, 0, 0, tiled=True)  11.8 us
    pallas_call x1, Pallas kernels, local_kernels(): on_device(functools.partial(middle_kernel, x_devices), [(devices * RETURN...  5.21 us
    unnamed x20, local copies, waits for them, and re-layouts  3.14 us
    pallas_call x1, Pallas kernels, local_kernels(): on_device(functools.partial(unpack_kernel, float(cells)), shapes)  1.05 us

profile of v2, /device:TPU:0, one launch (start us, length us, event | category | flops | bytes accessed | tf_op | source)
XLA Modules:
  0.0 37.8 jit_solution(11044912637061535426)
XLA Ops:
  0.6 0.0 copy-start
  0.6 0.8 %copy-done = f32[3,4,8,128]{3,2,1,0:T(8,128)S(1)} copy-done((f32[3,4,8,128]{3,2,1,0:T(8,128)S(1)}, f32[3,4,8,128]{3,2,1,0:T(8,128)}, u32[]{:S(2)}) %copy-start) | copy-done | bytes 49176
  1.4 0.0 copy-start.2
  1.4 0.8 %copy-done.2 = f32[3,4,8,128]{3,2,1,0:T(8,128)S(1)} copy-done((f32[3,4,8,128]{3,2,1,0:T(8,128)S(1)}, f32[3,4,8,128]{3,2,1,0:T(8,128)}, u32[]{:S(2)}) %copy-start.2) | copy-done | bytes 49176
  2.2 0.0 copy-start.4
  2.2 0.8 %copy-done.4 = f32[128,128]{1,0:T(8,128)S(1)} copy-done((f32[128,128]{1,0:T(8,128)S(1)}, f32[128,128]{1,0:T(8,128)}, u32[]{:S(2)}) %copy-start.4) | copy-done | bytes 65560
  3.1 0.4 %shard_map.119 = f32[288,128]{1,0:T(8,128)S(1)} custom-call(f32[3,4,8,128]{3,2,1,0:T(8,128)S(1)} %copy-done, f32[3,4,8,128]{3,2,1,0:T(8,128)S(1)} %copy-done.2, f32[128,128]{1,0:T(8,128)S(1)} %copy-done.4), custom_call_target="tpu_custom_call" | custom-call | tf_op jit(solution)/shard_map/pallas_call | solution.py:346
  3.5 0.0 copy-start.6
  3.5 0.0 copy-start.8
  3.5 15.5 %all_to_all.10 = f32[32,1,1152]{2,1,0:T(1,128)S(1)} all-to-all(f32[32,1,1152]{2,1,0:T(1,128)S(1)} %bitcast.11), channel_id=1, replica_groups=mesh['gx'=8,'gy'=4] {'gx','gy'}, dimensions={0} | all-to-all | bytes 294912 | tf_op jit(solution)/shard_map/all_to_all | solution.py:348
  19.1 0.0 copy-start.7
  19.1 0.0 copy-start.9
  19.1 0.0 copy-done.6
  19.1 0.0 copy-done.8
  19.1 0.7 %copy-done.7 = f32[6,64]{1,0:T(8,128)S(1)} copy-done((f32[6,64]{1,0:T(8,128)S(1)}, f32[6,64]{1,0:T(8,128)}, u32[]{:S(2)}) %copy-start.7) | copy-done | bytes 1560
  19.7 0.0 copy-done.9
  19.7 5.2 %shard_map.120 = f32[448,128]{1,0:T(8,128)S(1)} custom-call(f32[288,128]{1,0:T(8,128)S(1)} %bitcast.10, f32[32,32]{1,0:T(8,128)S(1)} %copy-done.6, f32[6,64]{1,0:T(8,128)S(1)} %copy-done.7, f32[1,64]{1,0:T(1,128)S(1)} %bitcast.13, f32[3,64]{1,0:T(4,128)S(1)} %bitcast.12), custom_call_target="tpu_custom_call" | custom-call | tf_op jit(solution)/shard_map/pallas_call | solution.py:349
  25.0 0.0 copy-start.1
  25.0 0.0 copy-start.3
  25.0 0.0 copy-start.5
  25.0 11.8 %all_to_all.11 = f32[32,1,1792]{2,1,0:T(1,128)S(1)} all-to-all(f32[32,1,1792]{2,1,0:T(1,128)S(1)} %bitcast.8), channel_id=1, replica_groups=mesh['gx'=8,'gy'=4] {'gx','gy'}, dimensions={0} | all-to-all | bytes 458752 | tf_op jit(solution)/shard_map/all_to_all | solution.py:355
  36.8 0.0 copy-done.1
  36.8 0.0 copy-done.3
  36.8 0.0 copy-done.5
  36.8 1.1 %shard_map.121 = (f32[3,4,8,128]{3,2,1,0:T(8,128)}, f32[3,4,8,128]{3,2,1,0:T(8,128)}, f32[6,64]{1,0:T(8,128)}, f32[1,64]{1,0:T(1,128)}, f32[3,64]{1,0:T(4,128)}) custom-call(f32[448,128]{1,0:T(8,128)S(1)} %bitcast.9, f32[3,4,8,128]{3,2,1,0:T(8,128)S(1)} %copy-done.1, f32[3,4,8,128]{3,2,1,0:T(8,128)S(1)} %copy-done.3, f32[128,128]{1,0:T(8,128)S(1)} %copy-done.5), custom_call_target="tpu_custom_call" | custom-call | tf_op jit(solution)/shard_map/pallas_call | solution.py:357
Async XLA Ops:
  0.6 0.8 %copy-start = (f32[3,4,8,128]{3,2,1,0:T(8,128)S(1)}, f32[3,4,8,128]{3,2,1,0:T(8,128)}, u32[]{:S(2)}) copy-start(f32[3,4,8,128]{3,2,1,0:T(8,128)} %velocity_ref.3) | copy-start | bytes 147460
  1.4 0.8 %copy-start.2 = (f32[3,4,8,128]{3,2,1,0:T(8,128)S(1)}, f32[3,4,8,128]{3,2,1,0:T(8,128)}, u32[]{:S(2)}) copy-start(f32[3,4,8,128]{3,2,1,0:T(8,128)} %cotangent_ref.3) | copy-start | bytes 147460
  2.2 0.8 %copy-start.4 = (f32[128,128]{1,0:T(8,128)S(1)}, f32[128,128]{1,0:T(8,128)}, u32[]{:S(2)}) copy-start(f32[128,128]{1,0:T(8,128)} %constant.6.clone.table_ref) | copy-start | bytes 196612
  3.5 15.6 %copy-start.6 = (f32[32,32]{1,0:T(8,128)S(1)}, f32[32,32]{1,0:T(8,128)}, u32[]{:S(2)}) copy-start(f32[32,32]{1,0:T(8,128)} %constant.7.clone.y_ref) | copy-start | bytes 12292
  3.5 15.5 %copy-start.8 = (f32[64,3]{0,1:T(4,128)S(1)}, f32[64,3]{0,1:T(4,128)}, u32[]{:S(2)}) copy-start(f32[64,3]{0,1:T(4,128)} %param.12) | copy-start | bytes 2308
  19.1 0.7 %copy-start.7 = (f32[6,64]{1,0:T(8,128)S(1)}, f32[6,64]{1,0:T(8,128)}, u32[]{:S(2)}) copy-start(f32[6,64]{1,0:T(8,128)} %weight_in_ref.1) | copy-start | bytes 4612
  19.1 0.7 %copy-start.9 = (f32[64]{0:T(128)S(1)}, f32[64]{0:T(128)}, u32[]{:S(2)}) copy-start(f32[64]{0:T(128)} %param.11) | copy-start | bytes 772
  25.0 11.8 %copy-start.1 = (f32[3,4,8,128]{3,2,1,0:T(8,128)S(1)}, f32[3,4,8,128]{3,2,1,0:T(8,128)}, u32[]{:S(2)}) copy-start(f32[3,4,8,128]{3,2,1,0:T(8,128)} %velocity_ref.3) | copy-start | bytes 147460
  25.0 11.8 %copy-start.3 = (f32[3,4,8,128]{3,2,1,0:T(8,128)S(1)}, f32[3,4,8,128]{3,2,1,0:T(8,128)}, u32[]{:S(2)}) copy-start(f32[3,4,8,128]{3,2,1,0:T(8,128)} %cotangent_ref.3) | copy-start | bytes 147460
  25.0 11.8 %copy-start.5 = (f32[128,128]{1,0:T(8,128)S(1)}, f32[128,128]{1,0:T(8,128)}, u32[]{:S(2)}) copy-start(f32[128,128]{1,0:T(8,128)} %constant.8.clone.table_ref) | copy-start | bytes 196612

commit v3 on v2

--- a/solution.py
+++ b/solution.py
@@ -2,6 +2,7 @@
 
 import jax
 import jax.numpy as jnp
+import ml_dtypes
 import numpy as np
 from jax import lax
 from jax.experimental import pallas as pl
@@ -16,6 +17,8 @@
 LANES = 128
 SENT = 9
 RETURNED = 14
+LEFT_PIECES = (0, 1, 0, 2, 1, 0)
+RIGHT_PIECES = (0, 0, 1, 0, 1, 2)
 
 
 def beside(length, offset):
@@ -38,6 +41,15 @@
 
 def table(values):
     return jnp.asarray(values.astype(np.float32))
+
+
+def split_table(values):
+    pieces = []
+    rest = values.astype(np.float32)
+    for _ in range(3):
+        pieces.append(rest.astype(ml_dtypes.bfloat16))
+        rest = rest - pieces[-1].astype(np.float32)
+    return jnp.asarray(np.concatenate([pieces[turn] for turn in RIGHT_PIECES], axis=0))
 
 
 def local_plain(velocity, cotangent, weight_in, bias_in, weight_out):
@@ -152,17 +164,72 @@
 
 def times(left, right, contract=(1, 0)):
     dims = (((contract[0],), (contract[1],)), ((), ()))
-    return lax.dot_general(left, right, dims, precision=PRECISE, preferred_element_type=jnp.float32)
-
-
-def pack_kernel(velocity_ref, cotangent_ref, table_ref, out_ref):
+    return lax.dot_general(left, right, dims, preferred_element_type=jnp.float32)
+
+
+def split(values, count):
+    pieces = []
+    for turn in range(count):
+        pieces.append(values.astype(jnp.bfloat16))
+        if turn + 1 < count:
+            values = values - pieces[-1].astype(jnp.float32)
+    return pieces
+
+
+def times_table(values, wide_table):
+    pieces = split(values, 3)
+    return times(jnp.concatenate([pieces[turn] for turn in LEFT_PIECES], axis=1), wide_table)
+
+
+def pack_kernel(
+    velocity_hbm,
+    cotangent_hbm,
+    z_hbm,
+    weight_in_hbm,
+    bias_hbm,
+    weight_out_hbm,
+    y_hbm,
+    y_back_hbm,
+    out_ref,
+    before_ref,
+    after_ref,
+    y_ref,
+    y_back_ref,
+    velocity_ref,
+    cotangent_ref,
+    z_ref,
+    weight_in_ref,
+    bias_ref,
+    weight_out_ref,
+    arrived,
+):
+    pairs = [
+        (velocity_hbm, velocity_ref),
+        (z_hbm, z_ref),
+        (cotangent_hbm, cotangent_ref),
+        (weight_in_hbm, weight_in_ref),
+        (bias_hbm, bias_ref),
+        (weight_out_hbm, weight_out_ref),
+        (y_hbm, y_ref),
+        (y_back_hbm, y_back_ref),
+    ]
+    copies = [
+        pltpu.make_async_copy(source, target, arrived.at[turn])
+        for turn, (source, target) in enumerate(pairs)
+    ]
+    for copy in copies:
+        copy.start()
+
     _, x_rows, y_rows, z_length = velocity_ref.shape
     block = x_rows * y_rows
     groups = LANES // block
     devices = z_length // groups
+    copies[0].wait()
     velocity = velocity_ref[...].reshape(3 * block, z_length)
+    copies[1].wait()
+    along_z = times_table(velocity, z_ref[...])
+    copies[2].wait()
     cotangent = cotangent_ref[...].reshape(3 * block, z_length)
-    along_z = times(velocity, table_ref[...])
     fill = jnp.zeros(((-SENT % groups) * block, z_length), jnp.float32)
     rows = jnp.concatenate(
         [velocity, along_z, cotangent[block:], cotangent[:block], fill], axis=0
@@ -174,19 +241,55 @@
         for field in range(start, min(start + groups, SENT)):
             out_ref[pl.ds(field, devices, stride=SENT), :] = parts[field - start]
 
-
-def middle_kernel(x_devices, in_ref, y_ref, weight_in_ref, bias_ref, weight_out_ref, out_ref, tail_ref):
+    for copy in copies[3:]:
+        copy.wait()
+    weight_in = weight_in_ref[...]
+    weight_out = weight_out_ref[...]
+    units = weight_in.shape[1]
+    zeros = functools.partial(jnp.zeros, dtype=jnp.float32)
+    before = jnp.concatenate(
+        [
+            jnp.concatenate([weight_in, bias_ref[...], zeros((9, units))], axis=0),
+            jnp.concatenate([zeros((13, units)), STEP_SIZE * weight_out], axis=0),
+        ],
+        axis=1,
+    )
+    after = jnp.concatenate(
+        [
+            jnp.concatenate([zeros((6, units)), weight_out, zeros((7, units))], axis=0),
+            jnp.concatenate([weight_in, zeros((10, units))], axis=0),
+        ],
+        axis=1,
+    )
+    pieces = [piece.astype(jnp.float32) for piece in split(before, 3)]
+    before = jnp.concatenate([pieces[turn] for turn in RIGHT_PIECES + (1, 2)], axis=0)
+    before_ref[...] = before.T.astype(jnp.bfloat16)
+    pieces = split(after, 3)
+    after_ref[...] = jnp.concatenate(
+        [
+            jnp.concatenate([pieces[0], pieces[0]], axis=1),
+            jnp.concatenate([pieces[1], pieces[1]], axis=1),
+            jnp.concatenate([pieces[2], jnp.zeros_like(pieces[2])], axis=1),
+        ],
+        axis=0,
+    )
+
+
+def middle_kernel(x_devices, in_ref, before_ref, after_ref, y_ref, y_back_ref, out_ref, tail_ref):
     y_devices = in_ref.shape[0] // SENT // x_devices
     x_rows = y_devices
     x_length = x_devices * x_rows
-    units = weight_in_ref.shape[1]
-    y_rows = y_ref.shape[0] // y_devices
+    units = before_ref.shape[0] // 2
+    y_rows = LANES // y_devices // x_rows
     row8 = lax.broadcasted_iota(jnp.int32, (8, LANES), 0)
 
     planes = []
     for x_device in range(x_devices):
         first = x_device * y_devices
-        parts = [in_ref[(first + turn) * SENT : (first + turn) * SENT + 8, :] for turn in range(y_devices)]
+        parts = [
+            in_ref[(first + turn) * SENT : (first + turn) * SENT + 8, :]
+            for turn in range(y_devices)
+        ]
         planes.extend(exchange(parts, y_rows))
     tails = [
         in_ref[pl.ds(turn * SENT + 8, x_devices, stride=y_devices * SENT), :]
@@ -194,16 +297,8 @@
     ]
     tails = exchange(tails, y_rows)
 
-    groups = LANES // y_ref.shape[0]
-    y_table = y_ref[...]
-    y_wide = jnp.concatenate([jnp.concatenate([y_table] * groups, axis=1)] * groups, axis=0)
-    same = [
-        lax.broadcasted_iota(jnp.int32, (LANES, LANES), dim) // y_ref.shape[0] for dim in (0, 1)
-    ]
-    y_wide = jnp.where(same[0] == same[1], y_wide, 0.0)
-
     smoothed = smooth_rows(planes)
-    along_y = times(jnp.concatenate(smoothed, axis=0), y_wide, (1, 1))
+    along_y = times_table(jnp.concatenate(smoothed, axis=0), y_ref[...])
     upper_rows = []
     lower_rows = []
     for x in range(x_length):
@@ -213,26 +308,10 @@
         upper_rows.append(features)
         lower_rows.append(jnp.where(row8 == 5, last, planes[x]))
 
-    weight_out = weight_out_ref[...]
-    weight_in = weight_in_ref[...]
-    zeros = functools.partial(jnp.zeros, dtype=jnp.float32)
-    before = jnp.concatenate(
-        [
-            jnp.concatenate([weight_in, bias_ref[...], zeros((9, units))], axis=0),
-            jnp.concatenate([zeros((13, units)), STEP_SIZE * weight_out], axis=0),
-        ],
-        axis=1,
-    )
-    after = jnp.concatenate(
-        [
-            jnp.concatenate([zeros((6, units)), weight_out, zeros((7, units))], axis=0),
-            jnp.concatenate([weight_in, zeros((10, units))], axis=0),
-        ],
-        axis=1,
-    )
-
+    before = before_ref[...]
+    after = after_ref[...]
     at_once = 8
-    sums = zeros((16, 2 * units))
+    sums = jnp.zeros((32, 4 * units), jnp.float32)
     results = []
     for start in range(0, x_length, at_once):
         stop = start + at_once
@@ -243,19 +322,22 @@
             ],
             axis=0,
         )
-        both = times(before, cells, (0, 0))
+        pieces = split(cells, 3)
+        both = times(before, jnp.concatenate([pieces[turn] for turn in LEFT_PIECES + (2, 1)], axis=0))
         hidden = jnp.tanh(both[:units])
         grad_pre = both[units:] * (1.0 - hidden * hidden)
         both = jnp.concatenate([hidden, grad_pre], axis=0)
-        sums = sums + times(cells, both, (1, 1))
+        both = jnp.concatenate(split(both, 2), axis=0)
+        sums = sums + times(jnp.concatenate(pieces[:2], axis=0), both, (1, 1))
         result = times(after, both)
+        result = result[:16] + result[16:32] + result[32:]
         for turn in range(at_once):
             results.append(result[:8, turn * LANES : (turn + 1) * LANES])
             x = start + turn
             place = (x % x_rows) * x_devices + x // x_rows
             tail_ref[place : place + 1, :] = result[8:9, turn * LANES : (turn + 1) * LANES]
 
-    back_y = times(jnp.concatenate(results, axis=0), y_wide)
+    back_y = times_table(jnp.concatenate(results, axis=0), y_back_ref[...])
     back = [
         jnp.where(row8 < 3, back_y[8 * x : 8 * x + 8], results[x]) for x in range(x_length)
     ]
@@ -272,6 +354,8 @@
     for turn in range(y_devices):
         out_ref[pl.ds(turn * RETURNED + 8, x_devices, stride=y_devices * RETURNED), :] = tails[turn]
 
+    sums = sums[:, : 2 * units] + sums[:, 2 * units :]
+    sums = sums[:16] + sums[16:]
     moved = jnp.concatenate([sums[5:7, units:], STEP_SIZE * sums[13:16, :units]], axis=0)
     packed = jnp.concatenate([sums[:5, units:], moved], axis=1)
     for device in range(x_devices * y_devices):
@@ -279,7 +363,18 @@
         out_ref[place : place + 5, :] = packed
 
 
-def unpack_kernel(cells, in_ref, velocity_ref, cotangent_ref, table_ref, new_ref, grad_ref, in_grad_ref, bias_grad_ref, out_grad_ref):
+def unpack_kernel(
+    cells,
+    in_ref,
+    velocity_ref,
+    cotangent_ref,
+    z_ref,
+    new_ref,
+    grad_ref,
+    in_grad_ref,
+    bias_grad_ref,
+    out_grad_ref,
+):
     _, x_rows, y_rows, z_length = velocity_ref.shape
     block = x_rows * y_rows
     groups = LANES // block
@@ -296,7 +391,7 @@
     shape = (3, x_rows, y_rows, z_length)
     forcing = jnp.concatenate(fields[6:9], axis=0).reshape(shape)
     new_ref[...] = velocity_ref[...] + STEP_SIZE * forcing
-    back_z = times(jnp.concatenate(fields[3:6], axis=0), table_ref[...])
+    back_z = times_table(jnp.concatenate(fields[3:6], axis=0), z_ref[...])
     back = jnp.concatenate(fields[:3], axis=0) + back_z
     grad_ref[...] = cotangent_ref[...] + back.reshape(shape)
 
@@ -311,12 +406,13 @@
     out_grad_ref[...] = sums[2:, units:]
 
 
-def on_device(kernel, shapes, scratch=()):
+def on_device(kernel, shapes, scratch=(), **more):
     return pl.pallas_call(
         kernel,
-        out_shape=[jax.ShapeDtypeStruct(shape, jnp.float32) for shape in shapes],
-        scratch_shapes=[pltpu.VMEM(shape, jnp.float32) for shape in scratch],
+        out_shape=[jax.ShapeDtypeStruct(shape, kind) for shape, kind in shapes],
+        scratch_shapes=[*scratch],
         compiler_params=pltpu.CompilerParams(vmem_limit_bytes=32 * 1024 * 1024),
+        **more,
     )
 
 
@@ -342,21 +438,47 @@
     units = weight_in.shape[1]
     cells = x_rows * x_devices * y_rows * y_devices * z_length
     z_table = derivative_table(z_length)
-
-    (sent,) = on_device(pack_kernel, [(devices * SENT, LANES)])(velocity, cotangent, table(z_table.T))
+    y_table = np.kron(np.eye(z_length // devices), derivative_table(y_rows * y_devices))
+    single, half = jnp.float32, jnp.bfloat16
+    wide = len(LEFT_PIECES) * LANES
+
+    arguments = [
+        velocity,
+        cotangent,
+        split_table(z_table.T),
+        weight_in,
+        bias_in[None],
+        weight_out.T,
+        split_table(y_table.T),
+        split_table(y_table),
+    ]
+    arguments = [pltpu.with_memory_space_constraint(each, pltpu.HBM) for each in arguments]
+    sent, *prepared = on_device(
+        pack_kernel,
+        [
+            ((devices * SENT, LANES), single),
+            ((2 * units, LANES), half),
+            ((48, 4 * units), half),
+            ((wide, LANES), half),
+            ((wide, LANES), half),
+        ],
+        [pltpu.VMEM(values.shape, values.dtype) for values in arguments[:6]]
+        + [pltpu.SemaphoreType.DMA((len(arguments),))],
+        in_specs=[pl.BlockSpec(memory_space=pltpu.HBM)] * len(arguments),
+    )(*arguments)
     sent = sent.reshape(devices, 1, SENT * LANES)
     sent = lax.all_to_all(sent, axes, 0, 0, tiled=True).reshape(devices * SENT, LANES)
     (back,) = on_device(
         functools.partial(middle_kernel, x_devices),
-        [(devices * RETURNED, LANES)],
-        [(x_devices * x_rows, LANES)],
-    )(sent, table(derivative_table(y_rows * y_devices)), weight_in, bias_in[None], weight_out.T)
+        [((devices * RETURNED, LANES), single)],
+        [pltpu.VMEM((x_devices * x_rows, LANES), single)],
+    )(sent, *prepared)
     back = back.reshape(devices, 1, RETURNED * LANES)
     back = lax.all_to_all(back, axes, 0, 0, tiled=True).reshape(devices * RETURNED, LANES)
     shapes = [velocity.shape, velocity.shape, (6, units), (1, units), (3, units)]
     new, grad, grad_in, grad_bias, grad_out = on_device(
-        functools.partial(unpack_kernel, float(cells)), shapes
-    )(back, velocity, cotangent, table(z_table))
+        functools.partial(unpack_kernel, float(cells)), [(shape, single) for shape in shapes]
+    )(back, velocity, cotangent, split_table(z_table))
     return (new, grad, grad_in, grad_bias[0], grad_out.T)
 
 

time: 38.2 us -> 33.1 us (0.87)
  local copies, waits for them, and re-layouts: 3.14 us -> 0.02 us
  Pallas kernels: 6.69 us -> 4.91 us
    unnamed x20 -> x6, local copies, waits for them, and re-layouts: 3.14 us -> 0.02 us
    pallas_call x3, Pallas kernels: 6.69 us -> 4.91 us  [the longest x1 2.14 us: local_kernels(): on_device(functools.partial(middle_kernel, x_devices), [((devices * RETUR...]
where the time goes in v3:
time: 33.1 us; the launch traced here: 32.9 us
  blocking collectives  27.3 us (82%)
  Pallas kernels  4.91 us (15%)
  between operations  0.68 us (2%)
    all_to_all x1, blocking collectives, local_kernels(): lax.all_to_all(sent, axes, 0, 0, tiled=True).reshape(devices * SENT, LANES)  15.5 us
    all_to_all x1, blocking collectives, local_kernels(): lax.all_to_all(back, axes, 0, 0, tiled=True)  11.8 us
    pallas_call x1, Pallas kernels, local_kernels(): on_device(functools.partial(middle_kernel, x_devices), [((devices * RETUR...  2.14 us
    pallas_call x1, Pallas kernels, local_kernels(): on_device(pack_kernel, [((devices * SENT, LANES), single), ((2 * units, L...  1.71 us
    pallas_call x1, Pallas kernels, local_kernels(): on_device(functools.partial(unpack_kernel, float(cells)), [(shape, single...  1.06 us

profile of v3, /device:TPU:0, one launch (start us, length us, event | category | flops | bytes accessed | tf_op | source)
XLA Modules:
  0.0 32.9 jit_solution(12867538611328469101)
XLA Ops:
  0.6 1.7 %shard_map.128 = (f32[288,128]{1,0:T(8,128)S(1)}, bf16[128,128]{1,0:T(8,128)(2,1)S(1)}, bf16[48,256]{1,0:T(8,128)(2,1)S(1)}, bf16[768,128]{1,0:T(8,128)(2,1)S(1)}, bf16[768,128]{1,0:T(8,128)(2,1)S(1)}) custom-call(f32[3,4,8,128]{3,2,1,0:T(8,128)} %velocity_ref.1, f32[3,4,8,128]{3,2,1,0:T(8,128)} %cotangent_ref.1, bf16[768,128]{1,0:T(8,128)(2,1)} %constant.8.clone.z_hbm, ...), custom_call_target="tpu_custom_call" | custom-call | tf_op jit(solution)/shard_map/pallas_call | solution.py:456
  2.3 15.5 %all_to_all.10 = f32[32,1,1152]{2,1,0:T(1,128)S(1)} all-to-all(f32[32,1,1152]{2,1,0:T(1,128)S(1)} %bitcast.11), channel_id=1, replica_groups=mesh['gx'=8,'gy'=4] {'gx','gy'}, dimensions={0} | all-to-all | bytes 294912 | tf_op jit(solution)/shard_map/all_to_all | solution.py:470
  17.9 2.1 %shard_map.129 = f32[448,128]{1,0:T(8,128)S(1)} custom-call(f32[288,128]{1,0:T(8,128)S(1)} %bitcast.10, bf16[128,128]{1,0:T(8,128)(2,1)S(1)} %get-tuple-element.16.before_ref, bf16[48,256]{1,0:T(8,128)(2,1)S(1)} %get-tuple-element.17.after_ref, bf16[768,128]{1,0:T(8,128)(2,1)S(1)} %get-tuple-element.18.y_ref, bf16[768,128]{1,0:T(8,128)(2,1)S(1)} %get-tuple-element.19.y_back_ref), custom_call_target="tpu_custom_call" | custom-call | tf_op jit(solution)/shard_map/pallas_call | solution.py:471
  20.0 0.0 copy-start
  20.0 0.0 copy-start.1
  20.0 0.0 copy-start.2
  20.1 11.8 %all_to_all.11 = f32[32,1,1792]{2,1,0:T(1,128)S(1)} all-to-all(f32[32,1,1792]{2,1,0:T(1,128)S(1)} %bitcast.9), channel_id=1, replica_groups=mesh['gx'=8,'gy'=4] {'gx','gy'}, dimensions={0} | all-to-all | bytes 458752 | tf_op jit(solution)/shard_map/all_to_all | solution.py:477
  31.8 0.0 copy-done
  31.8 0.0 copy-done.1
  31.8 0.0 copy-done.2
  31.8 1.1 %shard_map.130 = (f32[3,4,8,128]{3,2,1,0:T(8,128)}, f32[3,4,8,128]{3,2,1,0:T(8,128)}, f32[6,64]{1,0:T(8,128)}, f32[1,64]{1,0:T(1,128)}, f32[3,64]{1,0:T(4,128)}) custom-call(f32[448,128]{1,0:T(8,128)S(1)} %bitcast.8, f32[3,4,8,128]{3,2,1,0:T(8,128)S(1)} %copy-done, f32[3,4,8,128]{3,2,1,0:T(8,128)S(1)} %copy-done.1, bf16[768,128]{1,0:T(8,128)(2,1)S(1)} %copy-done.2), custom_call_target="tpu_custom_call" | custom-call | tf_op jit(solution)/shard_map/pallas_call | solution.py:479
Async XLA Ops:
  20.0 11.8 %copy-start = (f32[3,4,8,128]{3,2,1,0:T(8,128)S(1)}, f32[3,4,8,128]{3,2,1,0:T(8,128)}, u32[]{:S(2)}) copy-start(f32[3,4,8,128]{3,2,1,0:T(8,128)} %velocity_ref.1) | copy-start | bytes 147460
  20.0 11.8 %copy-start.1 = (f32[3,4,8,128]{3,2,1,0:T(8,128)S(1)}, f32[3,4,8,128]{3,2,1,0:T(8,128)}, u32[]{:S(2)}) copy-start(f32[3,4,8,128]{3,2,1,0:T(8,128)} %cotangent_ref.1) | copy-start | bytes 147460
  20.0 11.8 %copy-start.2 = (bf16[768,128]{1,0:T(8,128)(2,1)S(1)}, bf16[768,128]{1,0:T(8,128)(2,1)}, u32[]{:S(2)}) copy-start(bf16[768,128]{1,0:T(8,128)(2,1)} %constant.11.clone.z_ref) | copy-start | bytes 589828

commit v4 on v3

--- a/solution.py
+++ b/solution.py
@@ -2,7 +2,6 @@
 
 import jax
 import jax.numpy as jnp
-import ml_dtypes
 import numpy as np
 from jax import lax
 from jax.experimental import pallas as pl
@@ -41,15 +40,6 @@
 
 def table(values):
     return jnp.asarray(values.astype(np.float32))
-
-
-def split_table(values):
-    pieces = []
-    rest = values.astype(np.float32)
-    for _ in range(3):
-        pieces.append(rest.astype(ml_dtypes.bfloat16))
-        rest = rest - pieces[-1].astype(np.float32)
-    return jnp.asarray(np.concatenate([pieces[turn] for turn in RIGHT_PIECES], axis=0))
 
 
 def local_plain(velocity, cotangent, weight_in, bias_in, weight_out):
@@ -176,9 +166,13 @@
     return pieces
 
 
-def times_table(values, wide_table):
+def times_table(values, square_table, turned=False):
     pieces = split(values, 3)
-    return times(jnp.concatenate([pieces[turn] for turn in LEFT_PIECES], axis=1), wide_table)
+    left = jnp.concatenate([pieces[turn] for turn in LEFT_PIECES], axis=1)
+    pieces = split(square_table, 3)
+    axis = 1 if turned else 0
+    right = jnp.concatenate([pieces[turn] for turn in RIGHT_PIECES], axis=axis)
+    return times(left, right, (1, axis))
 
 
 def pack_kernel(
@@ -189,12 +183,10 @@
     bias_hbm,
     weight_out_hbm,
     y_hbm,
-    y_back_hbm,
     out_ref,
     before_ref,
     after_ref,
     y_ref,
-    y_back_ref,
     velocity_ref,
     cotangent_ref,
     z_ref,
@@ -205,13 +197,12 @@
 ):
     pairs = [
         (velocity_hbm, velocity_ref),
+        (cotangent_hbm, cotangent_ref),
         (z_hbm, z_ref),
-        (cotangent_hbm, cotangent_ref),
         (weight_in_hbm, weight_in_ref),
         (bias_hbm, bias_ref),
         (weight_out_hbm, weight_out_ref),
         (y_hbm, y_ref),
-        (y_back_hbm, y_back_ref),
     ]
     copies = [
         pltpu.make_async_copy(source, target, arrived.at[turn])
@@ -219,17 +210,16 @@
     ]
     for copy in copies:
         copy.start()
+    for copy in copies:
+        copy.wait()
 
     _, x_rows, y_rows, z_length = velocity_ref.shape
     block = x_rows * y_rows
     groups = LANES // block
     devices = z_length // groups
-    copies[0].wait()
     velocity = velocity_ref[...].reshape(3 * block, z_length)
-    copies[1].wait()
-    along_z = times_table(velocity, z_ref[...])
-    copies[2].wait()
     cotangent = cotangent_ref[...].reshape(3 * block, z_length)
+    along_z = times_table(velocity, z_ref[...], turned=True)
     fill = jnp.zeros(((-SENT % groups) * block, z_length), jnp.float32)
     rows = jnp.concatenate(
         [velocity, along_z, cotangent[block:], cotangent[:block], fill], axis=0
@@ -241,8 +231,6 @@
         for field in range(start, min(start + groups, SENT)):
             out_ref[pl.ds(field, devices, stride=SENT), :] = parts[field - start]
 
-    for copy in copies[3:]:
-        copy.wait()
     weight_in = weight_in_ref[...]
     weight_out = weight_out_ref[...]
     units = weight_in.shape[1]
@@ -275,7 +263,7 @@
     )
 
 
-def middle_kernel(x_devices, in_ref, before_ref, after_ref, y_ref, y_back_ref, out_ref, tail_ref):
+def middle_kernel(x_devices, in_ref, before_ref, after_ref, y_ref, out_ref, tail_ref):
     y_devices = in_ref.shape[0] // SENT // x_devices
     x_rows = y_devices
     x_length = x_devices * x_rows
@@ -298,7 +286,7 @@
     tails = exchange(tails, y_rows)
 
     smoothed = smooth_rows(planes)
-    along_y = times_table(jnp.concatenate(smoothed, axis=0), y_ref[...])
+    along_y = times_table(jnp.concatenate(smoothed, axis=0), y_ref[...], turned=True)
     upper_rows = []
     lower_rows = []
     for x in range(x_length):
@@ -337,7 +325,7 @@
             place = (x % x_rows) * x_devices + x // x_rows
             tail_ref[place : place + 1, :] = result[8:9, turn * LANES : (turn + 1) * LANES]
 
-    back_y = times_table(jnp.concatenate(results, axis=0), y_back_ref[...])
+    back_y = times_table(jnp.concatenate(results, axis=0), y_ref[...])
     back = [
         jnp.where(row8 < 3, back_y[8 * x : 8 * x + 8], results[x]) for x in range(x_length)
     ]
@@ -369,17 +357,49 @@
     velocity_ref,
     cotangent_ref,
     z_ref,
+    new_hbm,
+    grad_hbm,
+    in_grad_hbm,
+    bias_grad_hbm,
+    out_grad_hbm,
     new_ref,
     grad_ref,
     in_grad_ref,
     bias_grad_ref,
     out_grad_ref,
+    arrived,
 ):
+    pairs = [
+        (new_ref, new_hbm),
+        (grad_ref, grad_hbm),
+        (in_grad_ref, in_grad_hbm),
+        (bias_grad_ref, bias_grad_hbm),
+        (out_grad_ref, out_grad_hbm),
+    ]
+    copies = [
+        pltpu.make_async_copy(source, target, arrived.at[turn])
+        for turn, (source, target) in enumerate(pairs)
+    ]
     _, x_rows, y_rows, z_length = velocity_ref.shape
     block = x_rows * y_rows
     groups = LANES // block
     devices = z_length // groups
     units = in_grad_ref.shape[1]
+
+    sums = [
+        in_ref[device * RETURNED + SENT : device * RETURNED + SENT + 5, :]
+        for device in range(devices)
+    ]
+    while len(sums) > 1:
+        sums = [sum(sums[start : start + 2]) for start in range(0, len(sums), 2)]
+    sums = sums[0] * (1.0 / cells)
+    in_grad_ref[:5, :] = sums[:, :units]
+    in_grad_ref[5:, :] = sums[:1, units:]
+    bias_grad_ref[...] = sums[1:2, units:]
+    out_grad_ref[...] = sums[2:, units:]
+    for copy in copies[2:]:
+        copy.start()
+
     fields = []
     for start in range(0, SENT, groups):
         parts = [
@@ -390,20 +410,14 @@
         fields.extend(turned[turn * block : (turn + 1) * block] for turn in range(groups))
     shape = (3, x_rows, y_rows, z_length)
     forcing = jnp.concatenate(fields[6:9], axis=0).reshape(shape)
+    back_z = times_table(jnp.concatenate(fields[3:6], axis=0), z_ref[...])
     new_ref[...] = velocity_ref[...] + STEP_SIZE * forcing
-    back_z = times_table(jnp.concatenate(fields[3:6], axis=0), z_ref[...])
+    copies[0].start()
     back = jnp.concatenate(fields[:3], axis=0) + back_z
     grad_ref[...] = cotangent_ref[...] + back.reshape(shape)
-
-    sums = in_ref[SENT : SENT + 5, :]
-    for device in range(1, devices):
-        place = device * RETURNED + SENT
-        sums = sums + in_ref[place : place + 5, :]
-    sums = sums / cells
-    in_grad_ref[:5, :] = sums[:, :units]
-    in_grad_ref[5:, :] = sums[:1, units:]
-    bias_grad_ref[...] = sums[1:2, units:]
-    out_grad_ref[...] = sums[2:, units:]
+    copies[1].start()
+    for copy in copies:
+        copy.wait()
 
 
 def on_device(kernel, shapes, scratch=(), **more):
@@ -440,17 +454,17 @@
     z_table = derivative_table(z_length)
     y_table = np.kron(np.eye(z_length // devices), derivative_table(y_rows * y_devices))
     single, half = jnp.float32, jnp.bfloat16
-    wide = len(LEFT_PIECES) * LANES
+
+    in_place = pl.BlockSpec(memory_space=pltpu.HBM)
 
     arguments = [
         velocity,
         cotangent,
-        split_table(z_table.T),
+        table(z_table),
         weight_in,
         bias_in[None],
         weight_out.T,
-        split_table(y_table.T),
-        split_table(y_table),
+        table(y_table),
     ]
     arguments = [pltpu.with_memory_space_constraint(each, pltpu.HBM) for each in arguments]
     sent, *prepared = on_device(
@@ -459,12 +473,11 @@
             ((devices * SENT, LANES), single),
             ((2 * units, LANES), half),
             ((48, 4 * units), half),
-            ((wide, LANES), half),
-            ((wide, LANES), half),
+            ((LANES, LANES), single),
         ],
         [pltpu.VMEM(values.shape, values.dtype) for values in arguments[:6]]
         + [pltpu.SemaphoreType.DMA((len(arguments),))],
-        in_specs=[pl.BlockSpec(memory_space=pltpu.HBM)] * len(arguments),
+        in_specs=[in_place] * len(arguments),
     )(*arguments)
     sent = sent.reshape(devices, 1, SENT * LANES)
     sent = lax.all_to_all(sent, axes, 0, 0, tiled=True).reshape(devices * SENT, LANES)
@@ -477,8 +490,12 @@
     back = lax.all_to_all(back, axes, 0, 0, tiled=True).reshape(devices * RETURNED, LANES)
     shapes = [velocity.shape, velocity.shape, (6, units), (1, units), (3, units)]
     new, grad, grad_in, grad_bias, grad_out = on_device(
-        functools.partial(unpack_kernel, float(cells)), [(shape, single) for shape in shapes]
-    )(back, velocity, cotangent, split_table(z_table))
+        functools.partial(unpack_kernel, float(cells)),
+        [(shape, single) for shape in shapes],
+        [pltpu.VMEM(shape, single) for shape in shapes]
+        + [pltpu.SemaphoreType.DMA((len(shapes),))],
+        out_specs=[in_place] * len(shapes),
+    )(back, velocity, cotangent, table(z_table))
     return (new, grad, grad_in, grad_bias[0], grad_out.T)
 
 

time: 33.1 us -> 33.2 us (level)
  no operation moved by 1% of the time
where the time goes in v4:
time: 33.2 us; the launch traced here: 32.9 us
  blocking collectives  27.3 us (82%)
  Pallas kernels  4.94 us (15%)
  between operations  0.68 us (2%)
    all_to_all x1, blocking collectives, local_kernels(): lax.all_to_all(sent, axes, 0, 0, tiled=True).reshape(devices * SENT, LANES)  15.5 us
    all_to_all x1, blocking collectives, local_kernels(): lax.all_to_all(back, axes, 0, 0, tiled=True)  11.8 us
    pallas_call x1, Pallas kernels, local_kernels(): on_device(functools.partial(middle_kernel, x_devices), [((devices * RETUR...  2.29 us
    pallas_call x1, Pallas kernels, local_kernels(): on_device(pack_kernel, [((devices * SENT, LANES), single), ((2 * units, L...  1.53 us
    pallas_call x1, Pallas kernels, local_kernels(): on_device(functools.partial(unpack_kernel, float(cells)), [(shape, single...  1.12 us

profile of v4, /device:TPU:0, one launch (start us, length us, event | category | flops | bytes accessed | tf_op | source)
XLA Modules:
  0.0 32.9 jit_solution(837284975421978086)
XLA Ops:
  0.6 1.5 %shard_map.119 = (f32[288,128]{1,0:T(8,128)S(1)}, bf16[128,128]{1,0:T(8,128)(2,1)S(1)}, bf16[48,256]{1,0:T(8,128)(2,1)S(1)}, f32[128,128]{1,0:T(8,128)S(1)}) custom-call(f32[3,4,8,128]{3,2,1,0:T(8,128)} %velocity_ref.1, f32[3,4,8,128]{3,2,1,0:T(8,128)} %cotangent_ref.1, f32[128,128]{1,0:T(8,128)} %constant.4.clone.z_hbm.z_ref, f32[6,64]{1,0:T(8,128)} %weight_in_hbm.1, ...), custom_call_target="tpu_custom_call" | custom-call | tf_op jit(solution)/shard_map/pallas_call | solution.py:470
  2.2 15.5 %all_to_all.10 = f32[32,1,1152]{2,1,0:T(1,128)S(1)} all-to-all(f32[32,1,1152]{2,1,0:T(1,128)S(1)} %bitcast.11), channel_id=1, replica_groups=mesh['gx'=8,'gy'=4] {'gx','gy'}, dimensions={0} | all-to-all | bytes 294912 | tf_op jit(solution)/shard_map/all_to_all | solution.py:483
  17.7 2.3 %shard_map.120 = f32[448,128]{1,0:T(8,128)S(1)} custom-call(f32[288,128]{1,0:T(8,128)S(1)} %bitcast.10, bf16[128,128]{1,0:T(8,128)(2,1)S(1)} %get-tuple-element.15.before_ref, bf16[48,256]{1,0:T(8,128)(2,1)S(1)} %get-tuple-element.16.after_ref, f32[128,128]{1,0:T(8,128)S(1)} %get-tuple-element.17.y_ref), custom_call_target="tpu_custom_call" | custom-call | tf_op jit(solution)/shard_map/pallas_call | solution.py:484
  20.0 0.0 copy-start
  20.0 0.0 copy-start.1
  20.0 0.0 copy-start.2
  20.0 11.8 %all_to_all.11 = f32[32,1,1792]{2,1,0:T(1,128)S(1)} all-to-all(f32[32,1,1792]{2,1,0:T(1,128)S(1)} %bitcast.9), channel_id=1, replica_groups=mesh['gx'=8,'gy'=4] {'gx','gy'}, dimensions={0} | all-to-all | bytes 458752 | tf_op jit(solution)/shard_map/all_to_all | solution.py:490
  31.8 0.0 copy-done
  31.8 0.0 copy-done.1
  31.8 0.0 copy-done.2
  31.8 1.1 %shard_map.121 = (f32[3,4,8,128]{3,2,1,0:T(8,128)}, f32[3,4,8,128]{3,2,1,0:T(8,128)}, f32[6,64]{1,0:T(8,128)}, f32[1,64]{1,0:T(1,128)}, f32[3,64]{1,0:T(4,128)}) custom-call(f32[448,128]{1,0:T(8,128)S(1)} %bitcast.8, f32[3,4,8,128]{3,2,1,0:T(8,128)S(1)} %copy-done.1, f32[3,4,8,128]{3,2,1,0:T(8,128)S(1)} %copy-done.2, f32[128,128]{1,0:T(8,128)S(1)} %copy-done), custom_call_target="tpu_custom_call" | custom-call | tf_op jit(solution)/shard_map/pallas_call | solution.py:492
Async XLA Ops:
  20.0 11.8 %copy-start = (f32[128,128]{1,0:T(8,128)S(1)}, f32[128,128]{1,0:T(8,128)}, u32[]{:S(2)}) copy-start(f32[128,128]{1,0:T(8,128)} %constant.4.clone.z_hbm.z_ref) | copy-start | bytes 196612
  20.0 11.8 %copy-start.1 = (f32[3,4,8,128]{3,2,1,0:T(8,128)S(1)}, f32[3,4,8,128]{3,2,1,0:T(8,128)}, u32[]{:S(2)}) copy-start(f32[3,4,8,128]{3,2,1,0:T(8,128)} %velocity_ref.1) | copy-start | bytes 147460
  20.0 11.8 %copy-start.2 = (f32[3,4,8,128]{3,2,1,0:T(8,128)S(1)}, f32[3,4,8,128]{3,2,1,0:T(8,128)}, u32[]{:S(2)}) copy-start(f32[3,4,8,128]{3,2,1,0:T(8,128)} %cotangent_ref.1) | copy-start | bytes 147460

commit v5 on v3

--- a/solution.py
+++ b/solution.py
@@ -181,6 +181,11 @@
     return times(jnp.concatenate([pieces[turn] for turn in LEFT_PIECES], axis=1), wide_table)
 
 
+def widened(square_table):
+    pieces = split(square_table, 3)
+    return jnp.concatenate([pieces[turn] for turn in RIGHT_PIECES], axis=0)
+
+
 def pack_kernel(
     velocity_hbm,
     cotangent_hbm,
@@ -188,13 +193,9 @@
     weight_in_hbm,
     bias_hbm,
     weight_out_hbm,
-    y_hbm,
-    y_back_hbm,
     out_ref,
     before_ref,
     after_ref,
-    y_ref,
-    y_back_ref,
     velocity_ref,
     cotangent_ref,
     z_ref,
@@ -205,13 +206,11 @@
 ):
     pairs = [
         (velocity_hbm, velocity_ref),
+        (cotangent_hbm, cotangent_ref),
         (z_hbm, z_ref),
-        (cotangent_hbm, cotangent_ref),
         (weight_in_hbm, weight_in_ref),
         (bias_hbm, bias_ref),
         (weight_out_hbm, weight_out_ref),
-        (y_hbm, y_ref),
-        (y_back_hbm, y_back_ref),
     ]
     copies = [
         pltpu.make_async_copy(source, target, arrived.at[turn])
@@ -219,17 +218,16 @@
     ]
     for copy in copies:
         copy.start()
+    for copy in copies:
+        copy.wait()
 
     _, x_rows, y_rows, z_length = velocity_ref.shape
     block = x_rows * y_rows
     groups = LANES // block
     devices = z_length // groups
-    copies[0].wait()
     velocity = velocity_ref[...].reshape(3 * block, z_length)
-    copies[1].wait()
-    along_z = times_table(velocity, z_ref[...])
-    copies[2].wait()
     cotangent = cotangent_ref[...].reshape(3 * block, z_length)
+    along_z = times_table(velocity, widened(z_ref[...]))
     fill = jnp.zeros(((-SENT % groups) * block, z_length), jnp.float32)
     rows = jnp.concatenate(
         [velocity, along_z, cotangent[block:], cotangent[:block], fill], axis=0
@@ -241,8 +239,6 @@
         for field in range(start, min(start + groups, SENT)):
             out_ref[pl.ds(field, devices, stride=SENT), :] = parts[field - start]
 
-    for copy in copies[3:]:
-        copy.wait()
     weight_in = weight_in_ref[...]
     weight_out = weight_out_ref[...]
     units = weight_in.shape[1]
@@ -285,14 +281,11 @@
 
     planes = []
     for x_device in range(x_devices):
-        first = x_device * y_devices
-        parts = [
-            in_ref[(first + turn) * SENT : (first + turn) * SENT + 8, :]
-            for turn in range(y_devices)
-        ]
+        places = [(turn * x_devices + x_device) * SENT for turn in range(y_devices)]
+        parts = [in_ref[place : place + 8, :] for place in places]
         planes.extend(exchange(parts, y_rows))
     tails = [
-        in_ref[pl.ds(turn * SENT + 8, x_devices, stride=y_devices * SENT), :]
+        in_ref[pl.ds(turn * x_devices * SENT + 8, x_devices, stride=SENT), :]
         for turn in range(y_devices)
     ]
     tails = exchange(tails, y_rows)
@@ -344,15 +337,16 @@
     back = smooth_rows(back)
     back = [jnp.where(row8 < 6, value, result) for value, result in zip(back, results)]
     for x_device in range(x_devices):
-        first = x_device * y_devices
+        first = x_device * x_rows
         parts = exchange(back[first : first + x_rows], y_rows)
         for turn in range(y_devices):
-            place = (first + turn) * RETURNED
+            place = (turn * x_devices + x_device) * RETURNED
             out_ref[place : place + 8, :] = parts[turn]
     tails = [tail_ref[x * x_devices : (x + 1) * x_devices, :] for x in range(x_rows)]
     tails = exchange(tails, y_rows)
     for turn in range(y_devices):
-        out_ref[pl.ds(turn * RETURNED + 8, x_devices, stride=y_devices * RETURNED), :] = tails[turn]
+        place = turn * x_devices * RETURNED + 8
+        out_ref[pl.ds(place, x_devices, stride=RETURNED), :] = tails[turn]
 
     sums = sums[:, : 2 * units] + sums[:, 2 * units :]
     sums = sums[:16] + sums[16:]
@@ -399,7 +393,7 @@
     for device in range(1, devices):
         place = device * RETURNED + SENT
         sums = sums + in_ref[place : place + 5, :]
-    sums = sums / cells
+    sums = sums * (1.0 / cells)
     in_grad_ref[:5, :] = sums[:, :units]
     in_grad_ref[5:, :] = sums[:1, units:]
     bias_grad_ref[...] = sums[1:2, units:]
@@ -431,7 +425,7 @@
 
 
 def local_kernels(velocity, cotangent, weight_in, bias_in, weight_out):
-    axes = ("gx", "gy")
+    axes = ("gy", "gx")
     x_devices, y_devices = lax.axis_size("gx"), lax.axis_size("gy")
     devices = x_devices * y_devices
     _, x_rows, y_rows, z_length = velocity.shape
@@ -440,17 +434,16 @@
     z_table = derivative_table(z_length)
     y_table = np.kron(np.eye(z_length // devices), derivative_table(y_rows * y_devices))
     single, half = jnp.float32, jnp.bfloat16
-    wide = len(LEFT_PIECES) * LANES
+
+    in_place = pl.BlockSpec(memory_space=pltpu.HBM)
 
     arguments = [
         velocity,
         cotangent,
-        split_table(z_table.T),
+        table(z_table.T),
         weight_in,
         bias_in[None],
         weight_out.T,
-        split_table(y_table.T),
-        split_table(y_table),
     ]
     arguments = [pltpu.with_memory_space_constraint(each, pltpu.HBM) for each in arguments]
     sent, *prepared = on_device(
@@ -459,12 +452,10 @@
             ((devices * SENT, LANES), single),
             ((2 * units, LANES), half),
             ((48, 4 * units), half),
-            ((wide, LANES), half),
-            ((wide, LANES), half),
         ],
-        [pltpu.VMEM(values.shape, values.dtype) for values in arguments[:6]]
+        [pltpu.VMEM(values.shape, values.dtype) for values in arguments]
         + [pltpu.SemaphoreType.DMA((len(arguments),))],
-        in_specs=[pl.BlockSpec(memory_space=pltpu.HBM)] * len(arguments),
+        in_specs=[in_place] * len(arguments),
     )(*arguments)
     sent = sent.reshape(devices, 1, SENT * LANES)
     sent = lax.all_to_all(sent, axes, 0, 0, tiled=True).reshape(devices * SENT, LANES)
@@ -472,7 +463,7 @@
         functools.partial(middle_kernel, x_devices),
         [((devices * RETURNED, LANES), single)],
         [pltpu.VMEM((x_devices * x_rows, LANES), single)],
-    )(sent, *prepared)
+    )(sent, *prepared, split_table(y_table.T), split_table(y_table))
     back = back.reshape(devices, 1, RETURNED * LANES)
     back = lax.all_to_all(back, axes, 0, 0, tiled=True).reshape(devices * RETURNED, LANES)
     shapes = [velocity.shape, velocity.shape, (6, units), (1, units), (3, units)]

time: 33.1 us -> 32.8 us (level)
    all_to_all x1, blocking collectives: 15.5 us -> 14.9 us  [local_kernels(): lax.all_to_all(sent, axes, 0, 0, tiled=True).reshape(devices * SENT, LANES)]
    all_to_all x1, blocking collectives: 11.8 us -> 12.3 us  [local_kernels(): lax.all_to_all(back, axes, 0, 0, tiled=True)]
where the time goes in v5:
time: 32.8 us; the launch traced here: 32.7 us
  blocking collectives  27.3 us (83%)
  Pallas kernels  4.66 us (14%)
  between operations  0.69 us (2%)
    all_to_all x1, blocking collectives, local_kernels(): lax.all_to_all(sent, axes, 0, 0, tiled=True).reshape(devices * SENT, LANES)  14.9 us
    all_to_all x1, blocking collectives, local_kernels(): lax.all_to_all(back, axes, 0, 0, tiled=True)  12.3 us
    pallas_call x1, Pallas kernels, local_kernels(): on_device(functools.partial(middle_kernel, x_devices), [((devices * RETUR...  2.14 us
    pallas_call x1, Pallas kernels, local_kernels(): on_device(pack_kernel, [((devices * SENT, LANES), single), ((2 * units, L...  1.46 us
    pallas_call x1, Pallas kernels, local_kernels(): on_device(functools.partial(unpack_kernel, float(cells)), [(shape, single...  1.06 us

profile of v5, /device:TPU:0, one launch (start us, length us, event | category | flops | bytes accessed | tf_op | source)
XLA Modules:
  0.0 32.7 jit_solution(5807253143893782149)
XLA Ops:
  0.6 0.0 copy-start.3
  0.6 0.0 copy-start.4
  0.7 1.5 %shard_map.128 = (f32[288,128]{1,0:T(8,128)S(1)}, bf16[128,128]{1,0:T(8,128)(2,1)S(1)}, bf16[48,256]{1,0:T(8,128)(2,1)S(1)}) custom-call(f32[3,4,8,128]{3,2,1,0:T(8,128)} %velocity_ref.1, f32[3,4,8,128]{3,2,1,0:T(8,128)} %cotangent_ref.1, f32[128,128]{1,0:T(8,128)} %constant.8.clone.z_hbm, f32[6,64]{1,0:T(8,128)} %weight_in_hbm.1, f32[1,64]{1,0:T(1,128)} %bitcast.13, ...), custom_call_target="tpu_custom_call" | custom-call | tf_op jit(solution)/shard_map/pallas_call | solution.py:449
  2.1 14.9 %all_to_all.10 = f32[32,1,1152]{2,1,0:T(1,128)S(1)} all-to-all(f32[32,1,1152]{2,1,0:T(1,128)S(1)} %bitcast.11), channel_id=1, replica_groups=mesh['gx'=8,'gy'=4] {'gy','gx'}, dimensions={0} | all-to-all | bytes 294912 | tf_op jit(solution)/shard_map/all_to_all | solution.py:461
  17.1 0.0 copy-done.3
  17.1 0.0 copy-done.4
  17.1 2.1 %shard_map.129 = f32[448,128]{1,0:T(8,128)S(1)} custom-call(f32[288,128]{1,0:T(8,128)S(1)} %bitcast.10, bf16[128,128]{1,0:T(8,128)(2,1)S(1)} %get-tuple-element.14.before_ref, bf16[48,256]{1,0:T(8,128)(2,1)S(1)} %get-tuple-element.15.after_ref, bf16[768,128]{1,0:T(8,128)(2,1)S(1)} %copy-done.4, bf16[768,128]{1,0:T(8,128)(2,1)S(1)} %copy-done.3), custom_call_target="tpu_custom_call" | custom-call | tf_op jit(solution)/shard_map/pallas_call | solution.py:462
  19.2 0.0 copy-start
  19.2 0.0 copy-start.1
  19.2 0.0 copy-start.2
  19.3 12.3 %all_to_all.11 = f32[32,1,1792]{2,1,0:T(1,128)S(1)} all-to-all(f32[32,1,1792]{2,1,0:T(1,128)S(1)} %bitcast.9), channel_id=1, replica_groups=mesh['gx'=8,'gy'=4] {'gy','gx'}, dimensions={0} | all-to-all | bytes 458752 | tf_op jit(solution)/shard_map/all_to_all | solution.py:468
  31.6 0.0 copy-done
  31.6 0.0 copy-done.1
  31.6 0.0 copy-done.2
  31.6 1.1 %shard_map.130 = (f32[3,4,8,128]{3,2,1,0:T(8,128)}, f32[3,4,8,128]{3,2,1,0:T(8,128)}, f32[6,64]{1,0:T(8,128)}, f32[1,64]{1,0:T(1,128)}, f32[3,64]{1,0:T(4,128)}) custom-call(f32[448,128]{1,0:T(8,128)S(1)} %bitcast.8, f32[3,4,8,128]{3,2,1,0:T(8,128)S(1)} %copy-done, f32[3,4,8,128]{3,2,1,0:T(8,128)S(1)} %copy-done.1, bf16[768,128]{1,0:T(8,128)(2,1)S(1)} %copy-done.2), custom_call_target="tpu_custom_call" | custom-call | tf_op jit(solution)/shard_map/pallas_call | solution.py:470
Async XLA Ops:
  0.6 16.4 %copy-start.3 = (bf16[768,128]{1,0:T(8,128)(2,1)S(1)}, bf16[768,128]{1,0:T(8,128)(2,1)}, u32[]{:S(2)}) copy-start(bf16[768,128]{1,0:T(8,128)(2,1)} %constant.10.clone.y_back_ref) | copy-start | bytes 589828
  0.6 16.4 %copy-start.4 = (bf16[768,128]{1,0:T(8,128)(2,1)S(1)}, bf16[768,128]{1,0:T(8,128)(2,1)}, u32[]{:S(2)}) copy-start(bf16[768,128]{1,0:T(8,128)(2,1)} %constant.9.clone.y_ref) | copy-start | bytes 589828
  19.2 12.4 %copy-start = (f32[3,4,8,128]{3,2,1,0:T(8,128)S(1)}, f32[3,4,8,128]{3,2,1,0:T(8,128)}, u32[]{:S(2)}) copy-start(f32[3,4,8,128]{3,2,1,0:T(8,128)} %velocity_ref.1) | copy-start | bytes 147460
  19.2 12.4 %copy-start.1 = (f32[3,4,8,128]{3,2,1,0:T(8,128)S(1)}, f32[3,4,8,128]{3,2,1,0:T(8,128)}, u32[]{:S(2)}) copy-start(f32[3,4,8,128]{3,2,1,0:T(8,128)} %cotangent_ref.1) | copy-start | bytes 147460
  19.2 12.3 %copy-start.2 = (bf16[768,128]{1,0:T(8,128)(2,1)S(1)}, bf16[768,128]{1,0:T(8,128)(2,1)}, u32[]{:S(2)}) copy-start(bf16[768,128]{1,0:T(8,128)(2,1)} %constant.11.clone.z_ref) | copy-start | bytes 589828

commit v6 on v5

--- a/solution.py
+++ b/solution.py
@@ -187,31 +187,9 @@
 
 
 def pack_kernel(
-    velocity_hbm,
-    cotangent_hbm,
-    z_hbm,
-    weight_in_hbm,
-    bias_hbm,
-    weight_out_hbm,
-    out_ref,
-    before_ref,
-    after_ref,
-    velocity_ref,
-    cotangent_ref,
-    z_ref,
-    weight_in_ref,
-    bias_ref,
-    weight_out_ref,
-    arrived,
+    velocity_hbm, cotangent_hbm, z_hbm, out_ref, velocity_ref, cotangent_ref, z_ref, arrived
 ):
-    pairs = [
-        (velocity_hbm, velocity_ref),
-        (cotangent_hbm, cotangent_ref),
-        (z_hbm, z_ref),
-        (weight_in_hbm, weight_in_ref),
-        (bias_hbm, bias_ref),
-        (weight_out_hbm, weight_out_ref),
-    ]
+    pairs = [(velocity_hbm, velocity_ref), (cotangent_hbm, cotangent_ref), (z_hbm, z_ref)]
     copies = [
         pltpu.make_async_copy(source, target, arrived.at[turn])
         for turn, (source, target) in enumerate(pairs)
@@ -239,6 +217,8 @@
         for field in range(start, min(start + groups, SENT)):
             out_ref[pl.ds(field, devices, stride=SENT), :] = parts[field - start]
 
+
+def prepare_kernel(weight_in_ref, bias_ref, weight_out_ref, before_ref, after_ref):
     weight_in = weight_in_ref[...]
     weight_out = weight_out_ref[...]
     units = weight_in.shape[1]
@@ -435,28 +415,20 @@
     y_table = np.kron(np.eye(z_length // devices), derivative_table(y_rows * y_devices))
     single, half = jnp.float32, jnp.bfloat16
 
-    in_place = pl.BlockSpec(memory_space=pltpu.HBM)
-
-    arguments = [
-        velocity,
-        cotangent,
-        table(z_table.T),
-        weight_in,
-        bias_in[None],
-        weight_out.T,
-    ]
+    arguments = [velocity, cotangent, table(z_table.T)]
     arguments = [pltpu.with_memory_space_constraint(each, pltpu.HBM) for each in arguments]
-    sent, *prepared = on_device(
+    (sent,) = on_device(
         pack_kernel,
-        [
-            ((devices * SENT, LANES), single),
-            ((2 * units, LANES), half),
-            ((48, 4 * units), half),
-        ],
+        [((devices * SENT, LANES), single)],
         [pltpu.VMEM(values.shape, values.dtype) for values in arguments]
         + [pltpu.SemaphoreType.DMA((len(arguments),))],
-        in_specs=[in_place] * len(arguments),
+        in_specs=[pl.BlockSpec(memory_space=pltpu.HBM)] * len(arguments),
     )(*arguments)
+    prepared = on_device(
+        prepare_kernel,
+        [((2 * units, LANES), half), ((48, 4 * units), half)],
+        cost_estimate=pl.CostEstimate(flops=1 << 22, bytes_accessed=1 << 20, transcendentals=0),
+    )(weight_in, bias_in[None], weight_out.T)
     sent = sent.reshape(devices, 1, SENT * LANES)
     sent = lax.all_to_all(sent, axes, 0, 0, tiled=True).reshape(devices * SENT, LANES)
     (back,) = on_device(

time: 32.8 us -> 33.7 us (1.027)
  blocking collectives: 27.3 us -> 12.3 us
  starting transfers between devices: 0 us -> 7.3 us
  waiting for transfers between devices: 0 us -> 6.97 us
  Pallas kernels: 4.66 us -> 5.4 us
  local copies, waits for them, and re-layouts: 0.03 us -> 0.7 us
    all_to_all x1 -> x0, blocking collectives: 14.9 us -> none  [local_kernels(): lax.all_to_all(sent, axes, 0, 0, tiled=True).reshape(devices * SENT, LANES)]
    all_to_all x0 -> x1, starting transfers between devices: none -> 7.3 us  [local_kernels(): lax.all_to_all(sent, axes, 0, 0, tiled=True).reshape(devices * SENT, LANES)]
    all_to_all x0 -> x1, waiting for transfers between devices: none -> 6.97 us  [local_kernels(): lax.all_to_all(sent, axes, 0, 0, tiled=True).reshape(devices * SENT, LANES)]
    pallas_call x1 -> x2, Pallas kernels: 1.46 us -> 2.2 us  [the longest x1 2.04 us: local_kernels(): on_device(pack_kernel, [((devices * SENT, LANES), single)], [pltpu.VMEM(v...]
    unnamed x10 -> x16, local copies, waits for them, and re-layouts: 0.03 us -> 0.7 us
  transfers between devices with their start and end apart: 0 -> 1, of which waited for: 0 -> 1; matrix products, arithmetic and copies ran while one was open for 0% -> 0% of each run, Pallas kernels for 0% -> 0%
where the time goes in v6:
time: 33.7 us; the launch traced here: 33.4 us
  blocking collectives  12.3 us (36%)
  starting transfers between devices  7.3 us (22%)
  waiting for transfers between devices  6.97 us (21%)
  Pallas kernels  5.4 us (16%)
  between operations  0.74 us (2%)
  local copies, waits for them, and re-layouts  0.7 us (2%)
    all_to_all x1, blocking collectives, local_kernels(): lax.all_to_all(back, axes, 0, 0, tiled=True)  12.3 us
    all_to_all x1, starting transfers between devices, local_kernels(): lax.all_to_all(sent, axes, 0, 0, tiled=True).reshape(devices * SENT, LANES)  7.3 us
    all_to_all x1, waiting for transfers between devices, local_kernels(): lax.all_to_all(sent, axes, 0, 0, tiled=True).reshape(devices * SENT, LANES)  6.97 us
    pallas_call x1, Pallas kernels, local_kernels(): on_device(functools.partial(middle_kernel, x_devices), [((devices * RETUR...  2.14 us
    pallas_call x1, Pallas kernels, local_kernels(): on_device(pack_kernel, [((devices * SENT, LANES), single)], [pltpu.VMEM(v...  2.04 us
    pallas_call x1, Pallas kernels, local_kernels(): on_device(functools.partial(unpack_kernel, float(cells)), [(shape, single...  1.06 us
    unnamed x16, local copies, waits for them, and re-layouts  0.7 us
  transfers between devices with their start and end apart: 1, of which 1 were waited for; matrix products, arithmetic and copies ran while one was open for 0% of the time, Pallas kernels for 0%

profile of v6, /device:TPU:0, one launch (start us, length us, event | category | flops | bytes accessed | tf_op | source)
XLA Modules:
  0.0 33.4 jit_solution(9156131422497795457)
XLA Ops:
  0.6 0.0 copy-start.4
  0.6 2.0 %shard_map.128 = f32[288,128]{1,0:T(8,128)} custom-call(f32[3,4,8,128]{3,2,1,0:T(8,128)} %velocity_ref.1, f32[3,4,8,128]{3,2,1,0:T(8,128)} %cotangent_ref.1, f32[128,128]{1,0:T(8,128)} %constant.8.clone.z_hbm), custom_call_target="tpu_custom_call" | custom-call | tf_op jit(solution)/shard_map/pallas_call | solution.py:420
  2.7 0.0 copy-start.3
  2.7 0.0 copy-start.5
  2.7 7.3 %all-to-all-start = ((f32[32,1,1152]{2,1,0:T(1,128)}), f32[32,1,1152]{2,1,0:T(1,128)S(1)}, u32[]{:S(2)}, u32[]{:S(2)}) async-start(f32[32,1,1152]{2,1,0:T(1,128)} %bitcast), calls=%async_computation | async-start | bytes 294912 | tf_op jit(solution)/shard_map/all_to_all | solution.py:433
  10.0 0.0 copy-start.6
  10.0 0.0 copy-start.7
  10.0 0.0 copy-done.5
  10.0 0.7 %copy-done.6 = f32[64,3]{0,1:T(4,128)S(1)} copy-done((f32[64,3]{0,1:T(4,128)S(1)}, f32[64,3]{0,1:T(4,128)}, u32[]{:S(2)}) %copy-start.6) | copy-done | bytes 792
  10.7 0.0 copy-done.7
  10.7 0.2 shard_map.129
  10.9 7.0 %all-to-all-done = f32[32,1,1152]{2,1,0:T(1,128)S(1)} async-done(((f32[32,1,1152]{2,1,0:T(1,128)}), f32[32,1,1152]{2,1,0:T(1,128)S(1)}, u32[]{:S(2)}, u32[]{:S(2)}) %all-to-all-start) | async-done | bytes 147488 | tf_op jit(solution)/shard_map/all_to_all | solution.py:433
  17.8 0.0 copy-done.4
  17.8 0.0 copy-done.3
  17.8 2.1 %shard_map.130 = f32[448,128]{1,0:T(8,128)S(1)} custom-call(f32[288,128]{1,0:T(8,128)S(1)} %bitcast.10, bf16[128,128]{1,0:T(8,128)(2,1)S(1)} %get-tuple-element.12.before_ref, bf16[48,256]{1,0:T(8,128)(2,1)S(1)} %get-tuple-element.13.after_ref, bf16[768,128]{1,0:T(8,128)(2,1)S(1)} %copy-done.4, bf16[768,128]{1,0:T(8,128)(2,1)S(1)} %copy-done.3), custom_call_target="tpu_custom_call" | custom-call | tf_op jit(solution)/shard_map/pallas_call | solution.py:434
  20.0 0.0 copy-start
  20.0 0.0 copy-start.1
  20.0 0.0 copy-start.2
  20.0 12.3 %all_to_all.10 = f32[32,1,1792]{2,1,0:T(1,128)S(1)} all-to-all(f32[32,1,1792]{2,1,0:T(1,128)S(1)} %bitcast.9), channel_id=1, replica_groups=mesh['gx'=8,'gy'=4] {'gy','gx'}, dimensions={0} | all-to-all | bytes 458752 | tf_op jit(solution)/shard_map/all_to_all | solution.py:440
  32.4 0.0 copy-done
  32.4 0.0 copy-done.1
  32.4 0.0 copy-done.2
  32.4 1.1 %shard_map.131 = (f32[3,4,8,128]{3,2,1,0:T(8,128)}, f32[3,4,8,128]{3,2,1,0:T(8,128)}, f32[6,64]{1,0:T(8,128)}, f32[1,64]{1,0:T(1,128)}, f32[3,64]{1,0:T(4,128)}) custom-call(f32[448,128]{1,0:T(8,128)S(1)} %bitcast.8, f32[3,4,8,128]{3,2,1,0:T(8,128)S(1)} %copy-done, f32[3,4,8,128]{3,2,1,0:T(8,128)S(1)} %copy-done.1, bf16[768,128]{1,0:T(8,128)(2,1)S(1)} %copy-done.2), custom_call_target="tpu_custom_call" | custom-call | tf_op jit(solution)/shard_map/pallas_call | solution.py:442
Async XLA Ops:
  0.6 17.2 %copy-start.4 = (bf16[768,128]{1,0:T(8,128)(2,1)S(1)}, bf16[768,128]{1,0:T(8,128)(2,1)}, u32[]{:S(2)}) copy-start(bf16[768,128]{1,0:T(8,128)(2,1)} %constant.9.clone.y_ref) | copy-start | bytes 589828
  2.7 15.2 %copy-start.3 = (bf16[768,128]{1,0:T(8,128)(2,1)S(1)}, bf16[768,128]{1,0:T(8,128)(2,1)}, u32[]{:S(2)}) copy-start(bf16[768,128]{1,0:T(8,128)(2,1)} %constant.10.clone.y_back_ref) | copy-start | bytes 589828
  2.7 7.3 %copy-start.5 = (f32[6,64]{1,0:T(8,128)S(1)}, f32[6,64]{1,0:T(8,128)}, u32[]{:S(2)}) copy-start(f32[6,64]{1,0:T(8,128)} %weight_in_ref.1) | copy-start | bytes 4612
  2.7 15.1 %all-to-all-start = ((f32[32,1,1152]{2,1,0:T(1,128)}), f32[32,1,1152]{2,1,0:T(1,128)S(1)}, u32[]{:S(2)}, u32[]{:S(2)}) async-start(f32[32,1,1152]{2,1,0:T(1,128)} %bitcast), calls=%async_computation | async-start | bytes 294912 | tf_op jit(solution)/shard_map/all_to_all | solution.py:433
  10.0 0.7 %copy-start.6 = (f32[64,3]{0,1:T(4,128)S(1)}, f32[64,3]{0,1:T(4,128)}, u32[]{:S(2)}) copy-start(f32[64,3]{0,1:T(4,128)} %param.13) | copy-start | bytes 2308
  10.0 0.7 %copy-start.7 = (f32[64]{0:T(128)S(1)}, f32[64]{0:T(128)}, u32[]{:S(2)}) copy-start(f32[64]{0:T(128)} %param.12) | copy-start | bytes 772
  20.0 12.4 %copy-start = (f32[3,4,8,128]{3,2,1,0:T(8,128)S(1)}, f32[3,4,8,128]{3,2,1,0:T(8,128)}, u32[]{:S(2)}) copy-start(f32[3,4,8,128]{3,2,1,0:T(8,128)} %velocity_ref.1) | copy-start | bytes 147460
  20.0 12.4 %copy-start.1 = (f32[3,4,8,128]{3,2,1,0:T(8,128)S(1)}, f32[3,4,8,128]{3,2,1,0:T(8,128)}, u32[]{:S(2)}) copy-start(f32[3,4,8,128]{3,2,1,0:T(8,128)} %cotangent_ref.1) | copy-start | bytes 147460
  20.0 12.3 %copy-start.2 = (bf16[768,128]{1,0:T(8,128)(2,1)S(1)}, bf16[768,128]{1,0:T(8,128)(2,1)}, u32[]{:S(2)}) copy-start(bf16[768,128]{1,0:T(8,128)(2,1)} %constant.11.clone.z_ref) | copy-start | bytes 589828

commit v7 on v5

--- a/solution.py
+++ b/solution.py
@@ -126,7 +126,7 @@
     return parts
 
 
-def solve_rows(rows):
+def smooth_rows(rows):
     length = len(rows)
     half = length // 2
     scales = []
@@ -134,32 +134,30 @@
     for _ in range(half):
         scales.append(1.0 / (1.0 - FILTER_ALPHA * FILTER_ALPHA * before))
         before = scales[-1]
-    solved = [None] * length
-    for sign in (1, -1):
-        order = range(half) if sign == 1 else range(length - 1, length - 1 - half, -1)
-        last = None
-        for turn, row in enumerate(order):
-            value = rows[row] * scales[turn]
-            if last is not None:
-                value = value - last * (FILTER_ALPHA * scales[turn])
-            solved[row] = last = value
-    below, above = solved[half - 1], solved[half]
-    ratio = FILTER_ALPHA * scales[half - 1]
-    middle = 1.0 / (1.0 - ratio * ratio)
-    solved[half - 1] = (below - ratio * above) * middle
-    solved[half] = (above - ratio * below) * middle
-    for turn in reversed(range(half - 1)):
-        factor = FILTER_ALPHA * scales[turn]
-        solved[turn] = solved[turn] - factor * solved[turn + 1]
-        row = length - 1 - turn
-        solved[row] = solved[row] - factor * solved[row - 1]
-    return solved
-
-
-def smooth_rows(rows):
+    factors = [-FILTER_ALPHA * scale for scale in scales]
+    forward = np.cumprod([1.0] + factors[1:])
+    backward = np.cumprod([1.0] + factors[-2::-1])[::-1]
     own = 0.5 * FILTER_GAIN / FILTER_ALPHA
-    solved = solve_rows(rows)
-    return [own * row + (FILTER_GAIN - own) * value for row, value in zip(rows, solved)]
+
+    sides = [list(range(half)), list(range(length - 1, half - 1, -1))]
+    running = []
+    for side in sides:
+        sums = []
+        for turn, row in enumerate(side):
+            value = rows[row] * float(scales[turn] / forward[turn])
+            sums.append(value if turn == 0 else sums[-1] + value)
+        running.append(sums)
+    middle = forward[-1] / (1.0 - factors[-1] * factors[-1])
+    cross = middle * factors[-1]
+    smoothed = [None] * length
+    for side, sums, others in zip(sides, running, running[::-1]):
+        value = float(middle) * sums[-1] + float(cross) * others[-1]
+        for turn in reversed(range(half)):
+            if turn < half - 1:
+                value = value + float(forward[turn] / backward[turn]) * sums[turn]
+            row = side[turn]
+            smoothed[row] = own * rows[row] + float((FILTER_GAIN - own) * backward[turn]) * value
+    return smoothed
 
 
 def times(left, right, contract=(1, 0)):
@@ -205,12 +203,12 @@
     arrived,
 ):
     pairs = [
+        (weight_in_hbm, weight_in_ref),
+        (bias_hbm, bias_ref),
+        (weight_out_hbm, weight_out_ref),
         (velocity_hbm, velocity_ref),
         (cotangent_hbm, cotangent_ref),
         (z_hbm, z_ref),
-        (weight_in_hbm, weight_in_ref),
-        (bias_hbm, bias_ref),
-        (weight_out_hbm, weight_out_ref),
     ]
     copies = [
         pltpu.make_async_copy(source, target, arrived.at[turn])
@@ -218,27 +216,9 @@
     ]
     for copy in copies:
         copy.start()
-    for copy in copies:
+
+    for copy in copies[:3]:
         copy.wait()
-
-    _, x_rows, y_rows, z_length = velocity_ref.shape
-    block = x_rows * y_rows
-    groups = LANES // block
-    devices = z_length // groups
-    velocity = velocity_ref[...].reshape(3 * block, z_length)
-    cotangent = cotangent_ref[...].reshape(3 * block, z_length)
-    along_z = times_table(velocity, widened(z_ref[...]))
-    fill = jnp.zeros(((-SENT % groups) * block, z_length), jnp.float32)
-    rows = jnp.concatenate(
-        [velocity, along_z, cotangent[block:], cotangent[:block], fill], axis=0
-    )
-    for start in range(0, SENT, groups):
-        turned = rows[start * block : (start + groups) * block].T
-        parts = [turned[group * devices : (group + 1) * devices] for group in range(groups)]
-        parts = exchange(parts, block)
-        for field in range(start, min(start + groups, SENT)):
-            out_ref[pl.ds(field, devices, stride=SENT), :] = parts[field - start]
-
     weight_in = weight_in_ref[...]
     weight_out = weight_out_ref[...]
     units = weight_in.shape[1]
@@ -269,6 +249,26 @@
         ],
         axis=0,
     )
+
+    for copy in copies[3:]:
+        copy.wait()
+    _, x_rows, y_rows, z_length = velocity_ref.shape
+    block = x_rows * y_rows
+    groups = LANES // block
+    devices = z_length // groups
+    velocity = velocity_ref[...].reshape(3 * block, z_length)
+    cotangent = cotangent_ref[...].reshape(3 * block, z_length)
+    along_z = times_table(velocity, widened(z_ref[...]))
+    fill = jnp.zeros(((-SENT % groups) * block, z_length), jnp.float32)
+    rows = jnp.concatenate(
+        [velocity, along_z, cotangent[block:], cotangent[:block], fill], axis=0
+    )
+    for start in range(0, SENT, groups):
+        turned = rows[start * block : (start + groups) * block].T
+        parts = [turned[group * devices : (group + 1) * devices] for group in range(groups)]
+        parts = exchange(parts, block)
+        for field in range(start, min(start + groups, SENT)):
+            out_ref[pl.ds(field, devices, stride=SENT), :] = parts[field - start]
 
 
 def middle_kernel(x_devices, in_ref, before_ref, after_ref, y_ref, y_back_ref, out_ref, tail_ref):
@@ -363,17 +363,35 @@
     velocity_ref,
     cotangent_ref,
     z_ref,
+    new_hbm,
+    grad_hbm,
+    in_grad_hbm,
+    bias_grad_hbm,
+    out_grad_hbm,
     new_ref,
     grad_ref,
     in_grad_ref,
     bias_grad_ref,
     out_grad_ref,
+    arrived,
 ):
+    pairs = [
+        (new_ref, new_hbm),
+        (grad_ref, grad_hbm),
+        (in_grad_ref, in_grad_hbm),
+        (bias_grad_ref, bias_grad_hbm),
+        (out_grad_ref, out_grad_hbm),
+    ]
+    copies = [
+        pltpu.make_async_copy(source, target, arrived.at[turn])
+        for turn, (source, target) in enumerate(pairs)
+    ]
     _, x_rows, y_rows, z_length = velocity_ref.shape
     block = x_rows * y_rows
     groups = LANES // block
     devices = z_length // groups
     units = in_grad_ref.shape[1]
+
     fields = []
     for start in range(0, SENT, groups):
         parts = [
@@ -384,20 +402,27 @@
         fields.extend(turned[turn * block : (turn + 1) * block] for turn in range(groups))
     shape = (3, x_rows, y_rows, z_length)
     forcing = jnp.concatenate(fields[6:9], axis=0).reshape(shape)
+    back_z = times_table(jnp.concatenate(fields[3:6], axis=0), z_ref[...])
     new_ref[...] = velocity_ref[...] + STEP_SIZE * forcing
-    back_z = times_table(jnp.concatenate(fields[3:6], axis=0), z_ref[...])
+    copies[0].start()
     back = jnp.concatenate(fields[:3], axis=0) + back_z
     grad_ref[...] = cotangent_ref[...] + back.reshape(shape)
-
-    sums = in_ref[SENT : SENT + 5, :]
-    for device in range(1, devices):
-        place = device * RETURNED + SENT
-        sums = sums + in_ref[place : place + 5, :]
-    sums = sums * (1.0 / cells)
+    copies[1].start()
+    sums = [
+        in_ref[device * RETURNED + SENT : device * RETURNED + SENT + 5, :]
+        for device in range(devices)
+    ]
+    while len(sums) > 1:
+        sums = [one + other for one, other in zip(sums[::2], sums[1::2])]
+    sums = sums[0] * (1.0 / cells)
     in_grad_ref[:5, :] = sums[:, :units]
     in_grad_ref[5:, :] = sums[:1, units:]
     bias_grad_ref[...] = sums[1:2, units:]
     out_grad_ref[...] = sums[2:, units:]
+    for copy in copies[2:]:
+        copy.start()
+    for copy in copies:
+        copy.wait()
 
 
 def on_device(kernel, shapes, scratch=(), **more):
@@ -468,7 +493,11 @@
     back = lax.all_to_all(back, axes, 0, 0, tiled=True).reshape(devices * RETURNED, LANES)
     shapes = [velocity.shape, velocity.shape, (6, units), (1, units), (3, units)]
     new, grad, grad_in, grad_bias, grad_out = on_device(
-        functools.partial(unpack_kernel, float(cells)), [(shape, single) for shape in shapes]
+        functools.partial(unpack_kernel, float(cells)),
+        [(shape, single) for shape in shapes],
+        [pltpu.VMEM(shape, single) for shape in shapes]
+        + [pltpu.SemaphoreType.DMA((len(shapes),))],
+        out_specs=[in_place] * len(shapes),
     )(back, velocity, cotangent, split_table(z_table))
     return (new, grad, grad_in, grad_bias[0], grad_out.T)
 

time: 32.8 us -> 32.9 us (level)
  no operation moved by 1% of the time
where the time goes in v7:
time: 32.9 us; the launch traced here: 32.7 us
  blocking collectives  27.3 us (83%)
  Pallas kernels  4.7 us (14%)
  between operations  0.69 us (2%)
    all_to_all x1, blocking collectives, local_kernels(): lax.all_to_all(sent, axes, 0, 0, tiled=True).reshape(devices * SENT, LANES)  14.9 us
    all_to_all x1, blocking collectives, local_kernels(): lax.all_to_all(back, axes, 0, 0, tiled=True)  12.3 us
    pallas_call x1, Pallas kernels, local_kernels(): on_device(functools.partial(middle_kernel, x_devices), [((devices * RETUR...  2.11 us
    pallas_call x1, Pallas kernels, local_kernels(): on_device(pack_kernel, [((devices * SENT, LANES), single), ((2 * units, L...  1.47 us
    pallas_call x1, Pallas kernels, local_kernels(): on_device(functools.partial(unpack_kernel, float(cells)), [(shape, single...  1.12 us

profile of v7, /device:TPU:0, one launch (start us, length us, event | category | flops | bytes accessed | tf_op | source)
XLA Modules:
  0.0 32.7 jit_solution(13329461987952375328)
XLA Ops:
  0.6 0.0 copy-start.3
  0.6 0.0 copy-start.4
  0.7 1.5 %shard_map.128 = (f32[288,128]{1,0:T(8,128)S(1)}, bf16[128,128]{1,0:T(8,128)(2,1)S(1)}, bf16[48,256]{1,0:T(8,128)(2,1)S(1)}) custom-call(f32[3,4,8,128]{3,2,1,0:T(8,128)} %velocity_ref.1, f32[3,4,8,128]{3,2,1,0:T(8,128)} %cotangent_ref.1, f32[128,128]{1,0:T(8,128)} %constant.8.clone.z_hbm, f32[6,64]{1,0:T(8,128)} %weight_in_hbm.1, f32[1,64]{1,0:T(1,128)} %bitcast.13, ...), custom_call_target="tpu_custom_call" | custom-call | tf_op jit(solution)/shard_map/pallas_call | solution.py:474
  2.1 14.9 %all_to_all.10 = f32[32,1,1152]{2,1,0:T(1,128)S(1)} all-to-all(f32[32,1,1152]{2,1,0:T(1,128)S(1)} %bitcast.11), channel_id=1, replica_groups=mesh['gx'=8,'gy'=4] {'gy','gx'}, dimensions={0} | all-to-all | bytes 294912 | tf_op jit(solution)/shard_map/all_to_all | solution.py:486
  17.1 0.0 copy-done.3
  17.1 0.0 copy-done.4
  17.1 2.1 %shard_map.129 = f32[448,128]{1,0:T(8,128)S(1)} custom-call(f32[288,128]{1,0:T(8,128)S(1)} %bitcast.10, bf16[128,128]{1,0:T(8,128)(2,1)S(1)} %get-tuple-element.14.before_ref, bf16[48,256]{1,0:T(8,128)(2,1)S(1)} %get-tuple-element.15.after_ref, bf16[768,128]{1,0:T(8,128)(2,1)S(1)} %copy-done.4, bf16[768,128]{1,0:T(8,128)(2,1)S(1)} %copy-done.3), custom_call_target="tpu_custom_call" | custom-call | tf_op jit(solution)/shard_map/pallas_call | solution.py:487
  19.2 0.0 copy-start
  19.2 0.0 copy-start.1
  19.2 0.0 copy-start.2
  19.2 12.3 %all_to_all.11 = f32[32,1,1792]{2,1,0:T(1,128)S(1)} all-to-all(f32[32,1,1792]{2,1,0:T(1,128)S(1)} %bitcast.9), channel_id=1, replica_groups=mesh['gx'=8,'gy'=4] {'gy','gx'}, dimensions={0} | all-to-all | bytes 458752 | tf_op jit(solution)/shard_map/all_to_all | solution.py:493
  31.6 0.0 copy-done
  31.6 0.0 copy-done.1
  31.6 0.0 copy-done.2
  31.6 1.1 %shard_map.130 = (f32[3,4,8,128]{3,2,1,0:T(8,128)}, f32[3,4,8,128]{3,2,1,0:T(8,128)}, f32[6,64]{1,0:T(8,128)}, f32[1,64]{1,0:T(1,128)}, f32[3,64]{1,0:T(4,128)}) custom-call(f32[448,128]{1,0:T(8,128)S(1)} %bitcast.8, f32[3,4,8,128]{3,2,1,0:T(8,128)S(1)} %copy-done, f32[3,4,8,128]{3,2,1,0:T(8,128)S(1)} %copy-done.1, bf16[768,128]{1,0:T(8,128)(2,1)S(1)} %copy-done.2), custom_call_target="tpu_custom_call" | custom-call | tf_op jit(solution)/shard_map/pallas_call | solution.py:495
Async XLA Ops:
  0.6 16.4 %copy-start.3 = (bf16[768,128]{1,0:T(8,128)(2,1)S(1)}, bf16[768,128]{1,0:T(8,128)(2,1)}, u32[]{:S(2)}) copy-start(bf16[768,128]{1,0:T(8,128)(2,1)} %constant.10.clone.y_back_ref) | copy-start | bytes 589828
  0.6 16.4 %copy-start.4 = (bf16[768,128]{1,0:T(8,128)(2,1)S(1)}, bf16[768,128]{1,0:T(8,128)(2,1)}, u32[]{:S(2)}) copy-start(bf16[768,128]{1,0:T(8,128)(2,1)} %constant.9.clone.y_ref) | copy-start | bytes 589828
  19.2 12.4 %copy-start = (f32[3,4,8,128]{3,2,1,0:T(8,128)S(1)}, f32[3,4,8,128]{3,2,1,0:T(8,128)}, u32[]{:S(2)}) copy-start(f32[3,4,8,128]{3,2,1,0:T(8,128)} %velocity_ref.1) | copy-start | bytes 147460
  19.2 12.4 %copy-start.1 = (f32[3,4,8,128]{3,2,1,0:T(8,128)S(1)}, f32[3,4,8,128]{3,2,1,0:T(8,128)}, u32[]{:S(2)}) copy-start(f32[3,4,8,128]{3,2,1,0:T(8,128)} %cotangent_ref.1) | copy-start | bytes 147460
  19.2 12.3 %copy-start.2 = (bf16[768,128]{1,0:T(8,128)(2,1)S(1)}, bf16[768,128]{1,0:T(8,128)(2,1)}, u32[]{:S(2)}) copy-start(bf16[768,128]{1,0:T(8,128)(2,1)} %constant.11.clone.z_ref) | copy-start | bytes 589828

commit v8 on v7

--- a/solution.py
+++ b/solution.py
@@ -271,7 +271,18 @@
             out_ref[pl.ds(field, devices, stride=SENT), :] = parts[field - start]
 
 
-def middle_kernel(x_devices, in_ref, before_ref, after_ref, y_ref, y_back_ref, out_ref, tail_ref):
+def middle_kernel(
+    x_devices,
+    in_ref,
+    before_ref,
+    after_ref,
+    y_ref,
+    y_back_ref,
+    out_ref,
+    cells_ref,
+    result_ref,
+    tail_ref,
+):
     y_devices = in_ref.shape[0] // SENT // x_devices
     x_rows = y_devices
     x_length = x_devices * x_rows
@@ -292,44 +303,38 @@
 
     smoothed = smooth_rows(planes)
     along_y = times_table(jnp.concatenate(smoothed, axis=0), y_ref[...])
-    upper_rows = []
-    lower_rows = []
     for x in range(x_length):
         features = jnp.where(row8 < 3, along_y[8 * x : 8 * x + 8], smoothed[x])
         features = jnp.where(row8 < 6, features, jnp.where(row8 == 6, 1.0, 0.0))
         last = tails[x % x_rows][x // x_rows : x // x_rows + 1]
-        upper_rows.append(features)
-        lower_rows.append(jnp.where(row8 == 5, last, planes[x]))
-
-    before = before_ref[...]
-    after = after_ref[...]
-    at_once = 8
-    sums = jnp.zeros((32, 4 * units), jnp.float32)
-    results = []
-    for start in range(0, x_length, at_once):
-        stop = start + at_once
-        cells = jnp.concatenate(
-            [
-                jnp.concatenate(upper_rows[start:stop], axis=1),
-                jnp.concatenate(lower_rows[start:stop], axis=1),
-            ],
-            axis=0,
-        )
-        pieces = split(cells, 3)
-        both = times(before, jnp.concatenate([pieces[turn] for turn in LEFT_PIECES + (2, 1)], axis=0))
+        cells_ref[:8, x * LANES : (x + 1) * LANES] = features
+        cells_ref[8:, x * LANES : (x + 1) * LANES] = jnp.where(row8 == 5, last, planes[x])
+
+    at_once = 2 * x_rows
+
+    def network(chunk, sums):
+        start = pl.multiple_of(chunk * at_once * LANES, LANES)
+        pieces = split(cells_ref[:, pl.ds(start, at_once * LANES)], 3)
+        wide = jnp.concatenate([pieces[turn] for turn in LEFT_PIECES + (2, 1)], axis=0)
+        both = times(before_ref[...], wide)
         hidden = jnp.tanh(both[:units])
         grad_pre = both[units:] * (1.0 - hidden * hidden)
         both = jnp.concatenate([hidden, grad_pre], axis=0)
         both = jnp.concatenate(split(both, 2), axis=0)
         sums = sums + times(jnp.concatenate(pieces[:2], axis=0), both, (1, 1))
-        result = times(after, both)
+        result = times(after_ref[...], both)
         result = result[:16] + result[16:32] + result[32:]
         for turn in range(at_once):
-            results.append(result[:8, turn * LANES : (turn + 1) * LANES])
-            x = start + turn
-            place = (x % x_rows) * x_devices + x // x_rows
-            tail_ref[place : place + 1, :] = result[8:9, turn * LANES : (turn + 1) * LANES]
-
+            part = result[:9, turn * LANES : (turn + 1) * LANES]
+            row = pl.multiple_of((chunk * at_once + turn) * 8, 8)
+            result_ref[pl.ds(row, 8), :] = part[:8]
+            place = (turn % x_rows) * x_devices + chunk * 2 + turn // x_rows
+            tail_ref[pl.ds(place, 1), :] = part[8:]
+        return sums
+
+    sums = jnp.zeros((32, 4 * units), jnp.float32)
+    sums = lax.fori_loop(0, x_length // at_once, network, sums)
+    results = [result_ref[8 * x : 8 * x + 8, :] for x in range(x_length)]
     back_y = times_table(jnp.concatenate(results, axis=0), y_back_ref[...])
     back = [
         jnp.where(row8 < 3, back_y[8 * x : 8 * x + 8], results[x]) for x in range(x_length)
@@ -363,35 +368,17 @@
     velocity_ref,
     cotangent_ref,
     z_ref,
-    new_hbm,
-    grad_hbm,
-    in_grad_hbm,
-    bias_grad_hbm,
-    out_grad_hbm,
     new_ref,
     grad_ref,
     in_grad_ref,
     bias_grad_ref,
     out_grad_ref,
-    arrived,
 ):
-    pairs = [
-        (new_ref, new_hbm),
-        (grad_ref, grad_hbm),
-        (in_grad_ref, in_grad_hbm),
-        (bias_grad_ref, bias_grad_hbm),
-        (out_grad_ref, out_grad_hbm),
-    ]
-    copies = [
-        pltpu.make_async_copy(source, target, arrived.at[turn])
-        for turn, (source, target) in enumerate(pairs)
-    ]
     _, x_rows, y_rows, z_length = velocity_ref.shape
     block = x_rows * y_rows
     groups = LANES // block
     devices = z_length // groups
     units = in_grad_ref.shape[1]
-
     fields = []
     for start in range(0, SENT, groups):
         parts = [
@@ -402,27 +389,20 @@
         fields.extend(turned[turn * block : (turn + 1) * block] for turn in range(groups))
     shape = (3, x_rows, y_rows, z_length)
     forcing = jnp.concatenate(fields[6:9], axis=0).reshape(shape)
+    new_ref[...] = velocity_ref[...] + STEP_SIZE * forcing
     back_z = times_table(jnp.concatenate(fields[3:6], axis=0), z_ref[...])
-    new_ref[...] = velocity_ref[...] + STEP_SIZE * forcing
-    copies[0].start()
     back = jnp.concatenate(fields[:3], axis=0) + back_z
     grad_ref[...] = cotangent_ref[...] + back.reshape(shape)
-    copies[1].start()
-    sums = [
-        in_ref[device * RETURNED + SENT : device * RETURNED + SENT + 5, :]
-        for device in range(devices)
-    ]
-    while len(sums) > 1:
-        sums = [one + other for one, other in zip(sums[::2], sums[1::2])]
-    sums = sums[0] * (1.0 / cells)
+
+    sums = in_ref[SENT : SENT + 5, :]
+    for device in range(1, devices):
+        place = device * RETURNED + SENT
+        sums = sums + in_ref[place : place + 5, :]
+    sums = sums * (1.0 / cells)
     in_grad_ref[:5, :] = sums[:, :units]
     in_grad_ref[5:, :] = sums[:1, units:]
     bias_grad_ref[...] = sums[1:2, units:]
     out_grad_ref[...] = sums[2:, units:]
-    for copy in copies[2:]:
-        copy.start()
-    for copy in copies:
-        copy.wait()
 
 
 def on_device(kernel, shapes, scratch=(), **more):
@@ -487,17 +467,17 @@
     (back,) = on_device(
         functools.partial(middle_kernel, x_devices),
         [((devices * RETURNED, LANES), single)],
-        [pltpu.VMEM((x_devices * x_rows, LANES), single)],
+        [
+            pltpu.VMEM((16, x_devices * x_rows * LANES), single),
+            pltpu.VMEM((8 * x_devices * x_rows, LANES), single),
+            pltpu.VMEM((x_devices * x_rows, LANES), single),
+        ],
     )(sent, *prepared, split_table(y_table.T), split_table(y_table))
     back = back.reshape(devices, 1, RETURNED * LANES)
     back = lax.all_to_all(back, axes, 0, 0, tiled=True).reshape(devices * RETURNED, LANES)
     shapes = [velocity.shape, velocity.shape, (6, units), (1, units), (3, units)]
     new, grad, grad_in, grad_bias, grad_out = on_device(
-        functools.partial(unpack_kernel, float(cells)),
-        [(shape, single) for shape in shapes],
-        [pltpu.VMEM(shape, single) for shape in shapes]
-        + [pltpu.SemaphoreType.DMA((len(shapes),))],
-        out_specs=[in_place] * len(shapes),
+        functools.partial(unpack_kernel, float(cells)), [(shape, single) for shape in shapes]
     )(back, velocity, cotangent, split_table(z_table))
     return (new, grad, grad_in, grad_bias[0], grad_out.T)
 

time: 32.9 us -> 33.6 us (1.021)
  Pallas kernels: 4.7 us -> 5.44 us
    pallas_call x1, Pallas kernels: 2.11 us -> 2.92 us  [local_kernels(): on_device(functools.partial(middle_kernel, x_devices), [((devices * RETUR...]
where the time goes in v8:
time: 33.6 us; the launch traced here: 33.4 us
  blocking collectives  27.3 us (81%)
  Pallas kernels  5.44 us (16%)
  between operations  0.69 us (2%)
    all_to_all x1, blocking collectives, local_kernels(): lax.all_to_all(sent, axes, 0, 0, tiled=True).reshape(devices * SENT, LANES)  14.9 us
    all_to_all x1, blocking collectives, local_kernels(): lax.all_to_all(back, axes, 0, 0, tiled=True)  12.3 us
    pallas_call x1, Pallas kernels, local_kernels(): on_device(functools.partial(middle_kernel, x_devices), [((devices * RETUR...  2.92 us
    pallas_call x1, Pallas kernels, local_kernels(): on_device(pack_kernel, [((devices * SENT, LANES), single), ((2 * units, L...  1.47 us
    pallas_call x1, Pallas kernels, local_kernels(): on_device(functools.partial(unpack_kernel, float(cells)), [(shape, single...  1.06 us

profile of v8, /device:TPU:0, one launch (start us, length us, event | category | flops | bytes accessed | tf_op | source)
XLA Modules:
  0.0 33.4 jit_solution(7928556795227737566)
XLA Ops:
  0.6 0.0 copy-start.3
  0.6 0.0 copy-start.4
  0.7 1.5 %shard_map.128 = (f32[288,128]{1,0:T(8,128)S(1)}, bf16[128,128]{1,0:T(8,128)(2,1)S(1)}, bf16[48,256]{1,0:T(8,128)(2,1)S(1)}) custom-call(f32[3,4,8,128]{3,2,1,0:T(8,128)} %velocity_ref.1, f32[3,4,8,128]{3,2,1,0:T(8,128)} %cotangent_ref.1, f32[128,128]{1,0:T(8,128)} %constant.8.clone.z_hbm, f32[6,64]{1,0:T(8,128)} %weight_in_hbm.1, f32[1,64]{1,0:T(1,128)} %bitcast.13, ...), custom_call_target="tpu_custom_call" | custom-call | tf_op jit(solution)/shard_map/pallas_call | solution.py:454
  2.1 14.9 %all_to_all.10 = f32[32,1,1152]{2,1,0:T(1,128)S(1)} all-to-all(f32[32,1,1152]{2,1,0:T(1,128)S(1)} %bitcast.11), channel_id=1, replica_groups=mesh['gx'=8,'gy'=4] {'gy','gx'}, dimensions={0} | all-to-all | bytes 294912 | tf_op jit(solution)/shard_map/all_to_all | solution.py:466
  17.1 0.0 copy-done.3
  17.1 0.0 copy-done.4
  17.1 2.9 %shard_map.129 = f32[448,128]{1,0:T(8,128)S(1)} custom-call(f32[288,128]{1,0:T(8,128)S(1)} %bitcast.10, bf16[128,128]{1,0:T(8,128)(2,1)S(1)} %get-tuple-element.14.before_ref, bf16[48,256]{1,0:T(8,128)(2,1)S(1)} %get-tuple-element.15.after_ref, bf16[768,128]{1,0:T(8,128)(2,1)S(1)} %copy-done.4, bf16[768,128]{1,0:T(8,128)(2,1)S(1)} %copy-done.3), custom_call_target="tpu_custom_call" | custom-call | tf_op jit(solution)/shard_map/pallas_call | solution.py:467
  20.0 0.0 copy-start
  20.0 0.0 copy-start.1
  20.0 0.0 copy-start.2
  20.0 12.3 %all_to_all.11 = f32[32,1,1792]{2,1,0:T(1,128)S(1)} all-to-all(f32[32,1,1792]{2,1,0:T(1,128)S(1)} %bitcast.9), channel_id=1, replica_groups=mesh['gx'=8,'gy'=4] {'gy','gx'}, dimensions={0} | all-to-all | bytes 458752 | tf_op jit(solution)/shard_map/all_to_all | solution.py:477
  32.4 0.0 copy-done
  32.4 0.0 copy-done.1
  32.4 0.0 copy-done.2
  32.4 1.1 %shard_map.130 = (f32[3,4,8,128]{3,2,1,0:T(8,128)}, f32[3,4,8,128]{3,2,1,0:T(8,128)}, f32[6,64]{1,0:T(8,128)}, f32[1,64]{1,0:T(1,128)}, f32[3,64]{1,0:T(4,128)}) custom-call(f32[448,128]{1,0:T(8,128)S(1)} %bitcast.8, f32[3,4,8,128]{3,2,1,0:T(8,128)S(1)} %copy-done, f32[3,4,8,128]{3,2,1,0:T(8,128)S(1)} %copy-done.1, bf16[768,128]{1,0:T(8,128)(2,1)S(1)} %copy-done.2), custom_call_target="tpu_custom_call" | custom-call | tf_op jit(solution)/shard_map/pallas_call | solution.py:479
Async XLA Ops:
  0.6 16.4 %copy-start.3 = (bf16[768,128]{1,0:T(8,128)(2,1)S(1)}, bf16[768,128]{1,0:T(8,128)(2,1)}, u32[]{:S(2)}) copy-start(bf16[768,128]{1,0:T(8,128)(2,1)} %constant.10.clone.y_back_ref) | copy-start | bytes 589828
  0.6 16.4 %copy-start.4 = (bf16[768,128]{1,0:T(8,128)(2,1)S(1)}, bf16[768,128]{1,0:T(8,128)(2,1)}, u32[]{:S(2)}) copy-start(bf16[768,128]{1,0:T(8,128)(2,1)} %constant.9.clone.y_ref) | copy-start | bytes 589828
  20.0 12.4 %copy-start = (f32[3,4,8,128]{3,2,1,0:T(8,128)S(1)}, f32[3,4,8,128]{3,2,1,0:T(8,128)}, u32[]{:S(2)}) copy-start(f32[3,4,8,128]{3,2,1,0:T(8,128)} %velocity_ref.1) | copy-start | bytes 147460
  20.0 12.4 %copy-start.1 = (f32[3,4,8,128]{3,2,1,0:T(8,128)S(1)}, f32[3,4,8,128]{3,2,1,0:T(8,128)}, u32[]{:S(2)}) copy-start(f32[3,4,8,128]{3,2,1,0:T(8,128)} %cotangent_ref.1) | copy-start | bytes 147460
  20.0 12.4 %copy-start.2 = (bf16[768,128]{1,0:T(8,128)(2,1)S(1)}, bf16[768,128]{1,0:T(8,128)(2,1)}, u32[]{:S(2)}) copy-start(bf16[768,128]{1,0:T(8,128)(2,1)} %constant.11.clone.z_ref) | copy-start | bytes 589828

commit v9 on v7

--- a/solution.py
+++ b/solution.py
@@ -182,6 +182,15 @@
 def widened(square_table):
     pieces = split(square_table, 3)
     return jnp.concatenate([pieces[turn] for turn in RIGHT_PIECES], axis=0)
+
+
+def by_parts(rows, wide_table):
+    half = len(rows) // 2
+    outs = []
+    for start in (0, half):
+        out = times_table(jnp.concatenate(rows[start : start + half], axis=0), wide_table)
+        outs.extend(out[8 * turn : 8 * turn + 8] for turn in range(half))
+    return outs
 
 
 def pack_kernel(
@@ -291,11 +300,11 @@
     tails = exchange(tails, y_rows)
 
     smoothed = smooth_rows(planes)
-    along_y = times_table(jnp.concatenate(smoothed, axis=0), y_ref[...])
+    along_y = by_parts(smoothed, y_ref[...])
     upper_rows = []
     lower_rows = []
     for x in range(x_length):
-        features = jnp.where(row8 < 3, along_y[8 * x : 8 * x + 8], smoothed[x])
+        features = jnp.where(row8 < 3, along_y[x], smoothed[x])
         features = jnp.where(row8 < 6, features, jnp.where(row8 == 6, 1.0, 0.0))
         last = tails[x % x_rows][x // x_rows : x // x_rows + 1]
         upper_rows.append(features)
@@ -330,10 +339,8 @@
             place = (x % x_rows) * x_devices + x // x_rows
             tail_ref[place : place + 1, :] = result[8:9, turn * LANES : (turn + 1) * LANES]
 
-    back_y = times_table(jnp.concatenate(results, axis=0), y_back_ref[...])
-    back = [
-        jnp.where(row8 < 3, back_y[8 * x : 8 * x + 8], results[x]) for x in range(x_length)
-    ]
+    back_y = by_parts(results, y_back_ref[...])
+    back = [jnp.where(row8 < 3, back_y[x], results[x]) for x in range(x_length)]
     back = smooth_rows(back)
     back = [jnp.where(row8 < 6, value, result) for value, result in zip(back, results)]
     for x_device in range(x_devices):
@@ -363,35 +370,17 @@
     velocity_ref,
     cotangent_ref,
     z_ref,
-    new_hbm,
-    grad_hbm,
-    in_grad_hbm,
-    bias_grad_hbm,
-    out_grad_hbm,
     new_ref,
     grad_ref,
     in_grad_ref,
     bias_grad_ref,
     out_grad_ref,
-    arrived,
 ):
-    pairs = [
-        (new_ref, new_hbm),
-        (grad_ref, grad_hbm),
-        (in_grad_ref, in_grad_hbm),
-        (bias_grad_ref, bias_grad_hbm),
-        (out_grad_ref, out_grad_hbm),
-    ]
-    copies = [
-        pltpu.make_async_copy(source, target, arrived.at[turn])
-        for turn, (source, target) in enumerate(pairs)
-    ]
     _, x_rows, y_rows, z_length = velocity_ref.shape
     block = x_rows * y_rows
     groups = LANES // block
     devices = z_length // groups
     units = in_grad_ref.shape[1]
-
     fields = []
     for start in range(0, SENT, groups):
         parts = [
@@ -402,27 +391,20 @@
         fields.extend(turned[turn * block : (turn + 1) * block] for turn in range(groups))
     shape = (3, x_rows, y_rows, z_length)
     forcing = jnp.concatenate(fields[6:9], axis=0).reshape(shape)
+    new_ref[...] = velocity_ref[...] + STEP_SIZE * forcing
     back_z = times_table(jnp.concatenate(fields[3:6], axis=0), z_ref[...])
-    new_ref[...] = velocity_ref[...] + STEP_SIZE * forcing
-    copies[0].start()
     back = jnp.concatenate(fields[:3], axis=0) + back_z
     grad_ref[...] = cotangent_ref[...] + back.reshape(shape)
-    copies[1].start()
-    sums = [
-        in_ref[device * RETURNED + SENT : device * RETURNED + SENT + 5, :]
-        for device in range(devices)
-    ]
-    while len(sums) > 1:
-        sums = [one + other for one, other in zip(sums[::2], sums[1::2])]
-    sums = sums[0] * (1.0 / cells)
+
+    sums = in_ref[SENT : SENT + 5, :]
+    for device in range(1, devices):
+        place = device * RETURNED + SENT
+        sums = sums + in_ref[place : place + 5, :]
+    sums = sums * (1.0 / cells)
     in_grad_ref[:5, :] = sums[:, :units]
     in_grad_ref[5:, :] = sums[:1, units:]
     bias_grad_ref[...] = sums[1:2, units:]
     out_grad_ref[...] = sums[2:, units:]
-    for copy in copies[2:]:
-        copy.start()
-    for copy in copies:
-        copy.wait()
 
 
 def on_device(kernel, shapes, scratch=(), **more):
@@ -493,11 +475,7 @@
     back = lax.all_to_all(back, axes, 0, 0, tiled=True).reshape(devices * RETURNED, LANES)
     shapes = [velocity.shape, velocity.shape, (6, units), (1, units), (3, units)]
     new, grad, grad_in, grad_bias, grad_out = on_device(
-        functools.partial(unpack_kernel, float(cells)),
-        [(shape, single) for shape in shapes],
-        [pltpu.VMEM(shape, single) for shape in shapes]
-        + [pltpu.SemaphoreType.DMA((len(shapes),))],
-        out_specs=[in_place] * len(shapes),
+        functools.partial(unpack_kernel, float(cells)), [(shape, single) for shape in shapes]
     )(back, velocity, cotangent, split_table(z_table))
     return (new, grad, grad_in, grad_bias[0], grad_out.T)
 

time: 32.9 us -> 32.8 us (level)
  no operation moved by 1% of the time
where the time goes in v9:
time: 32.8 us; the launch traced here: 32.6 us
  blocking collectives  27.3 us (83%)
  Pallas kernels  4.65 us (14%)
  between operations  0.69 us (2%)
    all_to_all x1, blocking collectives, local_kernels(): lax.all_to_all(sent, axes, 0, 0, tiled=True).reshape(devices * SENT, LANES)  14.9 us
    all_to_all x1, blocking collectives, local_kernels(): lax.all_to_all(back, axes, 0, 0, tiled=True)  12.3 us
    pallas_call x1, Pallas kernels, local_kernels(): on_device(functools.partial(middle_kernel, x_devices), [((devices * RETUR...  2.12 us
    pallas_call x1, Pallas kernels, local_kernels(): on_device(pack_kernel, [((devices * SENT, LANES), single), ((2 * units, L...  1.47 us
    pallas_call x1, Pallas kernels, local_kernels(): on_device(functools.partial(unpack_kernel, float(cells)), [(shape, single...  1.06 us

profile of v9, /device:TPU:0, one launch (start us, length us, event | category | flops | bytes accessed | tf_op | source)
XLA Modules:
  0.0 32.6 jit_solution(1920900758316387949)
XLA Ops:
  0.6 0.0 copy-start.3
  0.6 0.0 copy-start.4
  0.7 1.5 %shard_map.128 = (f32[288,128]{1,0:T(8,128)S(1)}, bf16[128,128]{1,0:T(8,128)(2,1)S(1)}, bf16[48,256]{1,0:T(8,128)(2,1)S(1)}) custom-call(f32[3,4,8,128]{3,2,1,0:T(8,128)} %velocity_ref.1, f32[3,4,8,128]{3,2,1,0:T(8,128)} %cotangent_ref.1, f32[128,128]{1,0:T(8,128)} %constant.8.clone.z_hbm, f32[6,64]{1,0:T(8,128)} %weight_in_hbm.1, f32[1,64]{1,0:T(1,128)} %bitcast.13, ...), custom_call_target="tpu_custom_call" | custom-call | tf_op jit(solution)/shard_map/pallas_call | solution.py:456
  2.1 14.9 %all_to_all.10 = f32[32,1,1152]{2,1,0:T(1,128)S(1)} all-to-all(f32[32,1,1152]{2,1,0:T(1,128)S(1)} %bitcast.11), channel_id=1, replica_groups=mesh['gx'=8,'gy'=4] {'gy','gx'}, dimensions={0} | all-to-all | bytes 294912 | tf_op jit(solution)/shard_map/all_to_all | solution.py:468
  17.1 0.0 copy-done.3
  17.1 0.0 copy-done.4
  17.1 2.1 %shard_map.129 = f32[448,128]{1,0:T(8,128)S(1)} custom-call(f32[288,128]{1,0:T(8,128)S(1)} %bitcast.10, bf16[128,128]{1,0:T(8,128)(2,1)S(1)} %get-tuple-element.14.before_ref, bf16[48,256]{1,0:T(8,128)(2,1)S(1)} %get-tuple-element.15.after_ref, bf16[768,128]{1,0:T(8,128)(2,1)S(1)} %copy-done.4, bf16[768,128]{1,0:T(8,128)(2,1)S(1)} %copy-done.3), custom_call_target="tpu_custom_call" | custom-call | tf_op jit(solution)/shard_map/pallas_call | solution.py:469
  19.2 0.0 copy-start
  19.2 0.0 copy-start.1
  19.2 0.0 copy-start.2
  19.2 12.3 %all_to_all.11 = f32[32,1,1792]{2,1,0:T(1,128)S(1)} all-to-all(f32[32,1,1792]{2,1,0:T(1,128)S(1)} %bitcast.9), channel_id=1, replica_groups=mesh['gx'=8,'gy'=4] {'gy','gx'}, dimensions={0} | all-to-all | bytes 458752 | tf_op jit(solution)/shard_map/all_to_all | solution.py:475
  31.6 0.0 copy-done
  31.6 0.0 copy-done.1
  31.6 0.0 copy-done.2
  31.6 1.1 %shard_map.130 = (f32[3,4,8,128]{3,2,1,0:T(8,128)}, f32[3,4,8,128]{3,2,1,0:T(8,128)}, f32[6,64]{1,0:T(8,128)}, f32[1,64]{1,0:T(1,128)}, f32[3,64]{1,0:T(4,128)}) custom-call(f32[448,128]{1,0:T(8,128)S(1)} %bitcast.8, f32[3,4,8,128]{3,2,1,0:T(8,128)S(1)} %copy-done, f32[3,4,8,128]{3,2,1,0:T(8,128)S(1)} %copy-done.1, bf16[768,128]{1,0:T(8,128)(2,1)S(1)} %copy-done.2), custom_call_target="tpu_custom_call" | custom-call | tf_op jit(solution)/shard_map/pallas_call | solution.py:477
Async XLA Ops:
  0.6 16.4 %copy-start.3 = (bf16[768,128]{1,0:T(8,128)(2,1)S(1)}, bf16[768,128]{1,0:T(8,128)(2,1)}, u32[]{:S(2)}) copy-start(bf16[768,128]{1,0:T(8,128)(2,1)} %constant.10.clone.y_back_ref) | copy-start | bytes 589828
  0.6 16.4 %copy-start.4 = (bf16[768,128]{1,0:T(8,128)(2,1)S(1)}, bf16[768,128]{1,0:T(8,128)(2,1)}, u32[]{:S(2)}) copy-start(bf16[768,128]{1,0:T(8,128)(2,1)} %constant.9.clone.y_ref) | copy-start | bytes 589828
  19.2 12.4 %copy-start = (f32[3,4,8,128]{3,2,1,0:T(8,128)S(1)}, f32[3,4,8,128]{3,2,1,0:T(8,128)}, u32[]{:S(2)}) copy-start(f32[3,4,8,128]{3,2,1,0:T(8,128)} %velocity_ref.1) | copy-start | bytes 147460
  19.2 12.4 %copy-start.1 = (f32[3,4,8,128]{3,2,1,0:T(8,128)S(1)}, f32[3,4,8,128]{3,2,1,0:T(8,128)}, u32[]{:S(2)}) copy-start(f32[3,4,8,128]{3,2,1,0:T(8,128)} %cotangent_ref.1) | copy-start | bytes 147460
  19.2 12.3 %copy-start.2 = (bf16[768,128]{1,0:T(8,128)(2,1)S(1)}, bf16[768,128]{1,0:T(8,128)(2,1)}, u32[]{:S(2)}) copy-start(bf16[768,128]{1,0:T(8,128)(2,1)} %constant.11.clone.z_ref) | copy-start | bytes 589828

commit v10 on v9

--- a/solution.py
+++ b/solution.py
@@ -312,7 +312,7 @@
 
     before = before_ref[...]
     after = after_ref[...]
-    at_once = 8
+    at_once = 2
     sums = jnp.zeros((32, 4 * units), jnp.float32)
     results = []
     for start in range(0, x_length, at_once):

time: 32.8 us -> 34.7 us (1.058)
  Pallas kernels: 4.65 us -> 6.51 us
    pallas_call x1, Pallas kernels: 2.12 us -> 3.99 us  [local_kernels(): on_device(functools.partial(middle_kernel, x_devices), [((devices * RETUR...]
where the time goes in v10:
time: 34.7 us; the launch traced here: 34.5 us
  blocking collectives  27.3 us (79%)
  Pallas kernels  6.51 us (19%)
  between operations  0.69 us (2%)
    all_to_all x1, blocking collectives, local_kernels(): lax.all_to_all(sent, axes, 0, 0, tiled=True).reshape(devices * SENT, LANES)  14.9 us
    all_to_all x1, blocking collectives, local_kernels(): lax.all_to_all(back, axes, 0, 0, tiled=True)  12.3 us
    pallas_call x1, Pallas kernels, local_kernels(): on_device(functools.partial(middle_kernel, x_devices), [((devices * RETUR...  3.99 us
    pallas_call x1, Pallas kernels, local_kernels(): on_device(pack_kernel, [((devices * SENT, LANES), single), ((2 * units, L...  1.47 us
    pallas_call x1, Pallas kernels, local_kernels(): on_device(functools.partial(unpack_kernel, float(cells)), [(shape, single...  1.06 us

profile of v10, /device:TPU:0, one launch (start us, length us, event | category | flops | bytes accessed | tf_op | source)
XLA Modules:
  0.0 34.5 jit_solution(10578278630831304324)
XLA Ops:
  0.6 0.0 copy-start.3
  0.6 0.0 copy-start.4
  0.7 1.5 %shard_map.128 = (f32[288,128]{1,0:T(8,128)S(1)}, bf16[128,128]{1,0:T(8,128)(2,1)S(1)}, bf16[48,256]{1,0:T(8,128)(2,1)S(1)}) custom-call(f32[3,4,8,128]{3,2,1,0:T(8,128)} %velocity_ref.1, f32[3,4,8,128]{3,2,1,0:T(8,128)} %cotangent_ref.1, f32[128,128]{1,0:T(8,128)} %constant.8.clone.z_hbm, f32[6,64]{1,0:T(8,128)} %weight_in_hbm.1, f32[1,64]{1,0:T(1,128)} %bitcast.13, ...), custom_call_target="tpu_custom_call" | custom-call | tf_op jit(solution)/shard_map/pallas_call | solution.py:456
  2.1 14.9 %all_to_all.10 = f32[32,1,1152]{2,1,0:T(1,128)S(1)} all-to-all(f32[32,1,1152]{2,1,0:T(1,128)S(1)} %bitcast.11), channel_id=1, replica_groups=mesh['gx'=8,'gy'=4] {'gy','gx'}, dimensions={0} | all-to-all | bytes 294912 | tf_op jit(solution)/shard_map/all_to_all | solution.py:468
  17.1 0.0 copy-done.3
  17.1 0.0 copy-done.4
  17.1 4.0 %shard_map.129 = f32[448,128]{1,0:T(8,128)S(1)} custom-call(f32[288,128]{1,0:T(8,128)S(1)} %bitcast.10, bf16[128,128]{1,0:T(8,128)(2,1)S(1)} %get-tuple-element.14.before_ref, bf16[48,256]{1,0:T(8,128)(2,1)S(1)} %get-tuple-element.15.after_ref, bf16[768,128]{1,0:T(8,128)(2,1)S(1)} %copy-done.4, bf16[768,128]{1,0:T(8,128)(2,1)S(1)} %copy-done.3), custom_call_target="tpu_custom_call" | custom-call | tf_op jit(solution)/shard_map/pallas_call | solution.py:469
  21.1 0.0 copy-start
  21.1 0.0 copy-start.1
  21.1 0.0 copy-start.2
  21.1 12.3 %all_to_all.11 = f32[32,1,1792]{2,1,0:T(1,128)S(1)} all-to-all(f32[32,1,1792]{2,1,0:T(1,128)S(1)} %bitcast.9), channel_id=1, replica_groups=mesh['gx'=8,'gy'=4] {'gy','gx'}, dimensions={0} | all-to-all | bytes 458752 | tf_op jit(solution)/shard_map/all_to_all | solution.py:475
  33.4 0.0 copy-done
  33.4 0.0 copy-done.1
  33.4 0.0 copy-done.2
  33.4 1.1 %shard_map.130 = (f32[3,4,8,128]{3,2,1,0:T(8,128)}, f32[3,4,8,128]{3,2,1,0:T(8,128)}, f32[6,64]{1,0:T(8,128)}, f32[1,64]{1,0:T(1,128)}, f32[3,64]{1,0:T(4,128)}) custom-call(f32[448,128]{1,0:T(8,128)S(1)} %bitcast.8, f32[3,4,8,128]{3,2,1,0:T(8,128)S(1)} %copy-done, f32[3,4,8,128]{3,2,1,0:T(8,128)S(1)} %copy-done.1, bf16[768,128]{1,0:T(8,128)(2,1)S(1)} %copy-done.2), custom_call_target="tpu_custom_call" | custom-call | tf_op jit(solution)/shard_map/pallas_call | solution.py:477
Async XLA Ops:
  0.6 16.4 %copy-start.3 = (bf16[768,128]{1,0:T(8,128)(2,1)S(1)}, bf16[768,128]{1,0:T(8,128)(2,1)}, u32[]{:S(2)}) copy-start(bf16[768,128]{1,0:T(8,128)(2,1)} %constant.10.clone.y_back_ref) | copy-start | bytes 589828
  0.6 16.4 %copy-start.4 = (bf16[768,128]{1,0:T(8,128)(2,1)S(1)}, bf16[768,128]{1,0:T(8,128)(2,1)}, u32[]{:S(2)}) copy-start(bf16[768,128]{1,0:T(8,128)(2,1)} %constant.9.clone.y_ref) | copy-start | bytes 589828
  21.1 12.4 %copy-start = (f32[3,4,8,128]{3,2,1,0:T(8,128)S(1)}, f32[3,4,8,128]{3,2,1,0:T(8,128)}, u32[]{:S(2)}) copy-start(f32[3,4,8,128]{3,2,1,0:T(8,128)} %velocity_ref.1) | copy-start | bytes 147460
  21.1 12.4 %copy-start.1 = (f32[3,4,8,128]{3,2,1,0:T(8,128)S(1)}, f32[3,4,8,128]{3,2,1,0:T(8,128)}, u32[]{:S(2)}) copy-start(f32[3,4,8,128]{3,2,1,0:T(8,128)} %cotangent_ref.1) | copy-start | bytes 147460
  21.1 12.3 %copy-start.2 = (bf16[768,128]{1,0:T(8,128)(2,1)S(1)}, bf16[768,128]{1,0:T(8,128)(2,1)}, u32[]{:S(2)}) copy-start(bf16[768,128]{1,0:T(8,128)(2,1)} %constant.11.clone.z_ref) | copy-start | bytes 589828

commit v11 on v10

--- a/solution.py
+++ b/solution.py
@@ -184,13 +184,9 @@
     return jnp.concatenate([pieces[turn] for turn in RIGHT_PIECES], axis=0)
 
 
-def by_parts(rows, wide_table):
-    half = len(rows) // 2
-    outs = []
-    for start in (0, half):
-        out = times_table(jnp.concatenate(rows[start : start + half], axis=0), wide_table)
-        outs.extend(out[8 * turn : 8 * turn + 8] for turn in range(half))
-    return outs
+def on_rows(rows, wide_table):
+    out = times_table(jnp.concatenate(rows, axis=0), wide_table)
+    return [out[8 * turn : 8 * turn + 8] for turn in range(len(rows))]
 
 
 def pack_kernel(
@@ -300,7 +296,7 @@
     tails = exchange(tails, y_rows)
 
     smoothed = smooth_rows(planes)
-    along_y = by_parts(smoothed, y_ref[...])
+    along_y = on_rows(smoothed, y_ref[...])
     upper_rows = []
     lower_rows = []
     for x in range(x_length):
@@ -312,7 +308,7 @@
 
     before = before_ref[...]
     after = after_ref[...]
-    at_once = 2
+    at_once = x_length
     sums = jnp.zeros((32, 4 * units), jnp.float32)
     results = []
     for start in range(0, x_length, at_once):
@@ -339,7 +335,7 @@
             place = (x % x_rows) * x_devices + x // x_rows
             tail_ref[place : place + 1, :] = result[8:9, turn * LANES : (turn + 1) * LANES]
 
-    back_y = by_parts(results, y_back_ref[...])
+    back_y = on_rows(results, y_back_ref[...])
     back = [jnp.where(row8 < 3, back_y[x], results[x]) for x in range(x_length)]
     back = smooth_rows(back)
     back = [jnp.where(row8 < 6, value, result) for value, result in zip(back, results)]

time: 34.7 us -> 32.7 us (0.942)
  Pallas kernels: 6.51 us -> 4.51 us
    pallas_call x1, Pallas kernels: 3.99 us -> 1.98 us  [local_kernels(): on_device(functools.partial(middle_kernel, x_devices), [((devices * RETUR...]
where the time goes in v11:
time: 32.7 us; the launch traced here: 32.5 us
  blocking collectives  27.3 us (83%)
  Pallas kernels  4.51 us (14%)
  between operations  0.69 us (2%)
    all_to_all x1, blocking collectives, local_kernels(): lax.all_to_all(sent, axes, 0, 0, tiled=True).reshape(devices * SENT, LANES)  14.9 us
    all_to_all x1, blocking collectives, local_kernels(): lax.all_to_all(back, axes, 0, 0, tiled=True)  12.3 us
    pallas_call x1, Pallas kernels, local_kernels(): on_device(functools.partial(middle_kernel, x_devices), [((devices * RETUR...  1.98 us
    pallas_call x1, Pallas kernels, local_kernels(): on_device(pack_kernel, [((devices * SENT, LANES), single), ((2 * units, L...  1.47 us
    pallas_call x1, Pallas kernels, local_kernels(): on_device(functools.partial(unpack_kernel, float(cells)), [(shape, single...  1.06 us

profile of v11, /device:TPU:0, one launch (start us, length us, event | category | flops | bytes accessed | tf_op | source)
XLA Modules:
  0.0 32.5 jit_solution(3356431015837854062)
XLA Ops:
  0.6 0.0 copy-start.3
  0.6 0.0 copy-start.4
  0.7 1.5 %shard_map.128 = (f32[288,128]{1,0:T(8,128)S(1)}, bf16[128,128]{1,0:T(8,128)(2,1)S(1)}, bf16[48,256]{1,0:T(8,128)(2,1)S(1)}) custom-call(f32[3,4,8,128]{3,2,1,0:T(8,128)} %velocity_ref.1, f32[3,4,8,128]{3,2,1,0:T(8,128)} %cotangent_ref.1, f32[128,128]{1,0:T(8,128)} %constant.8.clone.z_hbm, f32[6,64]{1,0:T(8,128)} %weight_in_hbm.1, f32[1,64]{1,0:T(1,128)} %bitcast.13, ...), custom_call_target="tpu_custom_call" | custom-call | tf_op jit(solution)/shard_map/pallas_call | solution.py:452
  2.1 14.9 %all_to_all.10 = f32[32,1,1152]{2,1,0:T(1,128)S(1)} all-to-all(f32[32,1,1152]{2,1,0:T(1,128)S(1)} %bitcast.11), channel_id=1, replica_groups=mesh['gx'=8,'gy'=4] {'gy','gx'}, dimensions={0} | all-to-all | bytes 294912 | tf_op jit(solution)/shard_map/all_to_all | solution.py:464
  17.1 0.0 copy-done.3
  17.1 0.0 copy-done.4
  17.1 2.0 %shard_map.129 = f32[448,128]{1,0:T(8,128)S(1)} custom-call(f32[288,128]{1,0:T(8,128)S(1)} %bitcast.10, bf16[128,128]{1,0:T(8,128)(2,1)S(1)} %get-tuple-element.14.before_ref, bf16[48,256]{1,0:T(8,128)(2,1)S(1)} %get-tuple-element.15.after_ref, bf16[768,128]{1,0:T(8,128)(2,1)S(1)} %copy-done.4, bf16[768,128]{1,0:T(8,128)(2,1)S(1)} %copy-done.3), custom_call_target="tpu_custom_call" | custom-call | tf_op jit(solution)/shard_map/pallas_call | solution.py:465
  19.1 0.0 copy-start
  19.1 0.0 copy-start.1
  19.1 0.0 copy-start.2
  19.1 12.3 %all_to_all.11 = f32[32,1,1792]{2,1,0:T(1,128)S(1)} all-to-all(f32[32,1,1792]{2,1,0:T(1,128)S(1)} %bitcast.9), channel_id=1, replica_groups=mesh['gx'=8,'gy'=4] {'gy','gx'}, dimensions={0} | all-to-all | bytes 458752 | tf_op jit(solution)/shard_map/all_to_all | solution.py:471
  31.4 0.0 copy-done
  31.4 0.0 copy-done.1
  31.4 0.0 copy-done.2
  31.4 1.1 %shard_map.130 = (f32[3,4,8,128]{3,2,1,0:T(8,128)}, f32[3,4,8,128]{3,2,1,0:T(8,128)}, f32[6,64]{1,0:T(8,128)}, f32[1,64]{1,0:T(1,128)}, f32[3,64]{1,0:T(4,128)}) custom-call(f32[448,128]{1,0:T(8,128)S(1)} %bitcast.8, f32[3,4,8,128]{3,2,1,0:T(8,128)S(1)} %copy-done, f32[3,4,8,128]{3,2,1,0:T(8,128)S(1)} %copy-done.1, bf16[768,128]{1,0:T(8,128)(2,1)S(1)} %copy-done.2), custom_call_target="tpu_custom_call" | custom-call | tf_op jit(solution)/shard_map/pallas_call | solution.py:473
Async XLA Ops:
  0.6 16.4 %copy-start.3 = (bf16[768,128]{1,0:T(8,128)(2,1)S(1)}, bf16[768,128]{1,0:T(8,128)(2,1)}, u32[]{:S(2)}) copy-start(bf16[768,128]{1,0:T(8,128)(2,1)} %constant.10.clone.y_back_ref) | copy-start | bytes 589828
  0.6 16.4 %copy-start.4 = (bf16[768,128]{1,0:T(8,128)(2,1)S(1)}, bf16[768,128]{1,0:T(8,128)(2,1)}, u32[]{:S(2)}) copy-start(bf16[768,128]{1,0:T(8,128)(2,1)} %constant.9.clone.y_ref) | copy-start | bytes 589828
  19.1 12.4 %copy-start = (f32[3,4,8,128]{3,2,1,0:T(8,128)S(1)}, f32[3,4,8,128]{3,2,1,0:T(8,128)}, u32[]{:S(2)}) copy-start(f32[3,4,8,128]{3,2,1,0:T(8,128)} %velocity_ref.1) | copy-start | bytes 147460
  19.1 12.4 %copy-start.1 = (f32[3,4,8,128]{3,2,1,0:T(8,128)S(1)}, f32[3,4,8,128]{3,2,1,0:T(8,128)}, u32[]{:S(2)}) copy-start(f32[3,4,8,128]{3,2,1,0:T(8,128)} %cotangent_ref.1) | copy-start | bytes 147460
  19.1 12.3 %copy-start.2 = (bf16[768,128]{1,0:T(8,128)(2,1)S(1)}, bf16[768,128]{1,0:T(8,128)(2,1)}, u32[]{:S(2)}) copy-start(bf16[768,128]{1,0:T(8,128)(2,1)} %constant.11.clone.z_ref) | copy-start | bytes 589828

commit v12 on v11

--- a/solution.py
+++ b/solution.py
@@ -243,7 +243,7 @@
         axis=1,
     )
     pieces = [piece.astype(jnp.float32) for piece in split(before, 3)]
-    before = jnp.concatenate([pieces[turn] for turn in RIGHT_PIECES + (1, 2)], axis=0)
+    before = jnp.concatenate([pieces[turn] for turn in RIGHT_PIECES + (0, 0)], axis=0)
     before_ref[...] = before.T.astype(jnp.bfloat16)
     pieces = split(after, 3)
     after_ref[...] = jnp.concatenate(
@@ -306,10 +306,10 @@
         upper_rows.append(features)
         lower_rows.append(jnp.where(row8 == 5, last, planes[x]))
 
-    before = before_ref[...]
+    before = before_ref[:, : 16 * len(LEFT_PIECES)]
     after = after_ref[...]
     at_once = x_length
-    sums = jnp.zeros((32, 4 * units), jnp.float32)
+    sums = jnp.zeros((4 * units, 32), jnp.float32)
     results = []
     for start in range(0, x_length, at_once):
         stop = start + at_once
@@ -321,12 +321,12 @@
             axis=0,
         )
         pieces = split(cells, 3)
-        both = times(before, jnp.concatenate([pieces[turn] for turn in LEFT_PIECES + (2, 1)], axis=0))
+        both = times(before, jnp.concatenate([pieces[turn] for turn in LEFT_PIECES], axis=0))
         hidden = jnp.tanh(both[:units])
         grad_pre = both[units:] * (1.0 - hidden * hidden)
         both = jnp.concatenate([hidden, grad_pre], axis=0)
         both = jnp.concatenate(split(both, 2), axis=0)
-        sums = sums + times(jnp.concatenate(pieces[:2], axis=0), both, (1, 1))
+        sums = sums + times(both, jnp.concatenate(pieces[:2], axis=0), (1, 1))
         result = times(after, both)
         result = result[:16] + result[16:32] + result[32:]
         for turn in range(at_once):
@@ -351,8 +351,10 @@
         place = turn * x_devices * RETURNED + 8
         out_ref[pl.ds(place, x_devices, stride=RETURNED), :] = tails[turn]
 
-    sums = sums[:, : 2 * units] + sums[:, 2 * units :]
-    sums = sums[:16] + sums[16:]
+    sums = sums[: 2 * units] + sums[2 * units :]
+    fill = jnp.zeros((2 * units, LANES - 32), jnp.float32)
+    sums = jnp.concatenate([sums, fill], axis=1).T
+    sums = sums[:16] + sums[16:32]
     moved = jnp.concatenate([sums[5:7, units:], STEP_SIZE * sums[13:16, :units]], axis=0)
     packed = jnp.concatenate([sums[:5, units:], moved], axis=1)
     for device in range(x_devices * y_devices):

time: 32.7 us -> 32.7 us (level)
  no operation moved by 1% of the time
where the time goes in v12:
time: 32.7 us; the launch traced here: 32.6 us
  blocking collectives  27.3 us (83%)
  Pallas kernels  4.57 us (14%)
  between operations  0.69 us (2%)
    all_to_all x1, blocking collectives, local_kernels(): lax.all_to_all(sent, axes, 0, 0, tiled=True).reshape(devices * SENT, LANES)  14.9 us
    all_to_all x1, blocking collectives, local_kernels(): lax.all_to_all(back, axes, 0, 0, tiled=True)  12.3 us
    pallas_call x1, Pallas kernels, local_kernels(): on_device(functools.partial(middle_kernel, x_devices), [((devices * RETUR...  2.05 us
    pallas_call x1, Pallas kernels, local_kernels(): on_device(pack_kernel, [((devices * SENT, LANES), single), ((2 * units, L...  1.47 us
    pallas_call x1, Pallas kernels, local_kernels(): on_device(functools.partial(unpack_kernel, float(cells)), [(shape, single...  1.06 us

profile of v12, /device:TPU:0, one launch (start us, length us, event | category | flops | bytes accessed | tf_op | source)
XLA Modules:
  0.0 32.6 jit_solution(16813605096472395904)
XLA Ops:
  0.6 0.0 copy-start.3
  0.6 0.0 copy-start.4
  0.7 1.5 %shard_map.128 = (f32[288,128]{1,0:T(8,128)S(1)}, bf16[128,128]{1,0:T(8,128)(2,1)S(1)}, bf16[48,256]{1,0:T(8,128)(2,1)S(1)}) custom-call(f32[3,4,8,128]{3,2,1,0:T(8,128)} %velocity_ref.1, f32[3,4,8,128]{3,2,1,0:T(8,128)} %cotangent_ref.1, f32[128,128]{1,0:T(8,128)} %constant.8.clone.z_hbm, f32[6,64]{1,0:T(8,128)} %weight_in_hbm.1, f32[1,64]{1,0:T(1,128)} %bitcast.13, ...), custom_call_target="tpu_custom_call" | custom-call | tf_op jit(solution)/shard_map/pallas_call | solution.py:454
  2.1 14.9 %all_to_all.10 = f32[32,1,1152]{2,1,0:T(1,128)S(1)} all-to-all(f32[32,1,1152]{2,1,0:T(1,128)S(1)} %bitcast.11), channel_id=1, replica_groups=mesh['gx'=8,'gy'=4] {'gy','gx'}, dimensions={0} | all-to-all | bytes 294912 | tf_op jit(solution)/shard_map/all_to_all | solution.py:466
  17.1 0.0 copy-done.3
  17.1 0.0 copy-done.4
  17.1 2.0 %shard_map.129 = f32[448,128]{1,0:T(8,128)S(1)} custom-call(f32[288,128]{1,0:T(8,128)S(1)} %bitcast.10, bf16[128,128]{1,0:T(8,128)(2,1)S(1)} %get-tuple-element.14.before_ref, bf16[48,256]{1,0:T(8,128)(2,1)S(1)} %get-tuple-element.15.after_ref, bf16[768,128]{1,0:T(8,128)(2,1)S(1)} %copy-done.4, bf16[768,128]{1,0:T(8,128)(2,1)S(1)} %copy-done.3), custom_call_target="tpu_custom_call" | custom-call | tf_op jit(solution)/shard_map/pallas_call | solution.py:467
  19.1 0.0 copy-start
  19.1 0.0 copy-start.1
  19.1 0.0 copy-start.2
  19.2 12.3 %all_to_all.11 = f32[32,1,1792]{2,1,0:T(1,128)S(1)} all-to-all(f32[32,1,1792]{2,1,0:T(1,128)S(1)} %bitcast.9), channel_id=1, replica_groups=mesh['gx'=8,'gy'=4] {'gy','gx'}, dimensions={0} | all-to-all | bytes 458752 | tf_op jit(solution)/shard_map/all_to_all | solution.py:473
  31.5 0.0 copy-done
  31.5 0.0 copy-done.1
  31.5 0.0 copy-done.2
  31.5 1.1 %shard_map.130 = (f32[3,4,8,128]{3,2,1,0:T(8,128)}, f32[3,4,8,128]{3,2,1,0:T(8,128)}, f32[6,64]{1,0:T(8,128)}, f32[1,64]{1,0:T(1,128)}, f32[3,64]{1,0:T(4,128)}) custom-call(f32[448,128]{1,0:T(8,128)S(1)} %bitcast.8, f32[3,4,8,128]{3,2,1,0:T(8,128)S(1)} %copy-done, f32[3,4,8,128]{3,2,1,0:T(8,128)S(1)} %copy-done.1, bf16[768,128]{1,0:T(8,128)(2,1)S(1)} %copy-done.2), custom_call_target="tpu_custom_call" | custom-call | tf_op jit(solution)/shard_map/pallas_call | solution.py:475
Async XLA Ops:
  0.6 16.4 %copy-start.3 = (bf16[768,128]{1,0:T(8,128)(2,1)S(1)}, bf16[768,128]{1,0:T(8,128)(2,1)}, u32[]{:S(2)}) copy-start(bf16[768,128]{1,0:T(8,128)(2,1)} %constant.10.clone.y_back_ref) | copy-start | bytes 589828
  0.6 16.4 %copy-start.4 = (bf16[768,128]{1,0:T(8,128)(2,1)S(1)}, bf16[768,128]{1,0:T(8,128)(2,1)}, u32[]{:S(2)}) copy-start(bf16[768,128]{1,0:T(8,128)(2,1)} %constant.9.clone.y_ref) | copy-start | bytes 589828
  19.1 12.4 %copy-start = (f32[3,4,8,128]{3,2,1,0:T(8,128)S(1)}, f32[3,4,8,128]{3,2,1,0:T(8,128)}, u32[]{:S(2)}) copy-start(f32[3,4,8,128]{3,2,1,0:T(8,128)} %velocity_ref.1) | copy-start | bytes 147460
  19.1 12.4 %copy-start.1 = (f32[3,4,8,128]{3,2,1,0:T(8,128)S(1)}, f32[3,4,8,128]{3,2,1,0:T(8,128)}, u32[]{:S(2)}) copy-start(f32[3,4,8,128]{3,2,1,0:T(8,128)} %cotangent_ref.1) | copy-start | bytes 147460
  19.1 12.3 %copy-start.2 = (bf16[768,128]{1,0:T(8,128)(2,1)S(1)}, bf16[768,128]{1,0:T(8,128)(2,1)}, u32[]{:S(2)}) copy-start(bf16[768,128]{1,0:T(8,128)(2,1)} %constant.11.clone.z_ref) | copy-start | bytes 589828

commit v13 on v11

--- a/solution.py
+++ b/solution.py
@@ -343,13 +343,13 @@
         first = x_device * x_rows
         parts = exchange(back[first : first + x_rows], y_rows)
         for turn in range(y_devices):
-            place = (turn * x_devices + x_device) * RETURNED
+            place = (x_device * y_devices + turn) * RETURNED
             out_ref[place : place + 8, :] = parts[turn]
     tails = [tail_ref[x * x_devices : (x + 1) * x_devices, :] for x in range(x_rows)]
     tails = exchange(tails, y_rows)
     for turn in range(y_devices):
-        place = turn * x_devices * RETURNED + 8
-        out_ref[pl.ds(place, x_devices, stride=RETURNED), :] = tails[turn]
+        place = turn * RETURNED + 8
+        out_ref[pl.ds(place, x_devices, stride=y_devices * RETURNED), :] = tails[turn]
 
     sums = sums[:, : 2 * units] + sums[:, 2 * units :]
     sums = sums[:16] + sums[16:]
@@ -361,6 +361,7 @@
 
 
 def unpack_kernel(
+    x_devices,
     cells,
     in_ref,
     velocity_ref,
@@ -377,12 +378,16 @@
     groups = LANES // block
     devices = z_length // groups
     units = in_grad_ref.shape[1]
+    stride = devices // x_devices * RETURNED
     fields = []
     for start in range(0, SENT, groups):
-        parts = [
-            in_ref[pl.ds(min(field, SENT - 1), devices, stride=RETURNED), :]
-            for field in range(start, start + groups)
-        ]
+        parts = []
+        for field in range(start, start + groups):
+            rows = [
+                in_ref[pl.ds(place + min(field, SENT - 1), x_devices, stride=stride), :]
+                for place in range(0, stride, RETURNED)
+            ]
+            parts.append(jnp.concatenate(rows, axis=0))
         turned = jnp.concatenate(exchange(parts, block), axis=0).T
         fields.extend(turned[turn * block : (turn + 1) * block] for turn in range(groups))
     shape = (3, x_rows, y_rows, z_length)
@@ -428,7 +433,6 @@
 
 
 def local_kernels(velocity, cotangent, weight_in, bias_in, weight_out):
-    axes = ("gy", "gx")
     x_devices, y_devices = lax.axis_size("gx"), lax.axis_size("gy")
     devices = x_devices * y_devices
     _, x_rows, y_rows, z_length = velocity.shape
@@ -461,17 +465,19 @@
         in_specs=[in_place] * len(arguments),
     )(*arguments)
     sent = sent.reshape(devices, 1, SENT * LANES)
-    sent = lax.all_to_all(sent, axes, 0, 0, tiled=True).reshape(devices * SENT, LANES)
+    sent = lax.all_to_all(sent, ("gy", "gx"), 0, 0, tiled=True)
+    sent = sent.reshape(devices * SENT, LANES)
     (back,) = on_device(
         functools.partial(middle_kernel, x_devices),
         [((devices * RETURNED, LANES), single)],
         [pltpu.VMEM((x_devices * x_rows, LANES), single)],
     )(sent, *prepared, split_table(y_table.T), split_table(y_table))
     back = back.reshape(devices, 1, RETURNED * LANES)
-    back = lax.all_to_all(back, axes, 0, 0, tiled=True).reshape(devices * RETURNED, LANES)
+    back = lax.all_to_all(back, ("gx", "gy"), 0, 0, tiled=True)
+    back = back.reshape(devices * RETURNED, LANES)
     shapes = [velocity.shape, velocity.shape, (6, units), (1, units), (3, units)]
     new, grad, grad_in, grad_bias, grad_out = on_device(
-        functools.partial(unpack_kernel, float(cells)), [(shape, single) for shape in shapes]
+        functools.partial(unpack_kernel, x_devices, float(cells)), [(shape, single) for shape in shapes]
     )(back, velocity, cotangent, split_table(z_table))
     return (new, grad, grad_in, grad_bias[0], grad_out.T)
 

time: 32.7 us -> 32.7 us (level)
  no operation moved by 1% of the time
where the time goes in v13:
time: 32.7 us; the launch traced here: 32.5 us
  blocking collectives  27.3 us (83%)
  Pallas kernels  4.51 us (14%)
  between operations  0.69 us (2%)
    all_to_all x1, blocking collectives, local_kernels(): sent = lax.all_to_all(sent, ('gy', 'gx'), 0, 0, tiled=True)  14.9 us
    all_to_all x1, blocking collectives, local_kernels(): back = lax.all_to_all(back, ('gx', 'gy'), 0, 0, tiled=True)  12.3 us
    pallas_call x1, Pallas kernels, local_kernels(): on_device(functools.partial(middle_kernel, x_devices), [((devices * RETUR...  1.98 us
    pallas_call x1, Pallas kernels, local_kernels(): on_device(pack_kernel, [((devices * SENT, LANES), single), ((2 * units, L...  1.47 us
    pallas_call x1, Pallas kernels, local_kernels(): on_device(functools.partial(unpack_kernel, x_devices, float(cells)), [(sh...  1.06 us

profile of v13, /device:TPU:0, one launch (start us, length us, event | category | flops | bytes accessed | tf_op | source)
XLA Modules:
  0.0 32.5 jit_solution(12714075856105309462)
XLA Ops:
  0.6 0.0 copy-start.3
  0.6 0.0 copy-start.4
  0.7 1.5 %shard_map.128 = (f32[288,128]{1,0:T(8,128)S(1)}, bf16[128,128]{1,0:T(8,128)(2,1)S(1)}, bf16[48,256]{1,0:T(8,128)(2,1)S(1)}) custom-call(f32[3,4,8,128]{3,2,1,0:T(8,128)} %velocity_ref.1, f32[3,4,8,128]{3,2,1,0:T(8,128)} %cotangent_ref.1, f32[128,128]{1,0:T(8,128)} %constant.8.clone.z_hbm, f32[6,64]{1,0:T(8,128)} %weight_in_hbm.1, f32[1,64]{1,0:T(1,128)} %bitcast.13, ...), custom_call_target="tpu_custom_call" | custom-call | tf_op jit(solution)/shard_map/pallas_call | solution.py:456
  2.1 14.9 %all_to_all.10 = f32[32,1,1152]{2,1,0:T(1,128)S(1)} all-to-all(f32[32,1,1152]{2,1,0:T(1,128)S(1)} %bitcast.11), channel_id=1, replica_groups=mesh['gx'=8,'gy'=4] {'gy','gx'}, dimensions={0} | all-to-all | bytes 294912 | tf_op jit(solution)/shard_map/all_to_all | solution.py:468
  17.1 0.0 copy-done.3
  17.1 0.0 copy-done.4
  17.1 2.0 %shard_map.129 = f32[448,128]{1,0:T(8,128)S(1)} custom-call(f32[288,128]{1,0:T(8,128)S(1)} %bitcast.10, bf16[128,128]{1,0:T(8,128)(2,1)S(1)} %get-tuple-element.14.before_ref, bf16[48,256]{1,0:T(8,128)(2,1)S(1)} %get-tuple-element.15.after_ref, bf16[768,128]{1,0:T(8,128)(2,1)S(1)} %copy-done.4, bf16[768,128]{1,0:T(8,128)(2,1)S(1)} %copy-done.3), custom_call_target="tpu_custom_call" | custom-call | tf_op jit(solution)/shard_map/pallas_call | solution.py:470
  19.1 0.0 copy-start
  19.1 0.0 copy-start.1
  19.1 0.0 copy-start.2
  19.1 12.3 %all_to_all.11 = f32[32,1,1792]{2,1,0:T(1,128)S(1)} all-to-all(f32[32,1,1792]{2,1,0:T(1,128)S(1)} %bitcast.9), channel_id=1, replica_groups=mesh['gx'=8,'gy'=4] {'gx','gy'}, dimensions={0} | all-to-all | bytes 458752 | tf_op jit(solution)/shard_map/all_to_all | solution.py:476
  31.4 0.0 copy-done
  31.4 0.0 copy-done.1
  31.4 0.0 copy-done.2
  31.5 1.1 %shard_map.130 = (f32[3,4,8,128]{3,2,1,0:T(8,128)}, f32[3,4,8,128]{3,2,1,0:T(8,128)}, f32[6,64]{1,0:T(8,128)}, f32[1,64]{1,0:T(1,128)}, f32[3,64]{1,0:T(4,128)}) custom-call(f32[448,128]{1,0:T(8,128)S(1)} %bitcast.8, f32[3,4,8,128]{3,2,1,0:T(8,128)S(1)} %copy-done, f32[3,4,8,128]{3,2,1,0:T(8,128)S(1)} %copy-done.1, bf16[768,128]{1,0:T(8,128)(2,1)S(1)} %copy-done.2), custom_call_target="tpu_custom_call" | custom-call | tf_op jit(solution)/shard_map/pallas_call | solution.py:479
Async XLA Ops:
  0.6 16.4 %copy-start.3 = (bf16[768,128]{1,0:T(8,128)(2,1)S(1)}, bf16[768,128]{1,0:T(8,128)(2,1)}, u32[]{:S(2)}) copy-start(bf16[768,128]{1,0:T(8,128)(2,1)} %constant.10.clone.y_back_ref) | copy-start | bytes 589828
  0.6 16.4 %copy-start.4 = (bf16[768,128]{1,0:T(8,128)(2,1)S(1)}, bf16[768,128]{1,0:T(8,128)(2,1)}, u32[]{:S(2)}) copy-start(bf16[768,128]{1,0:T(8,128)(2,1)} %constant.9.clone.y_ref) | copy-start | bytes 589828
  19.1 12.4 %copy-start = (f32[3,4,8,128]{3,2,1,0:T(8,128)S(1)}, f32[3,4,8,128]{3,2,1,0:T(8,128)}, u32[]{:S(2)}) copy-start(f32[3,4,8,128]{3,2,1,0:T(8,128)} %velocity_ref.1) | copy-start | bytes 147460
  19.1 12.4 %copy-start.1 = (f32[3,4,8,128]{3,2,1,0:T(8,128)S(1)}, f32[3,4,8,128]{3,2,1,0:T(8,128)}, u32[]{:S(2)}) copy-start(f32[3,4,8,128]{3,2,1,0:T(8,128)} %cotangent_ref.1) | copy-start | bytes 147460
  19.1 12.4 %copy-start.2 = (bf16[768,128]{1,0:T(8,128)(2,1)S(1)}, bf16[768,128]{1,0:T(8,128)(2,1)}, u32[]{:S(2)}) copy-start(bf16[768,128]{1,0:T(8,128)(2,1)} %constant.11.clone.z_ref) | copy-start | bytes 589828

commit v14 on v11

--- a/solution.py
+++ b/solution.py
@@ -211,10 +211,14 @@
         (weight_in_hbm, weight_in_ref),
         (bias_hbm, bias_ref),
         (weight_out_hbm, weight_out_ref),
-        (velocity_hbm, velocity_ref),
-        (cotangent_hbm, cotangent_ref),
-        (z_hbm, z_ref),
     ]
+    pairs += [
+        (whole.at[part], held.at[part])
+        for whole, held in ((velocity_hbm, velocity_ref), (cotangent_hbm, cotangent_ref))
+        for part in range(3)
+    ]
+    half = z_ref.shape[0] // 2
+    pairs += [(z_hbm.at[part], z_ref.at[part]) for part in (pl.ds(0, half), pl.ds(half, half))]
     copies = [
         pltpu.make_async_copy(source, target, arrived.at[turn])
         for turn, (source, target) in enumerate(pairs)
@@ -308,32 +312,42 @@
 
     before = before_ref[...]
     after = after_ref[...]
-    at_once = x_length
+    at_once = 2 * x_rows
     sums = jnp.zeros((32, 4 * units), jnp.float32)
     results = []
-    for start in range(0, x_length, at_once):
-        stop = start + at_once
-        cells = jnp.concatenate(
-            [
-                jnp.concatenate(upper_rows[start:stop], axis=1),
-                jnp.concatenate(lower_rows[start:stop], axis=1),
-            ],
-            axis=0,
-        )
-        pieces = split(cells, 3)
-        both = times(before, jnp.concatenate([pieces[turn] for turn in LEFT_PIECES + (2, 1)], axis=0))
+
+    def first_layer(chunk):
+        planes_in = slice(chunk * at_once, (chunk + 1) * at_once)
+        upper = jnp.concatenate(upper_rows[planes_in], axis=1)
+        lower = jnp.concatenate(lower_rows[planes_in], axis=1)
+        pieces = split(jnp.concatenate([upper, lower], axis=0), 3)
+        wide = jnp.concatenate([pieces[turn] for turn in LEFT_PIECES + (2, 1)], axis=0)
+        return jnp.concatenate(pieces[:2], axis=0), times(before, wide)
+
+    def activation(both):
         hidden = jnp.tanh(both[:units])
         grad_pre = both[units:] * (1.0 - hidden * hidden)
-        both = jnp.concatenate([hidden, grad_pre], axis=0)
-        both = jnp.concatenate(split(both, 2), axis=0)
-        sums = sums + times(jnp.concatenate(pieces[:2], axis=0), both, (1, 1))
-        result = times(after, both)
-        result = result[:16] + result[16:32] + result[32:]
-        for turn in range(at_once):
-            results.append(result[:8, turn * LANES : (turn + 1) * LANES])
-            x = start + turn
-            place = (x % x_rows) * x_devices + x // x_rows
-            tail_ref[place : place + 1, :] = result[8:9, turn * LANES : (turn + 1) * LANES]
+        return jnp.concatenate(split(jnp.concatenate([hidden, grad_pre], axis=0), 2), axis=0)
+
+    chunks = x_length // at_once
+    staged = {}
+    for step in range(chunks + 2):
+        if step < chunks:
+            staged[step] = first_layer(step)
+        if 0 <= step - 1 < chunks:
+            cells, both = staged[step - 1]
+            staged[step - 1] = (cells, activation(both))
+        if 0 <= step - 2:
+            cells, both = staged.pop(step - 2)
+            result = times(after, both)
+            result = result[:16] + result[16:32] + result[32:]
+            sums = sums + times(cells, both, (1, 1))
+            for turn in range(at_once):
+                part = result[:, turn * LANES : (turn + 1) * LANES]
+                results.append(part[:8])
+                x = (step - 2) * at_once + turn
+                place = (x % x_rows) * x_devices + x // x_rows
+                tail_ref[place : place + 1, :] = part[8:9]
 
     back_y = on_rows(results, y_back_ref[...])
     back = [jnp.where(row8 < 3, back_y[x], results[x]) for x in range(x_length)]
@@ -457,7 +471,7 @@
             ((48, 4 * units), half),
         ],
         [pltpu.VMEM(values.shape, values.dtype) for values in arguments]
-        + [pltpu.SemaphoreType.DMA((len(arguments),))],
+        + [pltpu.SemaphoreType.DMA((11,))],
         in_specs=[in_place] * len(arguments),
     )(*arguments)
     sent = sent.reshape(devices, 1, SENT * LANES)

time: 32.7 us -> 32.8 us (level)
  no operation moved by 1% of the time
where the time goes in v14:
time: 32.8 us; the launch traced here: 32.6 us
  blocking collectives  27.3 us (83%)
  Pallas kernels  4.58 us (14%)
  between operations  0.69 us (2%)
    all_to_all x1, blocking collectives, local_kernels(): lax.all_to_all(sent, axes, 0, 0, tiled=True).reshape(devices * SENT, LANES)  14.9 us
    all_to_all x1, blocking collectives, local_kernels(): lax.all_to_all(back, axes, 0, 0, tiled=True)  12.3 us
    pallas_call x1, Pallas kernels, local_kernels(): on_device(functools.partial(middle_kernel, x_devices), [((devices * RETUR...  2.04 us
    pallas_call x1, Pallas kernels, local_kernels(): on_device(pack_kernel, [((devices * SENT, LANES), single), ((2 * units, L...  1.48 us
    pallas_call x1, Pallas kernels, local_kernels(): on_device(functools.partial(unpack_kernel, float(cells)), [(shape, single...  1.06 us

profile of v14, /device:TPU:0, one launch (start us, length us, event | category | flops | bytes accessed | tf_op | source)
XLA Modules:
  0.0 32.6 jit_solution(9353372864350106189)
XLA Ops:
  0.6 0.0 copy-start.3
  0.6 0.0 copy-start.4
  0.7 1.5 %shard_map.128 = (f32[288,128]{1,0:T(8,128)S(1)}, bf16[128,128]{1,0:T(8,128)(2,1)S(1)}, bf16[48,256]{1,0:T(8,128)(2,1)S(1)}) custom-call(f32[3,4,8,128]{3,2,1,0:T(8,128)} %velocity_ref.1, f32[3,4,8,128]{3,2,1,0:T(8,128)} %cotangent_ref.1, f32[128,128]{1,0:T(8,128)} %constant.8.clone.z_hbm, f32[6,64]{1,0:T(8,128)} %weight_in_hbm.1, f32[1,64]{1,0:T(1,128)} %bitcast.13, ...), custom_call_target="tpu_custom_call" | custom-call | tf_op jit(solution)/shard_map/pallas_call | solution.py:466
  2.1 14.9 %all_to_all.10 = f32[32,1,1152]{2,1,0:T(1,128)S(1)} all-to-all(f32[32,1,1152]{2,1,0:T(1,128)S(1)} %bitcast.11), channel_id=1, replica_groups=mesh['gx'=8,'gy'=4] {'gy','gx'}, dimensions={0} | all-to-all | bytes 294912 | tf_op jit(solution)/shard_map/all_to_all | solution.py:478
  17.1 0.0 copy-done.3
  17.1 0.0 copy-done.4
  17.1 2.0 %shard_map.129 = f32[448,128]{1,0:T(8,128)S(1)} custom-call(f32[288,128]{1,0:T(8,128)S(1)} %bitcast.10, bf16[128,128]{1,0:T(8,128)(2,1)S(1)} %get-tuple-element.14.before_ref, bf16[48,256]{1,0:T(8,128)(2,1)S(1)} %get-tuple-element.15.after_ref, bf16[768,128]{1,0:T(8,128)(2,1)S(1)} %copy-done.4, bf16[768,128]{1,0:T(8,128)(2,1)S(1)} %copy-done.3), custom_call_target="tpu_custom_call" | custom-call | tf_op jit(solution)/shard_map/pallas_call | solution.py:479
  19.1 0.0 copy-start
  19.1 0.0 copy-start.1
  19.2 0.0 copy-start.2
  19.2 12.3 %all_to_all.11 = f32[32,1,1792]{2,1,0:T(1,128)S(1)} all-to-all(f32[32,1,1792]{2,1,0:T(1,128)S(1)} %bitcast.9), channel_id=1, replica_groups=mesh['gx'=8,'gy'=4] {'gy','gx'}, dimensions={0} | all-to-all | bytes 458752 | tf_op jit(solution)/shard_map/all_to_all | solution.py:485
  31.5 0.0 copy-done
  31.5 0.0 copy-done.1
  31.5 0.0 copy-done.2
  31.5 1.1 %shard_map.130 = (f32[3,4,8,128]{3,2,1,0:T(8,128)}, f32[3,4,8,128]{3,2,1,0:T(8,128)}, f32[6,64]{1,0:T(8,128)}, f32[1,64]{1,0:T(1,128)}, f32[3,64]{1,0:T(4,128)}) custom-call(f32[448,128]{1,0:T(8,128)S(1)} %bitcast.8, f32[3,4,8,128]{3,2,1,0:T(8,128)S(1)} %copy-done, f32[3,4,8,128]{3,2,1,0:T(8,128)S(1)} %copy-done.1, bf16[768,128]{1,0:T(8,128)(2,1)S(1)} %copy-done.2), custom_call_target="tpu_custom_call" | custom-call | tf_op jit(solution)/shard_map/pallas_call | solution.py:487
Async XLA Ops:
  0.6 16.4 %copy-start.3 = (bf16[768,128]{1,0:T(8,128)(2,1)S(1)}, bf16[768,128]{1,0:T(8,128)(2,1)}, u32[]{:S(2)}) copy-start(bf16[768,128]{1,0:T(8,128)(2,1)} %constant.10.clone.y_back_ref) | copy-start | bytes 589828
  0.6 16.4 %copy-start.4 = (bf16[768,128]{1,0:T(8,128)(2,1)S(1)}, bf16[768,128]{1,0:T(8,128)(2,1)}, u32[]{:S(2)}) copy-start(bf16[768,128]{1,0:T(8,128)(2,1)} %constant.9.clone.y_ref) | copy-start | bytes 589828
  19.1 12.4 %copy-start = (f32[3,4,8,128]{3,2,1,0:T(8,128)S(1)}, f32[3,4,8,128]{3,2,1,0:T(8,128)}, u32[]{:S(2)}) copy-start(f32[3,4,8,128]{3,2,1,0:T(8,128)} %velocity_ref.1) | copy-start | bytes 147460
  19.1 12.4 %copy-start.1 = (f32[3,4,8,128]{3,2,1,0:T(8,128)S(1)}, f32[3,4,8,128]{3,2,1,0:T(8,128)}, u32[]{:S(2)}) copy-start(f32[3,4,8,128]{3,2,1,0:T(8,128)} %cotangent_ref.1) | copy-start | bytes 147460
  19.2 12.3 %copy-start.2 = (bf16[768,128]{1,0:T(8,128)(2,1)S(1)}, bf16[768,128]{1,0:T(8,128)(2,1)}, u32[]{:S(2)}) copy-start(bf16[768,128]{1,0:T(8,128)(2,1)} %constant.11.clone.z_ref) | copy-start | bytes 589828

commit v15 on v11

--- a/solution.py
+++ b/solution.py
@@ -242,18 +242,12 @@
         ],
         axis=1,
     )
-    pieces = [piece.astype(jnp.float32) for piece in split(before, 3)]
-    before = jnp.concatenate([pieces[turn] for turn in RIGHT_PIECES + (1, 2)], axis=0)
+    pieces = [piece.astype(jnp.float32) for piece in split(before, 2)]
+    before = jnp.concatenate([pieces[turn] for turn in (0, 0, 1, 1)] + [zeros((64, LANES))], axis=0)
     before_ref[...] = before.T.astype(jnp.bfloat16)
-    pieces = split(after, 3)
-    after_ref[...] = jnp.concatenate(
-        [
-            jnp.concatenate([pieces[0], pieces[0]], axis=1),
-            jnp.concatenate([pieces[1], pieces[1]], axis=1),
-            jnp.concatenate([pieces[2], jnp.zeros_like(pieces[2])], axis=1),
-        ],
-        axis=0,
-    )
+    pieces = split(after, 2)
+    pieces = [jnp.concatenate([piece, piece], axis=1) for piece in pieces]
+    after_ref[...] = jnp.concatenate(pieces, axis=0)
 
     for copy in copies[3:]:
         copy.wait()
@@ -306,7 +300,7 @@
         upper_rows.append(features)
         lower_rows.append(jnp.where(row8 == 5, last, planes[x]))
 
-    before = before_ref[...]
+    before = before_ref[:, :64]
     after = after_ref[...]
     at_once = x_length
     sums = jnp.zeros((32, 4 * units), jnp.float32)
@@ -320,15 +314,15 @@
             ],
             axis=0,
         )
-        pieces = split(cells, 3)
-        both = times(before, jnp.concatenate([pieces[turn] for turn in LEFT_PIECES + (2, 1)], axis=0))
+        pieces = split(cells, 2)
+        both = times(before, jnp.concatenate(pieces + pieces, axis=0))
         hidden = jnp.tanh(both[:units])
         grad_pre = both[units:] * (1.0 - hidden * hidden)
         both = jnp.concatenate([hidden, grad_pre], axis=0)
         both = jnp.concatenate(split(both, 2), axis=0)
-        sums = sums + times(jnp.concatenate(pieces[:2], axis=0), both, (1, 1))
+        sums = sums + times(jnp.concatenate(pieces, axis=0), both, (1, 1))
         result = times(after, both)
-        result = result[:16] + result[16:32] + result[32:]
+        result = result[:16] + result[16:]
         for turn in range(at_once):
             results.append(result[:8, turn * LANES : (turn + 1) * LANES])
             x = start + turn
@@ -454,7 +448,7 @@
         [
             ((devices * SENT, LANES), single),
             ((2 * units, LANES), half),
-            ((48, 4 * units), half),
+            ((32, 4 * units), half),
         ],
         [pltpu.VMEM(values.shape, values.dtype) for values in arguments]
         + [pltpu.SemaphoreType.DMA((len(arguments),))],

time: 32.7 us -> 32.7 us (level)
  no operation moved by 1% of the time
where the time goes in v15:
time: 32.7 us; the launch traced here: 32.5 us
  blocking collectives  27.3 us (83%)
  Pallas kernels  4.52 us (14%)
  between operations  0.69 us (2%)
    all_to_all x1, blocking collectives, local_kernels(): lax.all_to_all(sent, axes, 0, 0, tiled=True).reshape(devices * SENT, LANES)  14.9 us
    all_to_all x1, blocking collectives, local_kernels(): lax.all_to_all(back, axes, 0, 0, tiled=True)  12.3 us
    pallas_call x1, Pallas kernels, local_kernels(): on_device(functools.partial(middle_kernel, x_devices), [((devices * RETUR...  1.99 us
    pallas_call x1, Pallas kernels, local_kernels(): on_device(pack_kernel, [((devices * SENT, LANES), single), ((2 * units, L...  1.47 us
    pallas_call x1, Pallas kernels, local_kernels(): on_device(functools.partial(unpack_kernel, float(cells)), [(shape, single...  1.06 us

profile of v15, /device:TPU:0, one launch (start us, length us, event | category | flops | bytes accessed | tf_op | source)
XLA Modules:
  0.0 32.5 jit_solution(17359742585550082349)
XLA Ops:
  0.6 0.0 copy-start.3
  0.6 0.0 copy-start.4
  0.7 1.5 %shard_map.128 = (f32[288,128]{1,0:T(8,128)S(1)}, bf16[128,128]{1,0:T(8,128)(2,1)S(1)}, bf16[32,256]{1,0:T(8,128)(2,1)S(1)}) custom-call(f32[3,4,8,128]{3,2,1,0:T(8,128)} %velocity_ref.1, f32[3,4,8,128]{3,2,1,0:T(8,128)} %cotangent_ref.1, f32[128,128]{1,0:T(8,128)} %constant.8.clone.z_hbm, f32[6,64]{1,0:T(8,128)} %weight_in_hbm.1, f32[1,64]{1,0:T(1,128)} %bitcast.13, ...), custom_call_target="tpu_custom_call" | custom-call | tf_op jit(solution)/shard_map/pallas_call | solution.py:446
  2.1 14.9 %all_to_all.10 = f32[32,1,1152]{2,1,0:T(1,128)S(1)} all-to-all(f32[32,1,1152]{2,1,0:T(1,128)S(1)} %bitcast.11), channel_id=1, replica_groups=mesh['gx'=8,'gy'=4] {'gy','gx'}, dimensions={0} | all-to-all | bytes 294912 | tf_op jit(solution)/shard_map/all_to_all | solution.py:458
  17.1 0.0 copy-done.3
  17.1 0.0 copy-done.4
  17.1 2.0 %shard_map.129 = f32[448,128]{1,0:T(8,128)S(1)} custom-call(f32[288,128]{1,0:T(8,128)S(1)} %bitcast.10, bf16[128,128]{1,0:T(8,128)(2,1)S(1)} %get-tuple-element.14.before_ref, bf16[32,256]{1,0:T(8,128)(2,1)S(1)} %get-tuple-element.15.after_ref, bf16[768,128]{1,0:T(8,128)(2,1)S(1)} %copy-done.4, bf16[768,128]{1,0:T(8,128)(2,1)S(1)} %copy-done.3), custom_call_target="tpu_custom_call" | custom-call | tf_op jit(solution)/shard_map/pallas_call | solution.py:459
  19.1 0.0 copy-start
  19.1 0.0 copy-start.1
  19.1 0.0 copy-start.2
  19.1 12.3 %all_to_all.11 = f32[32,1,1792]{2,1,0:T(1,128)S(1)} all-to-all(f32[32,1,1792]{2,1,0:T(1,128)S(1)} %bitcast.9), channel_id=1, replica_groups=mesh['gx'=8,'gy'=4] {'gy','gx'}, dimensions={0} | all-to-all | bytes 458752 | tf_op jit(solution)/shard_map/all_to_all | solution.py:465
  31.4 0.0 copy-done
  31.4 0.0 copy-done.1
  31.4 0.0 copy-done.2
  31.4 1.1 %shard_map.130 = (f32[3,4,8,128]{3,2,1,0:T(8,128)}, f32[3,4,8,128]{3,2,1,0:T(8,128)}, f32[6,64]{1,0:T(8,128)}, f32[1,64]{1,0:T(1,128)}, f32[3,64]{1,0:T(4,128)}) custom-call(f32[448,128]{1,0:T(8,128)S(1)} %bitcast.8, f32[3,4,8,128]{3,2,1,0:T(8,128)S(1)} %copy-done, f32[3,4,8,128]{3,2,1,0:T(8,128)S(1)} %copy-done.1, bf16[768,128]{1,0:T(8,128)(2,1)S(1)} %copy-done.2), custom_call_target="tpu_custom_call" | custom-call | tf_op jit(solution)/shard_map/pallas_call | solution.py:467
Async XLA Ops:
  0.6 16.4 %copy-start.3 = (bf16[768,128]{1,0:T(8,128)(2,1)S(1)}, bf16[768,128]{1,0:T(8,128)(2,1)}, u32[]{:S(2)}) copy-start(bf16[768,128]{1,0:T(8,128)(2,1)} %constant.10.clone.y_back_ref) | copy-start | bytes 589828
  0.6 16.4 %copy-start.4 = (bf16[768,128]{1,0:T(8,128)(2,1)S(1)}, bf16[768,128]{1,0:T(8,128)(2,1)}, u32[]{:S(2)}) copy-start(bf16[768,128]{1,0:T(8,128)(2,1)} %constant.9.clone.y_ref) | copy-start | bytes 589828
  19.1 12.4 %copy-start = (f32[3,4,8,128]{3,2,1,0:T(8,128)S(1)}, f32[3,4,8,128]{3,2,1,0:T(8,128)}, u32[]{:S(2)}) copy-start(f32[3,4,8,128]{3,2,1,0:T(8,128)} %velocity_ref.1) | copy-start | bytes 147460
  19.1 12.4 %copy-start.1 = (f32[3,4,8,128]{3,2,1,0:T(8,128)S(1)}, f32[3,4,8,128]{3,2,1,0:T(8,128)}, u32[]{:S(2)}) copy-start(f32[3,4,8,128]{3,2,1,0:T(8,128)} %cotangent_ref.1) | copy-start | bytes 147460
  19.1 12.3 %copy-start.2 = (bf16[768,128]{1,0:T(8,128)(2,1)S(1)}, bf16[768,128]{1,0:T(8,128)(2,1)}, u32[]{:S(2)}) copy-start(bf16[768,128]{1,0:T(8,128)(2,1)} %constant.11.clone.z_ref) | copy-start | bytes 589828

commit v16 on v11

--- a/solution.py
+++ b/solution.py
@@ -197,14 +197,12 @@
     bias_hbm,
     weight_out_hbm,
     out_ref,
-    before_ref,
-    after_ref,
+    weight_in_ref,
+    bias_ref,
+    weight_out_ref,
     velocity_ref,
     cotangent_ref,
     z_ref,
-    weight_in_ref,
-    bias_ref,
-    weight_out_ref,
     arrived,
 ):
     pairs = [
@@ -222,39 +220,6 @@
     for copy in copies:
         copy.start()
 
-    for copy in copies[:3]:
-        copy.wait()
-    weight_in = weight_in_ref[...]
-    weight_out = weight_out_ref[...]
-    units = weight_in.shape[1]
-    zeros = functools.partial(jnp.zeros, dtype=jnp.float32)
-    before = jnp.concatenate(
-        [
-            jnp.concatenate([weight_in, bias_ref[...], zeros((9, units))], axis=0),
-            jnp.concatenate([zeros((13, units)), STEP_SIZE * weight_out], axis=0),
-        ],
-        axis=1,
-    )
-    after = jnp.concatenate(
-        [
-            jnp.concatenate([zeros((6, units)), weight_out, zeros((7, units))], axis=0),
-            jnp.concatenate([weight_in, zeros((10, units))], axis=0),
-        ],
-        axis=1,
-    )
-    pieces = [piece.astype(jnp.float32) for piece in split(before, 3)]
-    before = jnp.concatenate([pieces[turn] for turn in RIGHT_PIECES + (1, 2)], axis=0)
-    before_ref[...] = before.T.astype(jnp.bfloat16)
-    pieces = split(after, 3)
-    after_ref[...] = jnp.concatenate(
-        [
-            jnp.concatenate([pieces[0], pieces[0]], axis=1),
-            jnp.concatenate([pieces[1], pieces[1]], axis=1),
-            jnp.concatenate([pieces[2], jnp.zeros_like(pieces[2])], axis=1),
-        ],
-        axis=0,
-    )
-
     for copy in copies[3:]:
         copy.wait()
     _, x_rows, y_rows, z_length = velocity_ref.shape
@@ -274,13 +239,59 @@
         parts = exchange(parts, block)
         for field in range(start, min(start + groups, SENT)):
             out_ref[pl.ds(field, devices, stride=SENT), :] = parts[field - start]
-
-
-def middle_kernel(x_devices, in_ref, before_ref, after_ref, y_ref, y_back_ref, out_ref, tail_ref):
+    for copy in copies[:3]:
+        copy.wait()
+
+
+def network_matrices(weight_in_ref, bias_ref, weight_out_ref):
+    weight_in = weight_in_ref[...]
+    weight_out = weight_out_ref[...]
+    units = weight_in.shape[1]
+    zeros = functools.partial(jnp.zeros, dtype=jnp.float32)
+    before = jnp.concatenate(
+        [
+            jnp.concatenate([weight_in, bias_ref[...], zeros((9, units))], axis=0),
+            jnp.concatenate([zeros((13, units)), STEP_SIZE * weight_out], axis=0),
+        ],
+        axis=1,
+    )
+    after = jnp.concatenate(
+        [
+            jnp.concatenate([zeros((6, units)), weight_out, zeros((7, units))], axis=0),
+            jnp.concatenate([weight_in, zeros((10, units))], axis=0),
+        ],
+        axis=1,
+    )
+    pieces = [piece.astype(jnp.float32) for piece in split(before, 3)]
+    before = jnp.concatenate([pieces[turn] for turn in RIGHT_PIECES + (1, 2)], axis=0)
+    before = before.T.astype(jnp.bfloat16)
+    pieces = split(after, 3)
+    after = jnp.concatenate(
+        [
+            jnp.concatenate([pieces[0], pieces[0]], axis=1),
+            jnp.concatenate([pieces[1], pieces[1]], axis=1),
+            jnp.concatenate([pieces[2], jnp.zeros_like(pieces[2])], axis=1),
+        ],
+        axis=0,
+    )
+    return before, after
+
+
+def middle_kernel(
+    x_devices,
+    in_ref,
+    weight_in_ref,
+    bias_ref,
+    weight_out_ref,
+    y_ref,
+    y_back_ref,
+    out_ref,
+    tail_ref,
+):
     y_devices = in_ref.shape[0] // SENT // x_devices
     x_rows = y_devices
     x_length = x_devices * x_rows
-    units = before_ref.shape[0] // 2
+    units = weight_in_ref.shape[1]
     y_rows = LANES // y_devices // x_rows
     row8 = lax.broadcasted_iota(jnp.int32, (8, LANES), 0)
 
@@ -306,8 +317,7 @@
         upper_rows.append(features)
         lower_rows.append(jnp.where(row8 == 5, last, planes[x]))
 
-    before = before_ref[...]
-    after = after_ref[...]
+    before, after = network_matrices(weight_in_ref, bias_ref, weight_out_ref)
     at_once = x_length
     sums = jnp.zeros((32, 4 * units), jnp.float32)
     results = []
@@ -436,7 +446,7 @@
     cells = x_rows * x_devices * y_rows * y_devices * z_length
     z_table = derivative_table(z_length)
     y_table = np.kron(np.eye(z_length // devices), derivative_table(y_rows * y_devices))
-    single, half = jnp.float32, jnp.bfloat16
+    single = jnp.float32
 
     in_place = pl.BlockSpec(memory_space=pltpu.HBM)
 
@@ -453,10 +463,9 @@
         pack_kernel,
         [
             ((devices * SENT, LANES), single),
-            ((2 * units, LANES), half),
-            ((48, 4 * units), half),
+            *((values.shape, single) for values in arguments[3:]),
         ],
-        [pltpu.VMEM(values.shape, values.dtype) for values in arguments]
+        [pltpu.VMEM(values.shape, values.dtype) for values in arguments[:3]]
         + [pltpu.SemaphoreType.DMA((len(arguments),))],
         in_specs=[in_place] * len(arguments),
     )(*arguments)

time: 32.7 us -> 32.7 us (level)
  no operation moved by 1% of the time
where the time goes in v16:
time: 32.7 us; the launch traced here: 32.5 us
  blocking collectives  27.3 us (83%)
  Pallas kernels  4.53 us (14%)
  between operations  0.69 us (2%)
    all_to_all x1, blocking collectives, local_kernels(): lax.all_to_all(sent, axes, 0, 0, tiled=True).reshape(devices * SENT, LANES)  14.9 us
    all_to_all x1, blocking collectives, local_kernels(): lax.all_to_all(back, axes, 0, 0, tiled=True)  12.3 us
    pallas_call x1, Pallas kernels, local_kernels(): on_device(functools.partial(middle_kernel, x_devices), [((devices * RETUR...  2 us
    pallas_call x1, Pallas kernels, local_kernels(): on_device(pack_kernel, [((devices * SENT, LANES), single), *((values.shap...  1.47 us
    pallas_call x1, Pallas kernels, local_kernels(): on_device(functools.partial(unpack_kernel, float(cells)), [(shape, single...  1.06 us

profile of v16, /device:TPU:0, one launch (start us, length us, event | category | flops | bytes accessed | tf_op | source)
XLA Modules:
  0.0 32.5 jit_solution(1842621150763420664)
XLA Ops:
  0.6 0.0 copy-start.3
  0.6 0.0 copy-start.4
  0.7 1.5 %shard_map.128 = (f32[288,128]{1,0:T(8,128)S(1)}, f32[6,64]{1,0:T(8,128)S(1)}, f32[1,64]{1,0:T(1,128)S(1)}, f32[3,64]{1,0:T(4,128)S(1)}) custom-call(f32[3,4,8,128]{3,2,1,0:T(8,128)} %velocity_ref.1, f32[3,4,8,128]{3,2,1,0:T(8,128)} %cotangent_ref.1, f32[128,128]{1,0:T(8,128)} %constant.8.clone.z_hbm, f32[6,64]{1,0:T(8,128)} %weight_in_hbm.1, ...), custom_call_target="tpu_custom_call" | custom-call | tf_op jit(solution)/shard_map/pallas_call | solution.py:462
  2.1 14.9 %all_to_all.10 = f32[32,1,1152]{2,1,0:T(1,128)S(1)} all-to-all(f32[32,1,1152]{2,1,0:T(1,128)S(1)} %bitcast.11), channel_id=1, replica_groups=mesh['gx'=8,'gy'=4] {'gy','gx'}, dimensions={0} | all-to-all | bytes 294912 | tf_op jit(solution)/shard_map/all_to_all | solution.py:473
  17.1 0.0 copy-done.3
  17.1 0.0 copy-done.4
  17.1 2.0 %shard_map.129 = f32[448,128]{1,0:T(8,128)S(1)} custom-call(f32[288,128]{1,0:T(8,128)S(1)} %bitcast.10, f32[6,64]{1,0:T(8,128)S(1)} %get-tuple-element.15.weight_in_ref, f32[1,64]{1,0:T(1,128)S(1)} %get-tuple-element.16.bias_ref, f32[3,64]{1,0:T(4,128)S(1)} %get-tuple-element.17.weight_out_ref, bf16[768,128]{1,0:T(8,128)(2,1)S(1)} %copy-done.4, ...), custom_call_target="tpu_custom_call" | custom-call | tf_op jit(solution)/shard_map/pallas_call | solution.py:474
  19.1 0.0 copy-start
  19.1 0.0 copy-start.1
  19.1 0.0 copy-start.2
  19.1 12.3 %all_to_all.11 = f32[32,1,1792]{2,1,0:T(1,128)S(1)} all-to-all(f32[32,1,1792]{2,1,0:T(1,128)S(1)} %bitcast.9), channel_id=1, replica_groups=mesh['gx'=8,'gy'=4] {'gy','gx'}, dimensions={0} | all-to-all | bytes 458752 | tf_op jit(solution)/shard_map/all_to_all | solution.py:480
  31.4 0.0 copy-done
  31.4 0.0 copy-done.1
  31.5 0.0 copy-done.2
  31.5 1.1 %shard_map.130 = (f32[3,4,8,128]{3,2,1,0:T(8,128)}, f32[3,4,8,128]{3,2,1,0:T(8,128)}, f32[6,64]{1,0:T(8,128)}, f32[1,64]{1,0:T(1,128)}, f32[3,64]{1,0:T(4,128)}) custom-call(f32[448,128]{1,0:T(8,128)S(1)} %bitcast.8, f32[3,4,8,128]{3,2,1,0:T(8,128)S(1)} %copy-done, f32[3,4,8,128]{3,2,1,0:T(8,128)S(1)} %copy-done.1, bf16[768,128]{1,0:T(8,128)(2,1)S(1)} %copy-done.2), custom_call_target="tpu_custom_call" | custom-call | tf_op jit(solution)/shard_map/pallas_call | solution.py:482
Async XLA Ops:
  0.6 16.4 %copy-start.3 = (bf16[768,128]{1,0:T(8,128)(2,1)S(1)}, bf16[768,128]{1,0:T(8,128)(2,1)}, u32[]{:S(2)}) copy-start(bf16[768,128]{1,0:T(8,128)(2,1)} %constant.10.clone.y_back_ref) | copy-start | bytes 589828
  0.6 16.4 %copy-start.4 = (bf16[768,128]{1,0:T(8,128)(2,1)S(1)}, bf16[768,128]{1,0:T(8,128)(2,1)}, u32[]{:S(2)}) copy-start(bf16[768,128]{1,0:T(8,128)(2,1)} %constant.9.clone.y_ref) | copy-start | bytes 589828
  19.1 12.4 %copy-start = (f32[3,4,8,128]{3,2,1,0:T(8,128)S(1)}, f32[3,4,8,128]{3,2,1,0:T(8,128)}, u32[]{:S(2)}) copy-start(f32[3,4,8,128]{3,2,1,0:T(8,128)} %velocity_ref.1) | copy-start | bytes 147460
  19.1 12.4 %copy-start.1 = (f32[3,4,8,128]{3,2,1,0:T(8,128)S(1)}, f32[3,4,8,128]{3,2,1,0:T(8,128)}, u32[]{:S(2)}) copy-start(f32[3,4,8,128]{3,2,1,0:T(8,128)} %cotangent_ref.1) | copy-start | bytes 147460
  19.1 12.3 %copy-start.2 = (bf16[768,128]{1,0:T(8,128)(2,1)S(1)}, bf16[768,128]{1,0:T(8,128)(2,1)}, u32[]{:S(2)}) copy-start(bf16[768,128]{1,0:T(8,128)(2,1)} %constant.11.clone.z_ref) | copy-start | bytes 589828

commit v17 on v16

--- a/solution.py
+++ b/solution.py
@@ -185,8 +185,16 @@
 
 
 def on_rows(rows, wide_table):
-    out = times_table(jnp.concatenate(rows, axis=0), wide_table)
-    return [out[8 * turn : 8 * turn + 8] for turn in range(len(rows))]
+    row8 = lax.broadcasted_iota(jnp.int32, rows[0].shape, 0)
+    pairs = [
+        jnp.where(row8 < 3, even, pltpu.roll(odd, 3, 0)) for even, odd in zip(rows[::2], rows[1::2])
+    ]
+    out = times_table(jnp.concatenate(pairs, axis=0), wide_table)
+    outs = []
+    for turn in range(len(pairs)):
+        part = out[8 * turn : 8 * turn + 8]
+        outs.extend([part, pltpu.roll(part, 5, 0)])
+    return outs
 
 
 def pack_kernel(
@@ -220,25 +228,27 @@
     for copy in copies:
         copy.start()
 
-    for copy in copies[3:]:
-        copy.wait()
     _, x_rows, y_rows, z_length = velocity_ref.shape
     block = x_rows * y_rows
     groups = LANES // block
     devices = z_length // groups
-    velocity = velocity_ref[...].reshape(3 * block, z_length)
-    cotangent = cotangent_ref[...].reshape(3 * block, z_length)
-    along_z = times_table(velocity, widened(z_ref[...]))
-    fill = jnp.zeros(((-SENT % groups) * block, z_length), jnp.float32)
-    rows = jnp.concatenate(
-        [velocity, along_z, cotangent[block:], cotangent[:block], fill], axis=0
-    )
-    for start in range(0, SENT, groups):
-        turned = rows[start * block : (start + groups) * block].T
+
+    def store(fields, places):
+        fill = [jnp.zeros_like(fields[0])] * (groups - len(fields))
+        turned = jnp.concatenate([*fields, *fill], axis=0).T
         parts = [turned[group * devices : (group + 1) * devices] for group in range(groups)]
-        parts = exchange(parts, block)
-        for field in range(start, min(start + groups, SENT)):
-            out_ref[pl.ds(field, devices, stride=SENT), :] = parts[field - start]
+        for part, place in zip(exchange(parts, block), places):
+            out_ref[pl.ds(place, devices, stride=SENT), :] = part
+
+    for copy in copies[3:5]:
+        copy.wait()
+    velocity = [velocity_ref[part].reshape(block, z_length) for part in range(3)]
+    cotangent = [cotangent_ref[part].reshape(block, z_length) for part in range(3)]
+    store([*velocity, cotangent[1]], (0, 1, 2, 6))
+    store([cotangent[2], cotangent[0]], (7, 8))
+    copies[5].wait()
+    along_z = times_table(jnp.concatenate(velocity, axis=0), widened(z_ref[...]))
+    store([along_z[part * block : (part + 1) * block] for part in range(3)], (3, 4, 5))
     for copy in copies[:3]:
         copy.wait()
 

time: 32.7 us -> 32.9 us (level)
  no operation moved by 1% of the time
where the time goes in v17:
time: 32.9 us; the launch traced here: 32.7 us
  blocking collectives  27.3 us (83%)
  Pallas kernels  4.73 us (14%)
  between operations  0.69 us (2%)
    all_to_all x1, blocking collectives, local_kernels(): lax.all_to_all(sent, axes, 0, 0, tiled=True).reshape(devices * SENT, LANES)  14.9 us
    all_to_all x1, blocking collectives, local_kernels(): lax.all_to_all(back, axes, 0, 0, tiled=True)  12.3 us
    pallas_call x1, Pallas kernels, local_kernels(): on_device(functools.partial(middle_kernel, x_devices), [((devices * RETUR...  2.02 us
    pallas_call x1, Pallas kernels, local_kernels(): on_device(pack_kernel, [((devices * SENT, LANES), single), *((values.shap...  1.65 us
    pallas_call x1, Pallas kernels, local_kernels(): on_device(functools.partial(unpack_kernel, float(cells)), [(shape, single...  1.06 us

profile of v17, /device:TPU:0, one launch (start us, length us, event | category | flops | bytes accessed | tf_op | source)
XLA Modules:
  0.0 32.7 jit_solution(16378706633518234117)
XLA Ops:
  0.6 0.0 copy-start.3
  0.6 0.0 copy-start.4
  0.7 1.6 %shard_map.128 = (f32[288,128]{1,0:T(8,128)S(1)}, f32[6,64]{1,0:T(8,128)S(1)}, f32[1,64]{1,0:T(1,128)S(1)}, f32[3,64]{1,0:T(4,128)S(1)}) custom-call(f32[3,4,8,128]{3,2,1,0:T(8,128)} %velocity_ref.1, f32[3,4,8,128]{3,2,1,0:T(8,128)} %cotangent_ref.1, f32[128,128]{1,0:T(8,128)} %constant.8.clone.z_hbm, f32[6,64]{1,0:T(8,128)} %weight_in_hbm.1, ...), custom_call_target="tpu_custom_call" | custom-call | tf_op jit(solution)/shard_map/pallas_call | solution.py:472
  2.3 14.9 %all_to_all.10 = f32[32,1,1152]{2,1,0:T(1,128)S(1)} all-to-all(f32[32,1,1152]{2,1,0:T(1,128)S(1)} %bitcast.11), channel_id=1, replica_groups=mesh['gx'=8,'gy'=4] {'gy','gx'}, dimensions={0} | all-to-all | bytes 294912 | tf_op jit(solution)/shard_map/all_to_all | solution.py:483
  17.2 0.0 copy-done.3
  17.2 0.0 copy-done.4
  17.3 2.0 %shard_map.129 = f32[448,128]{1,0:T(8,128)S(1)} custom-call(f32[288,128]{1,0:T(8,128)S(1)} %bitcast.10, f32[6,64]{1,0:T(8,128)S(1)} %get-tuple-element.15.weight_in_ref, f32[1,64]{1,0:T(1,128)S(1)} %get-tuple-element.16.bias_ref, f32[3,64]{1,0:T(4,128)S(1)} %get-tuple-element.17.weight_out_ref, bf16[768,128]{1,0:T(8,128)(2,1)S(1)} %copy-done.4, ...), custom_call_target="tpu_custom_call" | custom-call | tf_op jit(solution)/shard_map/pallas_call | solution.py:484
  19.3 0.0 copy-start
  19.3 0.0 copy-start.1
  19.3 0.0 copy-start.2
  19.3 12.3 %all_to_all.11 = f32[32,1,1792]{2,1,0:T(1,128)S(1)} all-to-all(f32[32,1,1792]{2,1,0:T(1,128)S(1)} %bitcast.9), channel_id=1, replica_groups=mesh['gx'=8,'gy'=4] {'gy','gx'}, dimensions={0} | all-to-all | bytes 458752 | tf_op jit(solution)/shard_map/all_to_all | solution.py:490
  31.6 0.0 copy-done
  31.7 0.0 copy-done.1
  31.7 0.0 copy-done.2
  31.7 1.1 %shard_map.130 = (f32[3,4,8,128]{3,2,1,0:T(8,128)}, f32[3,4,8,128]{3,2,1,0:T(8,128)}, f32[6,64]{1,0:T(8,128)}, f32[1,64]{1,0:T(1,128)}, f32[3,64]{1,0:T(4,128)}) custom-call(f32[448,128]{1,0:T(8,128)S(1)} %bitcast.8, f32[3,4,8,128]{3,2,1,0:T(8,128)S(1)} %copy-done, f32[3,4,8,128]{3,2,1,0:T(8,128)S(1)} %copy-done.1, bf16[768,128]{1,0:T(8,128)(2,1)S(1)} %copy-done.2), custom_call_target="tpu_custom_call" | custom-call | tf_op jit(solution)/shard_map/pallas_call | solution.py:492
Async XLA Ops:
  0.6 16.6 %copy-start.3 = (bf16[768,128]{1,0:T(8,128)(2,1)S(1)}, bf16[768,128]{1,0:T(8,128)(2,1)}, u32[]{:S(2)}) copy-start(bf16[768,128]{1,0:T(8,128)(2,1)} %constant.10.clone.y_back_ref) | copy-start | bytes 589828
  0.6 16.6 %copy-start.4 = (bf16[768,128]{1,0:T(8,128)(2,1)S(1)}, bf16[768,128]{1,0:T(8,128)(2,1)}, u32[]{:S(2)}) copy-start(bf16[768,128]{1,0:T(8,128)(2,1)} %constant.9.clone.y_ref) | copy-start | bytes 589828
  19.3 12.4 %copy-start = (f32[3,4,8,128]{3,2,1,0:T(8,128)S(1)}, f32[3,4,8,128]{3,2,1,0:T(8,128)}, u32[]{:S(2)}) copy-start(f32[3,4,8,128]{3,2,1,0:T(8,128)} %velocity_ref.1) | copy-start | bytes 147460
  19.3 12.4 %copy-start.1 = (f32[3,4,8,128]{3,2,1,0:T(8,128)S(1)}, f32[3,4,8,128]{3,2,1,0:T(8,128)}, u32[]{:S(2)}) copy-start(f32[3,4,8,128]{3,2,1,0:T(8,128)} %cotangent_ref.1) | copy-start | bytes 147460
  19.3 12.3 %copy-start.2 = (bf16[768,128]{1,0:T(8,128)(2,1)S(1)}, bf16[768,128]{1,0:T(8,128)(2,1)}, u32[]{:S(2)}) copy-start(bf16[768,128]{1,0:T(8,128)(2,1)} %constant.11.clone.z_ref) | copy-start | bytes 589828

commit v18 on v16

--- a/solution.py
+++ b/solution.py
@@ -177,11 +177,6 @@
 def times_table(values, wide_table):
     pieces = split(values, 3)
     return times(jnp.concatenate([pieces[turn] for turn in LEFT_PIECES], axis=1), wide_table)
-
-
-def widened(square_table):
-    pieces = split(square_table, 3)
-    return jnp.concatenate([pieces[turn] for turn in RIGHT_PIECES], axis=0)
 
 
 def on_rows(rows, wide_table):
@@ -226,19 +221,26 @@
     block = x_rows * y_rows
     groups = LANES // block
     devices = z_length // groups
-    velocity = velocity_ref[...].reshape(3 * block, z_length)
-    cotangent = cotangent_ref[...].reshape(3 * block, z_length)
-    along_z = times_table(velocity, widened(z_ref[...]))
-    fill = jnp.zeros(((-SENT % groups) * block, z_length), jnp.float32)
-    rows = jnp.concatenate(
-        [velocity, along_z, cotangent[block:], cotangent[:block], fill], axis=0
-    )
-    for start in range(0, SENT, groups):
-        turned = rows[start * block : (start + groups) * block].T
-        parts = [turned[group * devices : (group + 1) * devices] for group in range(groups)]
-        parts = exchange(parts, block)
-        for field in range(start, min(start + groups, SENT)):
-            out_ref[pl.ds(field, devices, stride=SENT), :] = parts[field - start]
+    velocity = [velocity_ref[part].reshape(block, z_length) for part in range(3)]
+    cotangent = [cotangent_ref[part].reshape(block, z_length) for part in range(3)]
+
+    table_pieces = split(z_ref[...], 3)
+    pieces = split(jnp.concatenate([*velocity, velocity[0]], axis=0), 3)
+    along_z = times(
+        jnp.concatenate([table_pieces[turn] for turn in RIGHT_PIECES], axis=1),
+        jnp.concatenate([pieces[turn] for turn in LEFT_PIECES], axis=1),
+        (1, 1),
+    )
+    fill = jnp.zeros_like(velocity[0])
+    turned = [
+        (jnp.concatenate([*velocity, cotangent[1]], axis=0).T, (0, 1, 2, 6)),
+        (jnp.concatenate([cotangent[2], cotangent[0], fill, fill], axis=0).T, (7, 8)),
+        (along_z, (3, 4, 5)),
+    ]
+    for fields, places in turned:
+        parts = [fields[group * devices : (group + 1) * devices] for group in range(groups)]
+        for part, place in zip(exchange(parts, block), places):
+            out_ref[pl.ds(place, devices, stride=SENT), :] = part
     for copy in copies[:3]:
         copy.wait()
 
@@ -453,7 +455,7 @@
     arguments = [
         velocity,
         cotangent,
-        table(z_table.T),
+        table(z_table),
         weight_in,
         bias_in[None],
         weight_out.T,

time: 32.7 us -> 32.6 us (level)
  no operation moved by 1% of the time
where the time goes in v18:
time: 32.6 us; the launch traced here: 32.4 us
  blocking collectives  27.3 us (84%)
  Pallas kernels  4.46 us (14%)
  between operations  0.69 us (2%)
    all_to_all x1, blocking collectives, local_kernels(): lax.all_to_all(sent, axes, 0, 0, tiled=True).reshape(devices * SENT, LANES)  14.9 us
    all_to_all x1, blocking collectives, local_kernels(): lax.all_to_all(back, axes, 0, 0, tiled=True)  12.3 us
    pallas_call x1, Pallas kernels, local_kernels(): on_device(functools.partial(middle_kernel, x_devices), [((devices * RETUR...  2 us
    pallas_call x1, Pallas kernels, local_kernels(): on_device(pack_kernel, [((devices * SENT, LANES), single), *((values.shap...  1.4 us
    pallas_call x1, Pallas kernels, local_kernels(): on_device(functools.partial(unpack_kernel, float(cells)), [(shape, single...  1.06 us

profile of v18, /device:TPU:0, one launch (start us, length us, event | category | flops | bytes accessed | tf_op | source)
XLA Modules:
  0.0 32.4 jit_solution(17418566121119619043)
XLA Ops:
  0.6 0.0 copy-start.3
  0.6 0.0 copy-start.4
  0.7 1.4 %shard_map.128 = (f32[288,128]{1,0:T(8,128)S(1)}, f32[6,64]{1,0:T(8,128)S(1)}, f32[1,64]{1,0:T(1,128)S(1)}, f32[3,64]{1,0:T(4,128)S(1)}) custom-call(f32[3,4,8,128]{3,2,1,0:T(8,128)} %velocity_ref.1, f32[3,4,8,128]{3,2,1,0:T(8,128)} %cotangent_ref.1, f32[128,128]{1,0:T(8,128)} %constant.8.clone.z_hbm, f32[6,64]{1,0:T(8,128)} %weight_in_hbm.1, ...), custom_call_target="tpu_custom_call" | custom-call | tf_op jit(solution)/shard_map/pallas_call | solution.py:464
  2.1 14.9 %all_to_all.10 = f32[32,1,1152]{2,1,0:T(1,128)S(1)} all-to-all(f32[32,1,1152]{2,1,0:T(1,128)S(1)} %bitcast.11), channel_id=1, replica_groups=mesh['gx'=8,'gy'=4] {'gy','gx'}, dimensions={0} | all-to-all | bytes 294912 | tf_op jit(solution)/shard_map/all_to_all | solution.py:475
  17.0 0.0 copy-done.3
  17.0 0.0 copy-done.4
  17.0 2.0 %shard_map.129 = f32[448,128]{1,0:T(8,128)S(1)} custom-call(f32[288,128]{1,0:T(8,128)S(1)} %bitcast.10, f32[6,64]{1,0:T(8,128)S(1)} %get-tuple-element.15.weight_in_ref, f32[1,64]{1,0:T(1,128)S(1)} %get-tuple-element.16.bias_ref, f32[3,64]{1,0:T(4,128)S(1)} %get-tuple-element.17.weight_out_ref, bf16[768,128]{1,0:T(8,128)(2,1)S(1)} %copy-done.4, ...), custom_call_target="tpu_custom_call" | custom-call | tf_op jit(solution)/shard_map/pallas_call | solution.py:476
  19.0 0.0 copy-start
  19.0 0.0 copy-start.1
  19.0 0.0 copy-start.2
  19.0 12.3 %all_to_all.11 = f32[32,1,1792]{2,1,0:T(1,128)S(1)} all-to-all(f32[32,1,1792]{2,1,0:T(1,128)S(1)} %bitcast.9), channel_id=1, replica_groups=mesh['gx'=8,'gy'=4] {'gy','gx'}, dimensions={0} | all-to-all | bytes 458752 | tf_op jit(solution)/shard_map/all_to_all | solution.py:482
  31.4 0.0 copy-done
  31.4 0.0 copy-done.1
  31.4 0.0 copy-done.2
  31.4 1.1 %shard_map.130 = (f32[3,4,8,128]{3,2,1,0:T(8,128)}, f32[3,4,8,128]{3,2,1,0:T(8,128)}, f32[6,64]{1,0:T(8,128)}, f32[1,64]{1,0:T(1,128)}, f32[3,64]{1,0:T(4,128)}) custom-call(f32[448,128]{1,0:T(8,128)S(1)} %bitcast.8, f32[3,4,8,128]{3,2,1,0:T(8,128)S(1)} %copy-done, f32[3,4,8,128]{3,2,1,0:T(8,128)S(1)} %copy-done.1, bf16[768,128]{1,0:T(8,128)(2,1)S(1)} %copy-done.2), custom_call_target="tpu_custom_call" | custom-call | tf_op jit(solution)/shard_map/pallas_call | solution.py:484
Async XLA Ops:
  0.6 16.4 %copy-start.3 = (bf16[768,128]{1,0:T(8,128)(2,1)S(1)}, bf16[768,128]{1,0:T(8,128)(2,1)}, u32[]{:S(2)}) copy-start(bf16[768,128]{1,0:T(8,128)(2,1)} %constant.10.clone.y_back_ref) | copy-start | bytes 589828
  0.6 16.4 %copy-start.4 = (bf16[768,128]{1,0:T(8,128)(2,1)S(1)}, bf16[768,128]{1,0:T(8,128)(2,1)}, u32[]{:S(2)}) copy-start(bf16[768,128]{1,0:T(8,128)(2,1)} %constant.9.clone.y_ref) | copy-start | bytes 589828
  19.0 12.4 %copy-start = (f32[3,4,8,128]{3,2,1,0:T(8,128)S(1)}, f32[3,4,8,128]{3,2,1,0:T(8,128)}, u32[]{:S(2)}) copy-start(f32[3,4,8,128]{3,2,1,0:T(8,128)} %velocity_ref.1) | copy-start | bytes 147460
  19.0 12.4 %copy-start.1 = (f32[3,4,8,128]{3,2,1,0:T(8,128)S(1)}, f32[3,4,8,128]{3,2,1,0:T(8,128)}, u32[]{:S(2)}) copy-start(f32[3,4,8,128]{3,2,1,0:T(8,128)} %cotangent_ref.1) | copy-start | bytes 147460
  19.0 12.3 %copy-start.2 = (bf16[768,128]{1,0:T(8,128)(2,1)S(1)}, bf16[768,128]{1,0:T(8,128)(2,1)}, u32[]{:S(2)}) copy-start(bf16[768,128]{1,0:T(8,128)(2,1)} %constant.11.clone.z_ref) | copy-start | bytes 589828

commit v19 on v18

--- a/solution.py
+++ b/solution.py
@@ -389,19 +389,21 @@
     groups = LANES // block
     devices = z_length // groups
     units = in_grad_ref.shape[1]
-    fields = []
-    for start in range(0, SENT, groups):
+
+    def three_fields(start):
         parts = [
-            in_ref[pl.ds(min(field, SENT - 1), devices, stride=RETURNED), :]
-            for field in range(start, start + groups)
+            in_ref[pl.ds(start + min(field, 2), devices, stride=RETURNED), :]
+            for field in range(groups)
         ]
-        turned = jnp.concatenate(exchange(parts, block), axis=0).T
-        fields.extend(turned[turn * block : (turn + 1) * block] for turn in range(groups))
+        return jnp.concatenate(exchange(parts, block), axis=0).T[: 3 * block]
+
+    back_z = times_table(three_fields(3), z_ref[...])
+    back = three_fields(0)
+    forcing = three_fields(6)
     shape = (3, x_rows, y_rows, z_length)
-    forcing = jnp.concatenate(fields[6:9], axis=0).reshape(shape)
+    forcing = forcing.reshape(shape)
     new_ref[...] = velocity_ref[...] + STEP_SIZE * forcing
-    back_z = times_table(jnp.concatenate(fields[3:6], axis=0), z_ref[...])
-    back = jnp.concatenate(fields[:3], axis=0) + back_z
+    back = back + back_z
     grad_ref[...] = cotangent_ref[...] + back.reshape(shape)
 
     sums = in_ref[SENT : SENT + 5, :]

time: 32.6 us -> 32.6 us (level)
  no operation moved by 1% of the time
where the time goes in v19:
time: 32.6 us; the launch traced here: 32.4 us
  blocking collectives  27.3 us (84%)
  Pallas kernels  4.44 us (14%)
  between operations  0.69 us (2%)
    all_to_all x1, blocking collectives, local_kernels(): lax.all_to_all(sent, axes, 0, 0, tiled=True).reshape(devices * SENT, LANES)  14.9 us
    all_to_all x1, blocking collectives, local_kernels(): lax.all_to_all(back, axes, 0, 0, tiled=True)  12.3 us
    pallas_call x1, Pallas kernels, local_kernels(): on_device(functools.partial(middle_kernel, x_devices), [((devices * RETUR...  2 us
    pallas_call x1, Pallas kernels, local_kernels(): on_device(pack_kernel, [((devices * SENT, LANES), single), *((values.shap...  1.4 us
    pallas_call x1, Pallas kernels, local_kernels(): on_device(functools.partial(unpack_kernel, float(cells)), [(shape, single...  1.04 us

profile of v19, /device:TPU:0, one launch (start us, length us, event | category | flops | bytes accessed | tf_op | source)
XLA Modules:
  0.0 32.4 jit_solution(5982323339065023972)
XLA Ops:
  0.6 0.0 copy-start.3
  0.6 0.0 copy-start.4
  0.7 1.4 %shard_map.128 = (f32[288,128]{1,0:T(8,128)S(1)}, f32[6,64]{1,0:T(8,128)S(1)}, f32[1,64]{1,0:T(1,128)S(1)}, f32[3,64]{1,0:T(4,128)S(1)}) custom-call(f32[3,4,8,128]{3,2,1,0:T(8,128)} %velocity_ref.1, f32[3,4,8,128]{3,2,1,0:T(8,128)} %cotangent_ref.1, f32[128,128]{1,0:T(8,128)} %constant.8.clone.z_hbm, f32[6,64]{1,0:T(8,128)} %weight_in_hbm.1, ...), custom_call_target="tpu_custom_call" | custom-call | tf_op jit(solution)/shard_map/pallas_call | solution.py:466
  2.1 14.9 %all_to_all.10 = f32[32,1,1152]{2,1,0:T(1,128)S(1)} all-to-all(f32[32,1,1152]{2,1,0:T(1,128)S(1)} %bitcast.11), channel_id=1, replica_groups=mesh['gx'=8,'gy'=4] {'gy','gx'}, dimensions={0} | all-to-all | bytes 294912 | tf_op jit(solution)/shard_map/all_to_all | solution.py:477
  17.0 0.0 copy-done.3
  17.0 0.0 copy-done.4
  17.0 2.0 %shard_map.129 = f32[448,128]{1,0:T(8,128)S(1)} custom-call(f32[288,128]{1,0:T(8,128)S(1)} %bitcast.10, f32[6,64]{1,0:T(8,128)S(1)} %get-tuple-element.15.weight_in_ref, f32[1,64]{1,0:T(1,128)S(1)} %get-tuple-element.16.bias_ref, f32[3,64]{1,0:T(4,128)S(1)} %get-tuple-element.17.weight_out_ref, bf16[768,128]{1,0:T(8,128)(2,1)S(1)} %copy-done.4, ...), custom_call_target="tpu_custom_call" | custom-call | tf_op jit(solution)/shard_map/pallas_call | solution.py:478
  19.0 0.0 copy-start
  19.0 0.0 copy-start.1
  19.0 0.0 copy-start.2
  19.0 12.3 %all_to_all.11 = f32[32,1,1792]{2,1,0:T(1,128)S(1)} all-to-all(f32[32,1,1792]{2,1,0:T(1,128)S(1)} %bitcast.9), channel_id=1, replica_groups=mesh['gx'=8,'gy'=4] {'gy','gx'}, dimensions={0} | all-to-all | bytes 458752 | tf_op jit(solution)/shard_map/all_to_all | solution.py:484
  31.4 0.0 copy-done
  31.4 0.0 copy-done.1
  31.4 0.0 copy-done.2
  31.4 1.0 %shard_map.130 = (f32[3,4,8,128]{3,2,1,0:T(8,128)}, f32[3,4,8,128]{3,2,1,0:T(8,128)}, f32[6,64]{1,0:T(8,128)}, f32[1,64]{1,0:T(1,128)}, f32[3,64]{1,0:T(4,128)}) custom-call(f32[448,128]{1,0:T(8,128)S(1)} %bitcast.8, f32[3,4,8,128]{3,2,1,0:T(8,128)S(1)} %copy-done, f32[3,4,8,128]{3,2,1,0:T(8,128)S(1)} %copy-done.1, bf16[768,128]{1,0:T(8,128)(2,1)S(1)} %copy-done.2), custom_call_target="tpu_custom_call" | custom-call | tf_op jit(solution)/shard_map/pallas_call | solution.py:486
Async XLA Ops:
  0.6 16.4 %copy-start.3 = (bf16[768,128]{1,0:T(8,128)(2,1)S(1)}, bf16[768,128]{1,0:T(8,128)(2,1)}, u32[]{:S(2)}) copy-start(bf16[768,128]{1,0:T(8,128)(2,1)} %constant.10.clone.y_back_ref) | copy-start | bytes 589828
  0.6 16.4 %copy-start.4 = (bf16[768,128]{1,0:T(8,128)(2,1)S(1)}, bf16[768,128]{1,0:T(8,128)(2,1)}, u32[]{:S(2)}) copy-start(bf16[768,128]{1,0:T(8,128)(2,1)} %constant.9.clone.y_ref) | copy-start | bytes 589828
  19.0 12.4 %copy-start = (f32[3,4,8,128]{3,2,1,0:T(8,128)S(1)}, f32[3,4,8,128]{3,2,1,0:T(8,128)}, u32[]{:S(2)}) copy-start(f32[3,4,8,128]{3,2,1,0:T(8,128)} %velocity_ref.1) | copy-start | bytes 147460
  19.0 12.4 %copy-start.1 = (f32[3,4,8,128]{3,2,1,0:T(8,128)S(1)}, f32[3,4,8,128]{3,2,1,0:T(8,128)}, u32[]{:S(2)}) copy-start(f32[3,4,8,128]{3,2,1,0:T(8,128)} %cotangent_ref.1) | copy-start | bytes 147460
  19.0 12.3 %copy-start.2 = (bf16[768,128]{1,0:T(8,128)(2,1)S(1)}, bf16[768,128]{1,0:T(8,128)(2,1)}, u32[]{:S(2)}) copy-start(bf16[768,128]{1,0:T(8,128)(2,1)} %constant.11.clone.z_ref) | copy-start | bytes 589828
